TPU v7x, 32 devices: a whole 2x2x4 slice. The times are simulated.
32 devices in a mesh: stars: 32 (over z, y, x, core).
Axes of the slice: x: 2, y: 2, z: 4, core: 2. Of those that a mesh axis runs over, the one named last changes fastest.
Arguments:
- star_state: float32 [6, 131072], P(None, 'stars'), may hold values from -8 to 8
- old_force: float32 [6, 131072], P(None, 'stars'), may hold values from -3 to 3
- star_mass: float32 [131072], P('stars'), may hold values from 3.8146973e-06 to 1.5258789e-05
- elapsed: float32 [131072], P('stars'), may hold values from 0.02 to 0.08
- active_ids: int32 [256], P('stars'), may hold values from 0 to 131071, as said below
- neighbours: int32 [256, 128], P('stars'), may hold values from 0 to 131071, as said below
- list_length: int32 [256], P('stars'), may hold values from 64 to 128
Outputs:
- new_state: float32 [6, 256], P(None, 'stars')
- new_forces: float32 [12, 256], P(None, 'stars')
- corrector_terms: float32 [6, 256], P(None, 'stars')
Inputs may be any that keep to these rules, and one draw needn't show every extreme that they name: `active_ids`: star id s is owned by the device holding column s of the star arrays, that is device s // 4096. `neighbours`: among the 1024 entries in the rows of one device, at most 64 are ids owned by any one device, and exactly 64 are owned by some device.
All inputs are finite; a program needn't handle non-finite values.
Results may differ from a plain program's by a relative error of at most 0.00026.
Values sent between devices are 32-bit elements; how exact they have to be, the bound alone decides.
No kernel may reach another device: no remote copies, remote signals or barrier semaphores. Data moves between devices by JAX's collectives and lax.ppermute only.
A program may use at most 192 MiB of HBM per device.

v0:
```python
import math

import jax
import jax.numpy as jnp
from jax import lax
from jax.sharding import PartitionSpec as P


def predict(star_state, old_force, star_mass, elapsed):
    step_one = elapsed[None, :]
    position = star_state[0:3] + step_one * (
        star_state[3:6] + step_one * (0.5 * old_force[0:3] + step_one * old_force[3:6] / 6.0)
    )
    velocity = star_state[3:6] + step_one * (old_force[0:3] + 0.5 * step_one * old_force[3:6])
    return jnp.concatenate([position, velocity, star_mass[None, :]], axis=0)


def pair_terms(targets, sources, softening):
    separation = sources[0:3, None, :] - targets[0:3, :, None]
    relative = sources[3:6, None, :] - targets[3:6, :, None]
    dist_sq = jnp.sum(separation * separation, axis=0) + softening
    inverse = 1.0 / dist_sq
    strength = sources[6][None, :] * inverse * jnp.sqrt(inverse)
    radial = 3.0 * jnp.sum(separation * relative, axis=0) * inverse
    accel_sum = jnp.sum(strength[None] * separation, axis=2)
    jerk_sum = jnp.sum(strength[None] * (relative - radial[None] * separation), axis=2)
    return jnp.concatenate([accel_sum, jerk_sum], axis=0)


def listed_sum(targets, listed, in_list, softening):
    separation = listed[0:3] - targets[0:3, :, None]
    relative = listed[3:6] - targets[3:6, :, None]
    dist_sq = jnp.sum(separation * separation, axis=0) + softening
    inverse = 1.0 / dist_sq
    strength = jnp.where(in_list, listed[6], 0.0) * inverse * jnp.sqrt(inverse)
    radial = 3.0 * jnp.sum(separation * relative, axis=0) * inverse
    accel_sum = jnp.sum(strength[None] * separation, axis=2)
    jerk_sum = jnp.sum(strength[None] * (relative - radial[None] * separation), axis=2)
    return jnp.concatenate([accel_sum, jerk_sum], axis=0)


def correct(own_rows, total_force, irregular):
    step_size = own_rows[12][None, :]
    change = total_force[0:3] - own_rows[6:9]
    second = 3.0 * change - step_size * (2.0 * own_rows[9:12] + total_force[3:6])
    third = -2.0 * change + step_size * (own_rows[9:12] + total_force[3:6])
    position = own_rows[0:3] + step_size * step_size * (second / 12.0 + third / 20.0)
    velocity = own_rows[3:6] + step_size * (second / 3.0 + third / 4.0)
    forces = jnp.concatenate([irregular, total_force - irregular], axis=0)
    return (
        jnp.concatenate([position, velocity], axis=0),
        forces,
        jnp.concatenate([second, third], axis=0),
    )


def per_device(star_state, old_force, star_mass, elapsed, active_ids, neighbours, list_length):
    stars_dev = star_state.shape[1]
    devices = lax.axis_size("stars")
    my_rank = lax.axis_index("stars")
    active_dev = active_ids.shape[0]
    listed_count = neighbours.shape[1]
    softening = 0.25 * math.sqrt(listed_count) / (stars_dev * devices)
    predicted = predict(star_state, old_force, star_mass, elapsed)
    carried = jnp.concatenate([predicted[0:6], old_force, elapsed[None, :]], axis=0)
    every_id = lax.all_gather(active_ids, "stars", axis=0, tiled=True)
    owner_rank = every_id // stars_dev
    local_row = every_id - owner_rank * stars_dev
    filled = jnp.where((owner_rank == my_rank)[None, :], carried[:, local_row], 0.0)
    flat_ids = neighbours.reshape(-1)
    entries = flat_ids.shape[0]
    own_rows = lax.psum_scatter(filled, "stars", scatter_dimension=1, tiled=True)
    targets = own_rows[0:6]
    shard_piece = lax.all_gather(predicted, "stars", axis=1, tiled=True)
    running = jnp.zeros((6, active_dev), jnp.float32)
    fetched = jnp.zeros((7, entries), jnp.float32)
    piece_len = shard_piece.shape[1]
    block_size = math.gcd(piece_len, 65536)

    def add_block(block_index, summed):
        sources = lax.dynamic_slice_in_dim(shard_piece, block_index * block_size, block_size, 1)
        return summed + pair_terms(targets, sources, softening)

    running = lax.fori_loop(0, piece_len // block_size, add_block, running)
    inside = (flat_ids >= 0) & (flat_ids < piece_len)
    picked = shard_piece[:, jnp.clip(flat_ids, 0, piece_len - 1)]
    fetched = jnp.where(inside[None, :], picked, fetched)
    total_force, fetched = (running, fetched)
    listed = fetched.reshape(7, active_dev, listed_count)
    in_list = jnp.arange(listed_count)[None, :] < list_length[:, None]
    irregular = listed_sum(targets, listed, in_list, softening)
    return correct(own_rows, total_force, irregular)


def solution(mesh):
    placed = (
        P(None, "stars"),
        P(None, "stars"),
        P("stars"),
        P("stars"),
        P("stars"),
        P("stars", None),
        P("stars"),
    )
    return jax.shard_map(
        per_device,
        mesh=mesh,
        in_specs=placed,
        out_specs=(P(None, "stars"), P(None, "stars"), P(None, "stars")),
        check_vma=False,
    )
```

profile of v0, /device:TPU:0, one launch (start us, length us, event | category | flops | bytes accessed | tf_op | source)
XLA Modules:
  0.0 451.2 jit_solution(5922078266893715996)
XLA Ops:
  7.2 0.0 copy-start.1
  7.2 0.0 copy-start
  7.2 0.0 copy-start.4
  7.2 0.0 all-gather.2.cloned.1.call-start
  7.2 0.7 broadcast_multiply_fusion
  8.0 1.2 multiply_add_fusion.1
  9.2 0.0 copy-start.2
  9.2 0.8 pad_maximum_fusion.1
  9.9 2.0 copy.60
  11.9 0.0 all-gather.2.cloned.1.call-update
  12.0 0.0 copy-done.1
  12.0 0.0 copy-done
  12.0 0.1 pad_maximum_fusion
  12.1 0.6 copy.59
  12.7 0.0 copy-done.4
  12.8 0.2 dynamic-update-slice
  13.0 44.2 %all-reduce = s32[256]{0:T(256)S(1)} all-reduce(s32[256]{0:T(256)S(1)} %dynamic-update-slice), channel_id=1, replica_groups=mesh['stars'=32] {'stars'}, use_global_device_ids=true, to_apply=%add | all-reduce | flops 256 | bytes 2048
  57.2 0.7 gather_fusion
  58.0 0.1 select_bitcast_fusion.1
  58.1 45.1 %all-reduce.1 = f32[13,256]{0,1:T(8,128)S(1)} all-reduce(f32[13,256]{0,1:T(8,128)S(1)} %select_bitcast_fusion.1), channel_id=2, replica_groups=mesh['stars'=32] {'stars'}, use_global_device_ids=true, to_apply=%region_0.1.clone | all-reduce | flops 3328 | bytes 26624
  103.2 0.1 copy.62
  103.3 0.2 multiply_reduce_fusion.3
  103.5 0.0 copy-done.2
  103.5 269.2 %all-gather.2.cloned.1.call-done = f32[7,131072]{0,1:T(8,128)} async-done(((f32[7,4096]{0,1:T(8,128)}), f32[7,131072]{0,1:T(8,128)}) %all-gather.2.cloned.1.call-update) | async-done | bytes 3670032 | tf_op jit(solution)/shard_map/all_gather | solution.py:74
  372.8 35.0 %copy.61 = f32[7,131072]{1,0:T(8,128)} copy(f32[7,131072]{0,1:T(8,128)} %all-gather.2.cloned.1.call-done) | data formatting | bytes 7340032
  407.8 0.0 copy-start.3
  407.8 22.1 %while.14 = (s32[]{:T(128)}, f32[6,8]{1,0:T(8,128)S(1)}, f32[7,131072]{1,0:T(8,128)}, f32[6,8]{1,0:T(8,128)S(1)}, s32[]{:T(128)}, /*index=5*/s32[]{:T(128)}, s32[]{}, s32[]{:T(128)}, s32[]{:T(128)}, s32[]{}) while((s32[]{:T(128)}, f32[6,8]{1,0:T(8,128)S(1)}, f32[7,131072]{1,0:T(8,128)}, f32[6,8]{1,0:T(8,128)S(1)}, s32[]{:T(128)}, ...), condition=%wide.region_6.7_spmd.clone, body=%wide.region_1.6_spmd.clone.sunk | while | flops 24117352 | bytes 23856840 | solution.py:84
  407.8 2.2 dynamic-slice.10
  410.0 2.9 fusion.17
  412.9 2.0 fusion.18
  414.9 0.9 multiply_multiply_fusion.2
  415.8 2.9 fusion.19
  418.8 2.2 dynamic-slice.10
  421.0 2.9 fusion.17
  424.0 2.0 fusion.18
  426.0 0.9 multiply_multiply_fusion.2
  426.9 2.9 fusion.19
  429.8 0.1 copy.63
  429.9 10.5 %gather_fusion.1 = f32[1024,7]{1,0:T(8,128)S(1)} fusion(f32[7,131072]{0,1:T(8,128)} %all-gather.2.cloned.1.call-done, s32[1024]{0:T(1024)S(1)} %broadcast_clamp_fusion), kind=kCustom, calls=%fused_computation.1 | custom fusion | bytes 61440 | tf_op jit(solution)/shard_map/gather | solution.py:86
  440.4 0.2 select_bitcast_fusion
  440.6 0.4 slice_reduce_fusion
  441.0 0.1 multiply_add_fusion.3
  441.1 0.1 fusion.11
  441.1 0.1 pad_maximum_fusion.2
  441.2 0.7 copy.66
  441.9 0.7 copy.67
  442.5 0.5 multiply_reduce_fusion.2
  443.1 0.0 copy-done.3
  443.1 0.1 bitcast_multiply_fusion
  443.1 0.5 multiply_reduce_fusion.1
  443.6 0.1 maximum_subtract_fusion
  443.7 0.7 pad_maximum_fusion.3
  (14 shorter events, 0.1 us)
Async XLA Ops:
  7.2 4.8 %copy-start.1 = (f32[4096]{0:T(1024)S(1)}, f32[4096]{0:T(1024)}, u32[]{:S(2)}) copy-start(f32[4096]{0:T(1024)} %param.12) | copy-start | bytes 49156
  7.2 4.8 %copy-start = (f32[6,4096]{1,0:T(8,128)S(1)}, f32[6,4096]{1,0:T(8,128)}, u32[]{:S(2)}) copy-start(f32[6,4096]{1,0:T(8,128)} %param.10) | copy-start | bytes 294916
  7.2 5.6 %copy-start.4 = (s32[8]{0:T(128)S(1)}, s32[8]{0:T(128)}, u32[]{:S(2)}) copy-start(s32[8]{0:T(128)} %param.13) | copy-start | bytes 100
  7.2 365.6 %all-gather.2.cloned.1.call-start = ((), (), s32[]{:S(2)}) async-start(), calls=%async_computation | async-start | bytes 69206016 | tf_op jit(solution)/shard_map/all_gather | solution.py:74
  9.2 94.3 %copy-start.2 = (s32[8,128]{1,0:T(8,128)S(1)}, s32[8,128]{1,0:T(8,128)}, u32[]{:S(2)}) copy-start(s32[8,128]{1,0:T(8,128)} %param.14) | copy-start | bytes 12292
  407.8 35.3 %copy-start.3 = (s32[8]{0:T(128)S(1)}, s32[8]{0:T(128)}, u32[]{:S(2)}) copy-start(s32[8]{0:T(128)} %param.15) | copy-start | bytes 100
Sparse Core Ops, SparseCore 0:
  12.1 360.6 all-gather.1
where the time goes:
time: 452 us; the launch traced here: 451 us
  waiting for transfers between devices  269 us (60%)
  blocking collectives  89.3 us (20%)
  local copies, waits for them, and re-layouts  61.2 us (14%)
  other arithmetic  17.1 us (4%)
  between operations  14.3 us (3%)
    all_gather x1, waiting for transfers between devices, per_device(): shard_piece = lax.all_gather(predicted, 'stars', axis=1, tiled=True)  269 us
    unnamed x2, blocking collectives  89.3 us
    unnamed x17, local copies, waits for them, and re-layouts  36.7 us
    gather x1, local copies, waits for them, and re-layouts, per_device(): picked = shard_piece[:, jnp.clip(flat_ids, 0, piece_len - 1)]  10.5 us
  transfers between devices with their start and end apart: 1, of which 1 were waited for; matrix products, arithmetic and copies ran while one was open for 0% of the time, Pallas kernels for 0%

commit v1 on v0

v1 whole, which is shorter than its diff:
```python
import functools
import math

import jax
import jax.numpy as jnp
from jax import lax
from jax.experimental import pallas as pl
from jax.experimental.pallas import tpu as pltpu
from jax.sharding import PartitionSpec as P

LANES = 128
F32 = jnp.float32
I32 = jnp.int32
BF16 = jnp.bfloat16
VMEM = pl.BlockSpec(memory_space=pltpu.VMEM)
SMEM = pl.BlockSpec(memory_space=pltpu.SMEM)
PARAMS = pltpu.CompilerParams(vmem_limit_bytes=32 * 1024 * 1024)


def iota(shape, axis):
    return lax.broadcasted_iota(I32, shape, axis)


def split3(value):
    high = value.astype(BF16)
    rest = value - high.astype(F32)
    middle = rest.astype(BF16)
    low = (rest - middle.astype(F32)).astype(BF16)
    return jnp.concatenate([high, middle, low], axis=1)


def pick(table_ref, low, high, rows):
    count = low.shape[1]
    hot = jnp.where(iota((LANES, count), 0) == low, 1.0, 0.0).astype(BF16)
    found = jnp.dot(table_ref[...], jnp.concatenate([hot] * 3, axis=0), preferred_element_type=F32)
    total = jnp.zeros((rows, count), F32)
    for block in range(table_ref.shape[0] // rows):
        total += jnp.where(high == block, found[block * rows : (block + 1) * rows], 0.0)
    return total


def request_kernel(stars_dev, cap, active_ref, length_ref, listed_ref, out_ref):
    devices = out_ref.shape[0]
    targets, slots = listed_ref.shape
    listed = listed_ref[...]
    owner = listed // stars_dev if stars_dev & (stars_dev - 1) else lax.shift_right_logical(listed, stars_dev.bit_length() - 1)
    local = listed - owner * stars_dev
    low = (local & (LANES - 1)).astype(F32)
    high = lax.shift_right_logical(local, 7).astype(F32)
    lane = iota((devices, LANES), 1)
    row = iota((devices, LANES), 0)
    before = jnp.where(iota((slots, 2 * LANES), 0) < iota((slots, 2 * LANES), 1), 1.0, 0.0).astype(BF16)
    mine = [
        jnp.where((owner[k : k + 1] == row) & (lane < length_ref[k]), 1.0, 0.0) for k in range(targets)
    ]
    counts = jnp.dot(jnp.concatenate(mine, axis=0).astype(BF16), before, preferred_element_type=F32)
    base = jnp.zeros((devices, LANES), F32)
    order = iota((LANES, slots), 0).astype(F32)
    lows, highs, hots, bases = [], [], [], [base]
    for k in range(targets):
        ahead = counts[k * devices : (k + 1) * devices]
        rank = jnp.sum(mine[k] * (ahead[:, :LANES] + base), axis=0, keepdims=True)
        hots.append(jnp.where(order == rank, 1.0, 0.0).astype(BF16))
        lows.append((mine[k] * low[k : k + 1]).astype(BF16))
        highs.append((mine[k] * high[k : k + 1]).astype(BF16))
        base = base + ahead[:, LANES:]
        bases.append(base)
    planes = jnp.concatenate([jnp.concatenate(lows, axis=1), jnp.concatenate(highs, axis=1)], axis=0)
    placed = lax.dot_general(
        planes, jnp.concatenate(hots, axis=1), (((1,), (1,)), ((), ())), preferred_element_type=F32
    )
    result = (placed[:devices] + LANES * placed[devices:]).astype(I32)
    for k in range(targets + 1):
        result = jnp.where(lane == cap + k, bases[k].astype(I32), result)
    for k in range(targets):
        result = jnp.where(lane == cap + targets + 1 + k, active_ref[k], result)
    out_ref[...] = result


def predict_kernel(state_ref, force_ref, mass_ref, elapsed_ref, predicted_ref, own_table_ref, star_table_ref):
    for block in range(mass_ref.shape[0]):
        cols = slice(block * LANES, (block + 1) * LANES)
        state, force = state_ref[:, cols], force_ref[:, cols]
        step = elapsed_ref[block : block + 1]
        accel, jerk = force[0:3], force[3:6]
        position = state[0:3] + step * (state[3:6] + step * (0.5 * accel + step * jerk / 6.0))
        velocity = state[3:6] + step * (accel + 0.5 * step * jerk)
        stars = jnp.concatenate([position, velocity, mass_ref[block : block + 1], step], axis=0)
        predicted_ref[:, cols] = stars
        rows = jnp.concatenate([stars, force, jnp.zeros((2, LANES), F32)], axis=0)
        own_table_ref[block * 16 : (block + 1) * 16] = split3(rows)
        star_table_ref[block * 8 : (block + 1) * 8] = split3(stars)


def own_kernel(stars_dev, cap, targets, request_ref, table_ref, own_ref, out_ref):
    devices = request_ref.shape[0]
    first = cap + targets + 1
    lane = iota((devices, LANES), 1)
    ids = pltpu.roll(request_ref[...].astype(F32), LANES - first, 1)
    ids = jnp.where(lane < targets, ids, 0.0)
    width = targets
    while width < LANES:
        ids = ids + pltpu.roll(ids, width, 1)
        width *= 2
    per_tile = LANES // targets
    lane, row = iota((per_tile, LANES), 1), iota((per_tile, LANES), 0)
    on_row = (lane >= row * targets) & (lane < (row + 1) * targets)
    tiles = devices // per_tile
    flat = [
        jnp.sum(jnp.where(on_row, ids[t * per_tile : (t + 1) * per_tile], 0.0), axis=0, keepdims=True)
        for t in range(tiles)
    ]
    local = jnp.concatenate(flat, axis=1).astype(I32) - lax.axis_index("stars") * stars_dev
    inside = (local >= 0) & (local < stars_dev)
    low = jnp.where(inside, local & (LANES - 1), -1)
    own = pick(table_ref, low, lax.shift_right_logical(local, 7), 16)
    own_ref[...] = own
    block = jnp.concatenate([own[0:6, t * LANES : (t + 1) * LANES] for t in range(tiles)], axis=0)
    height = math.lcm(block.shape[0], 8)
    block = jnp.concatenate([block] * (height // block.shape[0]), axis=0)
    for i in range(out_ref.shape[0] // height):
        out_ref[i * height : (i + 1) * height] = block


def listed_kernel(cap, targets, request_ref, table_ref, own_ref, listed_ref, slot_ref, back_ref):
    devices = request_ref.shape[0]
    request = request_ref[...]
    lane = iota((devices, LANES), 1)
    slot = jnp.zeros((devices, LANES), I32)
    for k in range(targets):
        slot += jnp.where(lane >= request[:, cap + k + 1 : cap + k + 2], 1, 0)
    per_row = LANES // cap
    rows = devices // per_row
    lane = iota((rows, LANES), 1)
    ids, slots = request[:rows], slot[:rows]
    for j in range(1, per_row):
        here = lane >= j * cap
        part = slice(j * rows, (j + 1) * rows)
        ids = jnp.where(here, pltpu.roll(request[part], j * cap, 1), ids)
        slots = jnp.where(here, pltpu.roll(slot[part], j * cap, 1), slots)
    slot_ref[...] = slots
    low, high = ids & (LANES - 1), lax.shift_right_logical(ids, 7)
    for pair in range(rows // 2):
        halves = [slice(2 * pair + i, 2 * pair + i + 1) for i in range(2)]
        found = pick(
            table_ref,
            jnp.concatenate([low[half] for half in halves], axis=1),
            jnp.concatenate([high[half] for half in halves], axis=1),
            8,
        )
        for i in range(2):
            listed_ref[(2 * pair + i) * 8 : (2 * pair + i + 1) * 8] = found[:, i * LANES : (i + 1) * LANES]
    own = own_ref[...]
    per_tile = LANES // targets
    lane, row = iota((per_tile, LANES), 1), iota((per_tile, LANES), 0)
    on_row = (lane >= row * targets) & (lane < (row + 1) * targets)
    same = jnp.where(iota((LANES, LANES), 0) % targets == iota((LANES, LANES), 1) % targets, 1.0, 0.0).astype(BF16)
    same = jnp.concatenate([same] * 3, axis=0)
    for t in range(devices // per_tile):
        tile = own[:, t * LANES : (t + 1) * LANES]
        spread = jnp.concatenate([jnp.where(on_row, tile[c : c + 1], 0.0) for c in range(16)], axis=0)
        folded = jnp.dot(split3(spread), same, preferred_element_type=F32)
        back = jnp.zeros((per_tile, LANES), F32)
        for c in range(LANES // targets):
            here = (lane >= c * targets) & (lane < (c + 1) * targets)
            back = jnp.where(here, folded[c * per_tile : (c + 1) * per_tile], back)
        back_ref[t * per_tile : (t + 1) * per_tile] = back


def pair_sums(target, source, mass, softening, sums):
    x, y, z = (source[c] - target[c] for c in range(3))
    u, v, w = (source[c] - target[c] for c in range(3, 6))
    inverse = lax.rsqrt(x * x + y * y + z * z + softening)
    square = inverse * inverse
    strength = mass * inverse * square
    radial = (x * u + y * v + z * w) * (strength * square)
    return (
        sums[0] + strength * x,
        sums[1] + strength * y,
        sums[2] + strength * z,
        sums[3] + strength * u,
        sums[4] + strength * v,
        sums[5] + strength * w,
        sums[6] + radial * x,
        sums[7] + radial * y,
        sums[8] + radial * z,
    )


def force_kernel(
    softening, cap, targets, group_step, source_step,
    sent_ref, predicted_ref, listed_ref, slot_ref, back_ref, out_ref, target_ref, source_ref,
):
    devices = back_ref.shape[0]
    rows = sent_ref.shape[0] // devices
    height = math.lcm(rows, 8)
    sent = sent_ref[0:height]
    for i in range(1, sent_ref.shape[0] // height):
        sent = sent + sent_ref[i * height : (i + 1) * height]
    block = sent[0:rows]
    for i in range(1, height // rows):
        block = block + sent[i * rows : (i + 1) * rows]
    for t in range(rows // 6):
        tile = jnp.concatenate([block[t * 6 : (t + 1) * 6], jnp.zeros((2, LANES), F32)], axis=0)
        target_ref[t * LANES : (t + 1) * LANES, 0:8] = tile.T
    blocks = predicted_ref.shape[1] // LANES
    for s in range(blocks):
        tile = predicted_ref[:, s * LANES : (s + 1) * LANES]
        for c in range(7):
            source_ref[s, c] = jnp.broadcast_to(tile[c : c + 1], (8, LANES))
    lane, row = iota((8, LANES), 1), iota((8, LANES), 0)
    zero = jnp.zeros((8, LANES), F32)

    def finish(sums):
        return [*sums[0:3], *(sums[3 + c] - 3.0 * sums[6 + c] for c in range(3))]

    def add_groups(step, _):
        groups = [step * group_step + i for i in range(group_step)]
        held = []
        for group in groups:
            tile = target_ref[pl.ds(pl.multiple_of(group * 8, 8), 8), 0:8]
            held.append([jnp.broadcast_to(tile[:, c : c + 1], (8, LANES)) for c in range(6)])

        def add_sources(block_step, sums):
            for i in range(source_step):
                source = [source_ref[block_step * source_step + i, c] for c in range(7)]
                sums = tuple(
                    pair_sums(held[n], source, source[6], softening, sums[n]) for n in range(group_step)
                )
            return sums

        sums = lax.fori_loop(0, blocks // source_step, add_sources, tuple((zero,) * 9 for _ in groups))
        for n, group in enumerate(groups):
            packed = lax.rem(group, slot_ref.shape[0])
            part = lax.div(group, slot_ref.shape[0])
            near = listed_ref[pl.ds(pl.multiple_of(packed * 8, 8), 8), :]
            slot = slot_ref[pl.ds(packed, 1), :]
            here = (slot == row) & (lane >= part * cap) & (lane < (part + 1) * cap)
            mass = jnp.where(here, near[6:7], 0.0)
            irregular = pair_sums(held[n], [near[c : c + 1] for c in range(6)], mass, softening, (zero,) * 9)
            result = zero
            for c, values in enumerate(finish(sums[n]) + finish(irregular)):
                result = jnp.where(lane == c * targets + row, jnp.sum(values, axis=1, keepdims=True), result)
            out_ref[pl.ds(2 * group, 1), :] = jnp.sum(result, axis=0, keepdims=True)
            out_ref[pl.ds(2 * group + 1, 1), :] = back_ref[pl.ds(group, 1), :]
        return 0

    lax.fori_loop(0, devices // group_step, add_groups, 0)


def correct_kernel(targets, sums_ref, state_ref, forces_ref, terms_ref):
    total = sums_ref[0:8]
    for i in range(1, sums_ref.shape[0] // 8):
        total = total + sums_ref[i * 8 : (i + 1) * 8]
    pair = total[0:2] + total[2:4] + total[4:6] + total[6:8]

    def rows(which, first, count):
        return jnp.concatenate(
            [pair[which : which + 1, c * targets : (c + 1) * targets] for c in range(first, first + count)], axis=0
        )

    accel, jerk, irregular = rows(0, 0, 3), rows(0, 3, 3), rows(0, 6, 6)
    position, velocity, step = rows(1, 0, 3), rows(1, 3, 3), rows(1, 7, 1)
    old_accel, old_jerk = rows(1, 8, 3), rows(1, 11, 3)
    change = accel - old_accel
    second = 3.0 * change - step * (2.0 * old_jerk + jerk)
    third = -2.0 * change + step * (old_jerk + jerk)
    state_ref[0:3] = position + step * step * (second / 12.0 + third / 20.0)
    state_ref[3:6] = velocity + step * (second / 3.0 + third / 4.0)
    forces_ref[0:6] = irregular
    forces_ref[6:9] = accel - irregular[0:3]
    forces_ref[9:12] = jerk - irregular[3:6]
    terms_ref[0:3] = second
    terms_ref[3:6] = third


def exchange(rows, devices):
    wide = rows.reshape(devices, 1, -1)
    return lax.all_to_all(wide, "stars", 0, 0, tiled=True).reshape(rows.shape)


def per_device(star_state, old_force, star_mass, elapsed, active_ids, neighbours, list_length):
    stars_dev = star_state.shape[1]
    devices = lax.axis_size("stars")
    targets, slots = neighbours.shape
    active = devices * targets
    cap = 2 * targets * slots // devices
    blocks = stars_dev // LANES
    packed = devices * cap // LANES
    softening = 0.25 * math.sqrt(slots) / (stars_dev * devices)

    def shape(*dims, dtype=F32):
        return jax.ShapeDtypeStruct(dims, dtype)

    def cost(flops):
        return pl.CostEstimate(flops=flops, bytes_accessed=1 << 20, transcendentals=0)

    request = pl.pallas_call(
        functools.partial(request_kernel, stars_dev, cap),
        out_shape=shape(devices, LANES, dtype=I32),
        in_specs=[SMEM, SMEM, VMEM],
        out_specs=VMEM,
        compiler_params=PARAMS,
    )(active_ids, list_length, neighbours)
    request = exchange(request, devices)
    predicted, own_table, star_table = pl.pallas_call(
        predict_kernel,
        out_shape=(
            shape(8, stars_dev),
            shape(blocks * 16, 3 * LANES, dtype=BF16),
            shape(blocks * 8, 3 * LANES, dtype=BF16),
        ),
        in_specs=[VMEM] * 4,
        out_specs=(VMEM,) * 3,
        compiler_params=PARAMS,
        cost_estimate=cost(1 << 20),
    )(star_state, old_force, star_mass.reshape(blocks, LANES), elapsed.reshape(blocks, LANES))
    own, sent = pl.pallas_call(
        functools.partial(own_kernel, stars_dev, cap, targets),
        out_shape=(shape(16, active), shape(devices * 6 * active // LANES, LANES)),
        in_specs=[VMEM] * 2,
        out_specs=(VMEM,) * 2,
        compiler_params=PARAMS,
    )(request, own_table)
    sent = exchange(sent, devices)
    listed, slot, back = pl.pallas_call(
        functools.partial(listed_kernel, cap, targets),
        out_shape=(shape(packed * 8, LANES), shape(packed, LANES, dtype=I32), shape(devices, LANES)),
        in_specs=[VMEM] * 3,
        out_specs=(VMEM,) * 3,
        compiler_params=PARAMS,
        cost_estimate=cost(1 << 24),
    )(request, star_table, own)
    sums = pl.pallas_call(
        functools.partial(force_kernel, softening, cap, targets, 2, 4),
        out_shape=shape(devices * 2, LANES),
        in_specs=[VMEM] * 5,
        out_specs=VMEM,
        scratch_shapes=[pltpu.VMEM((active, LANES), F32), pltpu.VMEM((blocks, 7, 8, LANES), F32)],
        compiler_params=PARAMS,
    )(sent, predicted, listed, slot, back)
    sums = exchange(sums, devices)
    return pl.pallas_call(
        functools.partial(correct_kernel, targets),
        out_shape=(shape(6, targets), shape(12, targets), shape(6, targets)),
        in_specs=[VMEM],
        out_specs=(VMEM,) * 3,
        compiler_params=PARAMS,
    )(sums)


def solution(mesh):
    placed = (
        P(None, "stars"),
        P(None, "stars"),
        P("stars"),
        P("stars"),
        P("stars"),
        P("stars", None),
        P("stars"),
    )
    return jax.shard_map(
        per_device,
        mesh=mesh,
        in_specs=placed,
        out_specs=(P(None, "stars"), P(None, "stars"), P(None, "stars")),
        check_vma=False,
    )
```

time: 452 us -> 53.1 us (0.12)
  waiting for transfers between devices: 269 us -> 12.9 us
  blocking collectives: 89.3 us -> 9.67 us
  local copies, waits for them, and re-layouts: 61.2 us -> 4.47 us
  other arithmetic: 17.1 us -> 0 us
  Pallas kernels: 0 us -> 15.1 us
  between operations: 14.3 us -> 0.7 us
  starting transfers between devices: 0.04 us -> 9.87 us
    all_gather x1 -> x0, waiting for transfers between devices: 269 us -> none  [per_device(): shard_piece = lax.all_gather(predicted, 'stars', axis=1, tiled=True)]
    unnamed x2 -> x0, blocking collectives: 89.3 us -> none
    unnamed x17 -> x14, local copies, waits for them, and re-layouts: 36.7 us -> 3.8 us
    pallas_call x0 -> x6, Pallas kernels: none -> 15.1 us  [the longest x1 9.89 us: per_device(): pl.pallas_call(functools.partial(force_kernel, softening, cap, targets, 2...]
    all_to_all x0 -> x2, waiting for transfers between devices: none -> 12.9 us  [exchange(): return lax.all_to_all(wide, 'stars', 0, 0, tiled=True).reshape(rows.shape)]
    gather x2 -> x0, local copies, waits for them, and re-layouts: 11.2 us -> none  [the longest x1 10.5 us: per_device(): picked = shard_piece[:, jnp.clip(flat_ids, 0, piece_len - 1)]]
    reduce_sum x6 -> x0, other arithmetic: 10.9 us -> none  [the longest x2 5.89 us: pair_terms(): accel_sum = jnp.sum(strength[None] * separation, axis=2)]
    slice x7 -> x0, local copies, waits for them, and re-layouts: 10.6 us -> none  [the longest x4 5.87 us: pair_terms(): relative = sources[3:6, None, :] - targets[3:6, :, None]]
  transfers between devices with their start and end apart: 1 -> 2, of which waited for: 1 -> 2; matrix products, arithmetic and copies ran while one was open for 0% -> 0% of each run, Pallas kernels for 0% -> 2%
where the time goes in v1:
time: 53.1 us; the launch traced here: 52.8 us
  Pallas kernels  15.1 us (28%)
  waiting for transfers between devices  12.9 us (24%)
  starting transfers between devices  9.87 us (19%)
  blocking collectives  9.67 us (18%)
  local copies, waits for them, and re-layouts  4.47 us (8%)
  between operations  0.7 us (1%)
    all_to_all x2, waiting for transfers between devices, exchange(): return lax.all_to_all(wide, 'stars', 0, 0, tiled=True).reshape(rows.shape)  12.9 us
    pallas_call x1, Pallas kernels, per_device(): pl.pallas_call(functools.partial(force_kernel, softening, cap, targets, 2...  9.89 us
    all_to_all x2, starting transfers between devices, exchange(): return lax.all_to_all(wide, 'stars', 0, 0, tiled=True).reshape(rows.shape)  9.87 us
    all_to_all x1, blocking collectives, exchange(): return lax.all_to_all(wide, 'stars', 0, 0, tiled=True).reshape(rows.shape)  9.67 us
    unnamed x14, local copies, waits for them, and re-layouts  3.8 us
    pallas_call x1, Pallas kernels, per_device(): pl.pallas_call(functools.partial(request_kernel, stars_dev, cap), out_sha...  1.56 us
    pallas_call x1, Pallas kernels, per_device(): pl.pallas_call(functools.partial(own_kernel, stars_dev, cap, targets), ou...  1.35 us
    pallas_call x1, Pallas kernels, per_device(): pl.pallas_call(functools.partial(correct_kernel, targets), out_shape=(sha...  1.09 us
  transfers between devices with their start and end apart: 2, of which 2 were waited for; matrix products, arithmetic and copies ran while one was open for 0% of the time, Pallas kernels for 2%

profile of v1, /device:TPU:0, one launch (start us, length us, event | category | flops | bytes accessed | tf_op | source)
XLA Modules:
  0.0 52.8 jit_solution(15350492755181858889)
XLA Ops:
  0.6 0.0 copy-start.4
  0.6 0.7 %copy-done.4 = s32[8,128]{1,0:T(8,128)S(1)} copy-done((s32[8,128]{1,0:T(8,128)S(1)}, s32[8,128]{1,0:T(8,128)}, u32[]{:S(2)}) %copy-start.4) | copy-done | bytes 4120
  1.3 0.0 copy-start.5
  1.3 0.7 %copy-done.5 = s32[8]{0:T(128)S(1)} copy-done((s32[8]{0:T(128)S(1)}, s32[8]{0:T(128)}, u32[]{:S(2)}) %copy-start.5) | copy-done | bytes 56
  2.0 0.0 copy-start.6
  2.0 0.7 %copy-done.6 = s32[8]{0:T(128)S(1)} copy-done((s32[8]{0:T(128)S(1)}, s32[8]{0:T(128)}, u32[]{:S(2)}) %copy-start.6) | copy-done | bytes 56
  2.6 1.6 %shard_map.94 = s32[32,128]{1,0:T(8,128)} custom-call(s32[8]{0:T(128)S(1)} %copy-done.5, s32[8]{0:T(128)S(1)} %copy-done.6, s32[8,128]{1,0:T(8,128)S(1)} %copy-done.4), custom_call_target="tpu_custom_call" | custom-call | tf_op jit(solution)/shard_map/pallas_call | solution.py:298
  4.2 0.0 copy-start.2
  4.2 0.0 copy-start.3
  4.2 7.3 %all-to-all-start = ((s32[32,1,128]{2,1,0:T(1,128)}), s32[32,1,128]{2,1,0:T(1,128)S(1)}, u32[]{:S(2)}, u32[]{:S(2)}) async-start(s32[32,1,128]{2,1,0:T(1,128)} %bitcast.1), calls=%async_computation | async-start | bytes 32768 | tf_op jit(solution)/shard_map/all_to_all | solution.py:279
  11.5 0.0 copy-done.2
  11.5 0.0 copy-done.3
  11.5 0.0 copy-start
  11.5 0.9 %copy-done = f32[6,4096]{1,0:T(8,128)S(1)} copy-done((f32[6,4096]{1,0:T(8,128)S(1)}, f32[6,4096]{1,0:T(8,128)}, u32[]{:S(2)}) %copy-start) | copy-done | bytes 98328
  12.4 0.0 copy-start.1
  12.4 0.9 %copy-done.1 = f32[6,4096]{1,0:T(8,128)S(1)} copy-done((f32[6,4096]{1,0:T(8,128)S(1)}, f32[6,4096]{1,0:T(8,128)}, u32[]{:S(2)}) %copy-start.1) | copy-done | bytes 98328
  13.3 0.2 shard_map.95
  13.5 5.1 %all-to-all-done = s32[32,1,128]{2,1,0:T(1,128)S(1)} async-done(((s32[32,1,128]{2,1,0:T(1,128)}), s32[32,1,128]{2,1,0:T(1,128)S(1)}, u32[]{:S(2)}, u32[]{:S(2)}) %all-to-all-start) | async-done | bytes 16416 | tf_op jit(solution)/shard_map/all_to_all | solution.py:279
  18.6 1.3 %shard_map.96 = (f32[16,256]{1,0:T(8,128)S(1)}, f32[384,128]{1,0:T(8,128)}) custom-call(s32[32,128]{1,0:T(8,128)S(1)} %bitcast.11, bf16[512,384]{1,0:T(8,128)(2,1)S(1)} %get-tuple-element.11.table_ref), custom_call_target="tpu_custom_call" | custom-call | tf_op jit(solution)/shard_map/pallas_call | solution.py:318
  20.0 2.6 %all-to-all-start.1 = ((f32[32,1,1536]{2,1,0:T(1,128)}), f32[32,1,1536]{2,1,0:T(1,128)S(1)}, u32[]{:S(2)}, u32[]{:S(2)}) async-start(f32[32,1,1536]{2,1,0:T(1,128)} %bitcast.5), calls=%async_computation.1 | async-start | bytes 393216 | tf_op jit(solution)/shard_map/all_to_all | solution.py:279
  22.6 1.0 %shard_map.97 = (f32[128,128]{1,0:T(8,128)S(1)}, s32[16,128]{1,0:T(8,128)S(1)}, f32[32,128]{1,0:T(8,128)S(1)}) custom-call(s32[32,128]{1,0:T(8,128)S(1)} %bitcast.12, bf16[256,384]{1,0:T(8,128)(2,1)S(1)} %get-tuple-element.14.table_ref, f32[16,256]{1,0:T(8,128)S(1)} %get-tuple-element.15.own_ref), custom_call_target="tpu_custom_call" | custom-call | flops 16777216 | bytes 1048576 | tf_op jit(solution)/shard_map/pallas_call | solution.py:326
  23.6 7.8 %all-to-all-done.1 = f32[32,1,1536]{2,1,0:T(1,128)S(1)} async-done(((f32[32,1,1536]{2,1,0:T(1,128)}), f32[32,1,1536]{2,1,0:T(1,128)S(1)}, u32[]{:S(2)}, u32[]{:S(2)}) %all-to-all-start.1) | async-done | bytes 196640 | tf_op jit(solution)/shard_map/all_to_all | solution.py:279
  31.5 9.9 %shard_map.98 = f32[64,128]{1,0:T(8,128)S(1)} custom-call(f32[384,128]{1,0:T(8,128)S(1)} %bitcast.10, f32[8,4096]{1,0:T(8,128)S(1)} %get-tuple-element.13.predicted_ref, f32[128,128]{1,0:T(8,128)S(1)} %get-tuple-element.16.listed_ref, s32[16,128]{1,0:T(8,128)S(1)} %get-tuple-element.17.slot_ref, f32[32,128]{1,0:T(8,128)S(1)} %get-tuple-element.18.back_ref), custom_call_target="tpu_custom_call" | custom-call | tf_op jit(solution)/shard_map/pallas_call | solution.py:334
  41.4 9.7 %all_to_all.15 = f32[32,1,256]{2,1,0:T(1,128)S(1)} all-to-all(f32[32,1,256]{2,1,0:T(1,128)S(1)} %bitcast.13), channel_id=1, replica_groups=mesh['stars'=32] {'stars'}, dimensions={0} | all-to-all | bytes 65536 | tf_op jit(solution)/shard_map/all_to_all | solution.py:279
  51.0 1.1 %shard_map.99 = (f32[6,8]{1,0:T(8,128)}, f32[12,8]{1,0:T(8,128)S(1)}, f32[6,8]{1,0:T(8,128)}) custom-call(f32[64,128]{1,0:T(8,128)S(1)} %bitcast.14), custom_call_target="tpu_custom_call" | custom-call | tf_op jit(solution)/shard_map/pallas_call | solution.py:343
  52.1 0.7 %copy.14 = f32[12,8]{0,1:T(8,128)} copy(f32[12,8]{1,0:T(8,128)S(1)} %get-tuple-element.23) | data formatting | bytes 768 | tf_op jit(solution)/shard_map/pallas_call | solution.py:343
Async XLA Ops:
  0.6 0.7 %copy-start.4 = (s32[8,128]{1,0:T(8,128)S(1)}, s32[8,128]{1,0:T(8,128)}, u32[]{:S(2)}) copy-start(s32[8,128]{1,0:T(8,128)} %listed_ref.1) | copy-start | bytes 12292
  1.3 0.7 %copy-start.5 = (s32[8]{0:T(128)S(1)}, s32[8]{0:T(128)}, u32[]{:S(2)}) copy-start(s32[8]{0:T(128)} %active_ref.1) | copy-start | bytes 100
  2.0 0.7 %copy-start.6 = (s32[8]{0:T(128)S(1)}, s32[8]{0:T(128)}, u32[]{:S(2)}) copy-start(s32[8]{0:T(128)} %length_ref.1) | copy-start | bytes 100
  4.2 7.3 %copy-start.2 = (f32[4096]{0:T(1024)S(1)}, f32[4096]{0:T(1024)}, u32[]{:S(2)}) copy-start(f32[4096]{0:T(1024)} %param.9) | copy-start | bytes 49156
  4.2 7.3 %copy-start.3 = (f32[4096]{0:T(1024)S(1)}, f32[4096]{0:T(1024)}, u32[]{:S(2)}) copy-start(f32[4096]{0:T(1024)} %param.10) | copy-start | bytes 49156
  4.2 14.4 %all-to-all-start = ((s32[32,1,128]{2,1,0:T(1,128)}), s32[32,1,128]{2,1,0:T(1,128)S(1)}, u32[]{:S(2)}, u32[]{:S(2)}) async-start(s32[32,1,128]{2,1,0:T(1,128)} %bitcast.1), calls=%async_computation | async-start | bytes 32768 | tf_op jit(solution)/shard_map/all_to_all | solution.py:279
  11.5 0.9 %copy-start = (f32[6,4096]{1,0:T(8,128)S(1)}, f32[6,4096]{1,0:T(8,128)}, u32[]{:S(2)}) copy-start(f32[6,4096]{1,0:T(8,128)} %state_ref.1) | copy-start | bytes 294916
  12.4 0.9 %copy-start.1 = (f32[6,4096]{1,0:T(8,128)S(1)}, f32[6,4096]{1,0:T(8,128)}, u32[]{:S(2)}) copy-start(f32[6,4096]{1,0:T(8,128)} %force_ref.1) | copy-start | bytes 294916
  20.0 11.5 %all-to-all-start.1 = ((f32[32,1,1536]{2,1,0:T(1,128)}), f32[32,1,1536]{2,1,0:T(1,128)S(1)}, u32[]{:S(2)}, u32[]{:S(2)}) async-start(f32[32,1,1536]{2,1,0:T(1,128)} %bitcast.5), calls=%async_computation.1 | async-start | bytes 393216 | tf_op jit(solution)/shard_map/all_to_all | solution.py:279

commit v2 on v1

--- a/solution.py
+++ b/solution.py
@@ -13,7 +13,7 @@
 I32 = jnp.int32
 BF16 = jnp.bfloat16
 VMEM = pl.BlockSpec(memory_space=pltpu.VMEM)
-SMEM = pl.BlockSpec(memory_space=pltpu.SMEM)
+HBM = pl.BlockSpec(memory_space=pltpu.HBM)
 PARAMS = pltpu.CompilerParams(vmem_limit_bytes=32 * 1024 * 1024)
 
 
@@ -29,17 +29,32 @@
     return jnp.concatenate([high, middle, low], axis=1)
 
 
-def pick(table_ref, low, high, rows):
-    count = low.shape[1]
+def folding(targets):
+    same = iota((LANES, LANES), 0) % targets == iota((LANES, LANES), 1) % targets
+    return jnp.concatenate([jnp.where(same, 1.0, 0.0).astype(BF16)] * 3, axis=0)
+
+
+def pick(table_ref, column):
+    count = column.shape[1]
+    low = jnp.where(column < 0, -1, column & (LANES - 1))
+    high = lax.shift_right_logical(column, 7)
     hot = jnp.where(iota((LANES, count), 0) == low, 1.0, 0.0).astype(BF16)
     found = jnp.dot(table_ref[...], jnp.concatenate([hot] * 3, axis=0), preferred_element_type=F32)
-    total = jnp.zeros((rows, count), F32)
-    for block in range(table_ref.shape[0] // rows):
-        total += jnp.where(high == block, found[block * rows : (block + 1) * rows], 0.0)
+    total = jnp.zeros((8, count), F32)
+    for block in range(table_ref.shape[0] // 8):
+        total += jnp.where(high == block, found[block * 8 : (block + 1) * 8], 0.0)
     return total
 
 
-def request_kernel(stars_dev, cap, active_ref, length_ref, listed_ref, out_ref):
+def request_kernel(
+    stars_dev, cap, active_hbm, length_hbm, listed_hbm, out_ref, active_ref, length_ref, listed_ref, sems
+):
+    pairs = ((listed_hbm, listed_ref), (length_hbm, length_ref), (active_hbm, active_ref))
+    copies = [pltpu.make_async_copy(*pair, sems.at[i]) for i, pair in enumerate(pairs)]
+    for copy in copies:
+        copy.start()
+    for copy in copies:
+        copy.wait()
     devices = out_ref.shape[0]
     targets, slots = listed_ref.shape
     listed = listed_ref[...]
@@ -77,7 +92,7 @@
     out_ref[...] = result
 
 
-def predict_kernel(state_ref, force_ref, mass_ref, elapsed_ref, predicted_ref, own_table_ref, star_table_ref):
+def predict_kernel(state_ref, force_ref, mass_ref, elapsed_ref, source_ref, star_table_ref, force_table_ref):
     for block in range(mass_ref.shape[0]):
         cols = slice(block * LANES, (block + 1) * LANES)
         state, force = state_ref[:, cols], force_ref[:, cols]
@@ -86,13 +101,14 @@
         position = state[0:3] + step * (state[3:6] + step * (0.5 * accel + step * jerk / 6.0))
         velocity = state[3:6] + step * (accel + 0.5 * step * jerk)
         stars = jnp.concatenate([position, velocity, mass_ref[block : block + 1], step], axis=0)
-        predicted_ref[:, cols] = stars
-        rows = jnp.concatenate([stars, force, jnp.zeros((2, LANES), F32)], axis=0)
-        own_table_ref[block * 16 : (block + 1) * 16] = split3(rows)
-        star_table_ref[block * 8 : (block + 1) * 8] = split3(stars)
-
-
-def own_kernel(stars_dev, cap, targets, request_ref, table_ref, own_ref, out_ref):
+        for c in range(7):
+            source_ref[block, c] = jnp.broadcast_to(stars[c : c + 1], (8, LANES))
+        rows = slice(block * 8, (block + 1) * 8)
+        star_table_ref[rows] = split3(stars)
+        force_table_ref[rows] = split3(jnp.concatenate([force, jnp.zeros((2, LANES), F32)], axis=0))
+
+
+def own_kernel(stars_dev, cap, targets, request_ref, table_ref, own_ref, local_ref, out_ref):
     devices = request_ref.shape[0]
     first = cap + targets + 1
     lane = iota((devices, LANES), 1)
@@ -111,9 +127,9 @@
         for t in range(tiles)
     ]
     local = jnp.concatenate(flat, axis=1).astype(I32) - lax.axis_index("stars") * stars_dev
-    inside = (local >= 0) & (local < stars_dev)
-    low = jnp.where(inside, local & (LANES - 1), -1)
-    own = pick(table_ref, low, lax.shift_right_logical(local, 7), 16)
+    local = jnp.where((local >= 0) & (local < stars_dev), local, -1)
+    local_ref[...] = jnp.broadcast_to(local, local_ref.shape)
+    own = pick(table_ref, local)
     own_ref[...] = own
     block = jnp.concatenate([own[0:6, t * LANES : (t + 1) * LANES] for t in range(tiles)], axis=0)
     height = math.lcm(block.shape[0], 8)
@@ -122,7 +138,9 @@
         out_ref[i * height : (i + 1) * height] = block
 
 
-def listed_kernel(cap, targets, request_ref, table_ref, own_ref, listed_ref, slot_ref, back_ref):
+def listed_kernel(
+    cap, targets, request_ref, star_table_ref, force_table_ref, own_ref, local_ref, listed_ref, slot_ref, back_ref
+):
     devices = request_ref.shape[0]
     request = request_ref[...]
     lane = iota((devices, LANES), 1)
@@ -139,27 +157,20 @@
         ids = jnp.where(here, pltpu.roll(request[part], j * cap, 1), ids)
         slots = jnp.where(here, pltpu.roll(slot[part], j * cap, 1), slots)
     slot_ref[...] = slots
-    low, high = ids & (LANES - 1), lax.shift_right_logical(ids, 7)
     for pair in range(rows // 2):
-        halves = [slice(2 * pair + i, 2 * pair + i + 1) for i in range(2)]
-        found = pick(
-            table_ref,
-            jnp.concatenate([low[half] for half in halves], axis=1),
-            jnp.concatenate([high[half] for half in halves], axis=1),
-            8,
-        )
-        for i in range(2):
-            listed_ref[(2 * pair + i) * 8 : (2 * pair + i + 1) * 8] = found[:, i * LANES : (i + 1) * LANES]
-    own = own_ref[...]
+        halves = [2 * pair, 2 * pair + 1]
+        found = pick(star_table_ref, jnp.concatenate([ids[half : half + 1] for half in halves], axis=1))
+        for i, half in enumerate(halves):
+            listed_ref[half * 8 : (half + 1) * 8] = found[:, i * LANES : (i + 1) * LANES]
+    own = jnp.concatenate([own_ref[...], pick(force_table_ref, local_ref[0:1])], axis=0)
     per_tile = LANES // targets
     lane, row = iota((per_tile, LANES), 1), iota((per_tile, LANES), 0)
     on_row = (lane >= row * targets) & (lane < (row + 1) * targets)
-    same = jnp.where(iota((LANES, LANES), 0) % targets == iota((LANES, LANES), 1) % targets, 1.0, 0.0).astype(BF16)
-    same = jnp.concatenate([same] * 3, axis=0)
+    fold = folding(targets)
     for t in range(devices // per_tile):
         tile = own[:, t * LANES : (t + 1) * LANES]
         spread = jnp.concatenate([jnp.where(on_row, tile[c : c + 1], 0.0) for c in range(16)], axis=0)
-        folded = jnp.dot(split3(spread), same, preferred_element_type=F32)
+        folded = jnp.dot(split3(spread), fold, preferred_element_type=F32)
         back = jnp.zeros((per_tile, LANES), F32)
         for c in range(LANES // targets):
             here = (lane >= c * targets) & (lane < (c + 1) * targets)
@@ -173,23 +184,20 @@
     inverse = lax.rsqrt(x * x + y * y + z * z + softening)
     square = inverse * inverse
     strength = mass * inverse * square
-    radial = (x * u + y * v + z * w) * (strength * square)
+    radial = (x * u + y * v + z * w) * (3.0 * square)
     return (
         sums[0] + strength * x,
         sums[1] + strength * y,
         sums[2] + strength * z,
-        sums[3] + strength * u,
-        sums[4] + strength * v,
-        sums[5] + strength * w,
-        sums[6] + radial * x,
-        sums[7] + radial * y,
-        sums[8] + radial * z,
+        sums[3] + strength * (u - radial * x),
+        sums[4] + strength * (v - radial * y),
+        sums[5] + strength * (w - radial * z),
     )
 
 
 def force_kernel(
-    softening, cap, targets, group_step, source_step,
-    sent_ref, predicted_ref, listed_ref, slot_ref, back_ref, out_ref, target_ref, source_ref,
+    softening, cap, targets, group_step, source_step, sum_step,
+    sent_ref, source_ref, listed_ref, slot_ref, back_ref, out_ref, target_ref, sums_ref,
 ):
     devices = back_ref.shape[0]
     rows = sent_ref.shape[0] // devices
@@ -203,16 +211,9 @@
     for t in range(rows // 6):
         tile = jnp.concatenate([block[t * 6 : (t + 1) * 6], jnp.zeros((2, LANES), F32)], axis=0)
         target_ref[t * LANES : (t + 1) * LANES, 0:8] = tile.T
-    blocks = predicted_ref.shape[1] // LANES
-    for s in range(blocks):
-        tile = predicted_ref[:, s * LANES : (s + 1) * LANES]
-        for c in range(7):
-            source_ref[s, c] = jnp.broadcast_to(tile[c : c + 1], (8, LANES))
+    blocks = source_ref.shape[0]
     lane, row = iota((8, LANES), 1), iota((8, LANES), 0)
-    zero = jnp.zeros((8, LANES), F32)
-
-    def finish(sums):
-        return [*sums[0:3], *(sums[3 + c] - 3.0 * sums[6 + c] for c in range(3))]
+    zeros = (jnp.zeros((8, LANES), F32),) * 6
 
     def add_groups(step, _):
         groups = [step * group_step + i for i in range(group_step)]
@@ -229,7 +230,7 @@
                 )
             return sums
 
-        sums = lax.fori_loop(0, blocks // source_step, add_sources, tuple((zero,) * 9 for _ in groups))
+        sums = lax.fori_loop(0, blocks // source_step, add_sources, (zeros,) * group_step)
         for n, group in enumerate(groups):
             packed = lax.rem(group, slot_ref.shape[0])
             part = lax.div(group, slot_ref.shape[0])
@@ -237,15 +238,25 @@
             slot = slot_ref[pl.ds(packed, 1), :]
             here = (slot == row) & (lane >= part * cap) & (lane < (part + 1) * cap)
             mass = jnp.where(here, near[6:7], 0.0)
-            irregular = pair_sums(held[n], [near[c : c + 1] for c in range(6)], mass, softening, (zero,) * 9)
-            result = zero
-            for c, values in enumerate(finish(sums[n]) + finish(irregular)):
-                result = jnp.where(lane == c * targets + row, jnp.sum(values, axis=1, keepdims=True), result)
+            irregular = pair_sums(held[n], [near[c : c + 1] for c in range(6)], mass, softening, zeros)
+            for c, values in enumerate(sums[n] + irregular):
+                sums_ref[group, c] = values
+        return 0
+
+    lax.fori_loop(0, devices // group_step, add_groups, 0)
+
+    def add_lanes(step, _):
+        for i in range(sum_step):
+            group = step * sum_step + i
+            result = zeros[0]
+            for c in range(12):
+                value = jnp.sum(sums_ref[group, c], axis=1, keepdims=True)
+                result = jnp.where(lane == c * targets + row, value, result)
             out_ref[pl.ds(2 * group, 1), :] = jnp.sum(result, axis=0, keepdims=True)
             out_ref[pl.ds(2 * group + 1, 1), :] = back_ref[pl.ds(group, 1), :]
         return 0
 
-    lax.fori_loop(0, devices // group_step, add_groups, 0)
+    lax.fori_loop(0, devices // sum_step, add_lanes, 0)
 
 
 def correct_kernel(targets, sums_ref, state_ref, forces_ref, terms_ref):
@@ -253,23 +264,20 @@
     for i in range(1, sums_ref.shape[0] // 8):
         total = total + sums_ref[i * 8 : (i + 1) * 8]
     pair = total[0:2] + total[2:4] + total[4:6] + total[6:8]
-
-    def rows(which, first, count):
-        return jnp.concatenate(
-            [pair[which : which + 1, c * targets : (c + 1) * targets] for c in range(first, first + count)], axis=0
-        )
-
-    accel, jerk, irregular = rows(0, 0, 3), rows(0, 3, 3), rows(0, 6, 6)
-    position, velocity, step = rows(1, 0, 3), rows(1, 3, 3), rows(1, 7, 1)
-    old_accel, old_jerk = rows(1, 8, 3), rows(1, 11, 3)
+    lane, row = iota((16, LANES), 1), iota((16, LANES), 0)
+    on_row = (lane >= row * targets) & (lane < (row + 1) * targets)
+    spread = jnp.concatenate([jnp.where(on_row, pair[i : i + 1], 0.0) for i in range(2)], axis=0)
+    rows = jnp.dot(split3(spread), folding(targets), preferred_element_type=F32)[:, 0:targets]
+    accel, jerk, irregular = rows[0:3], rows[3:6], rows[6:12]
+    position, velocity, step = rows[16:19], rows[19:22], rows[23:24]
+    old_accel, old_jerk = rows[24:27], rows[27:30]
     change = accel - old_accel
     second = 3.0 * change - step * (2.0 * old_jerk + jerk)
     third = -2.0 * change + step * (old_jerk + jerk)
     state_ref[0:3] = position + step * step * (second / 12.0 + third / 20.0)
     state_ref[3:6] = velocity + step * (second / 3.0 + third / 4.0)
-    forces_ref[0:6] = irregular
-    forces_ref[6:9] = accel - irregular[0:3]
-    forces_ref[9:12] = jerk - irregular[3:6]
+    forces = jnp.concatenate([irregular, rows[0:6] - irregular, jnp.zeros((4, targets), F32)], axis=0)
+    forces_ref[...] = forces.T[:, 0:12]
     terms_ref[0:3] = second
     terms_ref[3:6] = third
 
@@ -298,16 +306,22 @@
     request = pl.pallas_call(
         functools.partial(request_kernel, stars_dev, cap),
         out_shape=shape(devices, LANES, dtype=I32),
-        in_specs=[SMEM, SMEM, VMEM],
+        in_specs=[HBM] * 3,
         out_specs=VMEM,
+        scratch_shapes=[
+            pltpu.SMEM((targets,), I32),
+            pltpu.SMEM((targets,), I32),
+            pltpu.VMEM((targets, slots), I32),
+            pltpu.SemaphoreType.DMA((3,)),
+        ],
         compiler_params=PARAMS,
     )(active_ids, list_length, neighbours)
     request = exchange(request, devices)
-    predicted, own_table, star_table = pl.pallas_call(
+    source, star_table, force_table = pl.pallas_call(
         predict_kernel,
         out_shape=(
-            shape(8, stars_dev),
-            shape(blocks * 16, 3 * LANES, dtype=BF16),
+            shape(blocks, 7, 8, LANES),
+            shape(blocks * 8, 3 * LANES, dtype=BF16),
             shape(blocks * 8, 3 * LANES, dtype=BF16),
         ),
         in_specs=[VMEM] * 4,
@@ -315,38 +329,39 @@
         compiler_params=PARAMS,
         cost_estimate=cost(1 << 20),
     )(star_state, old_force, star_mass.reshape(blocks, LANES), elapsed.reshape(blocks, LANES))
-    own, sent = pl.pallas_call(
+    own, local, sent = pl.pallas_call(
         functools.partial(own_kernel, stars_dev, cap, targets),
-        out_shape=(shape(16, active), shape(devices * 6 * active // LANES, LANES)),
+        out_shape=(shape(8, active), shape(8, active, dtype=I32), shape(devices * 6 * active // LANES, LANES)),
         in_specs=[VMEM] * 2,
-        out_specs=(VMEM,) * 2,
-        compiler_params=PARAMS,
-    )(request, own_table)
+        out_specs=(VMEM,) * 3,
+        compiler_params=PARAMS,
+    )(request, star_table)
     sent = exchange(sent, devices)
     listed, slot, back = pl.pallas_call(
         functools.partial(listed_kernel, cap, targets),
         out_shape=(shape(packed * 8, LANES), shape(packed, LANES, dtype=I32), shape(devices, LANES)),
-        in_specs=[VMEM] * 3,
+        in_specs=[VMEM] * 5,
         out_specs=(VMEM,) * 3,
         compiler_params=PARAMS,
         cost_estimate=cost(1 << 24),
-    )(request, star_table, own)
+    )(request, star_table, force_table, own, local)
     sums = pl.pallas_call(
-        functools.partial(force_kernel, softening, cap, targets, 2, 4),
+        functools.partial(force_kernel, softening, cap, targets, 4, 32, 16),
         out_shape=shape(devices * 2, LANES),
         in_specs=[VMEM] * 5,
         out_specs=VMEM,
-        scratch_shapes=[pltpu.VMEM((active, LANES), F32), pltpu.VMEM((blocks, 7, 8, LANES), F32)],
-        compiler_params=PARAMS,
-    )(sent, predicted, listed, slot, back)
+        scratch_shapes=[pltpu.VMEM((active, LANES), F32), pltpu.VMEM((devices, 12, 8, LANES), F32)],
+        compiler_params=PARAMS,
+    )(sent, source, listed, slot, back)
     sums = exchange(sums, devices)
-    return pl.pallas_call(
+    state, forces, terms = pl.pallas_call(
         functools.partial(correct_kernel, targets),
-        out_shape=(shape(6, targets), shape(12, targets), shape(6, targets)),
+        out_shape=(shape(6, targets), shape(targets, 12), shape(6, targets)),
         in_specs=[VMEM],
         out_specs=(VMEM,) * 3,
         compiler_params=PARAMS,
     )(sums)
+    return state, forces.T, terms
 
 
 def solution(mesh):

time: 53.1 us -> 49.5 us (0.932)
  Pallas kernels: 15.1 us -> 12.4 us
  local copies, waits for them, and re-layouts: 4.47 us -> 3.81 us
    pallas_call x2, Pallas kernels: 10.1 us -> 7.41 us  [the longest x1 7.19 us: per_device(): pl.pallas_call(functools.partial(force_kernel, softening, cap, targets, 4...]
    pallas_call x1 -> x0, local copies, waits for them, and re-layouts: 0.67 us -> none  [per_device(): pl.pallas_call(functools.partial(correct_kernel, targets), out_shape=(sha...]
  transfers between devices with their start and end apart: 2 -> 2, of which waited for: 2 -> 2; matrix products, arithmetic and copies ran while one was open for 0% -> 0% of each run, Pallas kernels for 2% -> 3%
where the time goes in v2:
time: 49.5 us; the launch traced here: 49.1 us
  waiting for transfers between devices  12.7 us (26%)
  Pallas kernels  12.4 us (25%)
  starting transfers between devices  9.88 us (20%)
  blocking collectives  9.67 us (20%)
  local copies, waits for them, and re-layouts  3.81 us (8%)
  between operations  0.72 us (1%)
    all_to_all x2, waiting for transfers between devices, exchange(): return lax.all_to_all(wide, 'stars', 0, 0, tiled=True).reshape(rows.shape)  12.7 us
    all_to_all x2, starting transfers between devices, exchange(): return lax.all_to_all(wide, 'stars', 0, 0, tiled=True).reshape(rows.shape)  9.88 us
    all_to_all x1, blocking collectives, exchange(): return lax.all_to_all(wide, 'stars', 0, 0, tiled=True).reshape(rows.shape)  9.67 us
    pallas_call x1, Pallas kernels, per_device(): pl.pallas_call(functools.partial(force_kernel, softening, cap, targets, 4...  7.19 us
    unnamed x14, local copies, waits for them, and re-layouts  3.81 us
    pallas_call x1, Pallas kernels, per_device(): pl.pallas_call(functools.partial(request_kernel, stars_dev, cap), out_sha...  1.59 us
    pallas_call x1, Pallas kernels, per_device(): pl.pallas_call(functools.partial(listed_kernel, cap, targets), out_shape=...  1.31 us
    pallas_call x1, Pallas kernels, per_device(): pl.pallas_call(functools.partial(own_kernel, stars_dev, cap, targets), ou...  1.28 us
  transfers between devices with their start and end apart: 2, of which 2 were waited for; matrix products, arithmetic and copies ran while one was open for 0% of the time, Pallas kernels for 3%

profile of v2, /device:TPU:0, one launch (start us, length us, event | category | flops | bytes accessed | tf_op | source)
XLA Modules:
  0.0 49.1 jit_solution(7787727514621113352)
XLA Ops:
  0.6 0.0 copy-start.4
  0.6 0.7 %copy-done.4 = s32[8,128]{1,0:T(8,128)S(1)} copy-done((s32[8,128]{1,0:T(8,128)S(1)}, s32[8,128]{1,0:T(8,128)}, u32[]{:S(2)}) %copy-start.4) | copy-done | bytes 4120
  1.3 0.0 copy-start.5
  1.3 0.7 %copy-done.5 = s32[8]{0:T(128)S(1)} copy-done((s32[8]{0:T(128)S(1)}, s32[8]{0:T(128)}, u32[]{:S(2)}) %copy-start.5) | copy-done | bytes 56
  2.0 0.0 copy-start.6
  2.0 0.7 %copy-done.6 = s32[8]{0:T(128)S(1)} copy-done((s32[8]{0:T(128)S(1)}, s32[8]{0:T(128)}, u32[]{:S(2)}) %copy-start.6) | copy-done | bytes 56
  2.6 1.6 %shard_map.94 = s32[32,128]{1,0:T(8,128)} custom-call(s32[8]{0:T(128)S(1)} %copy-done.5, s32[8]{0:T(128)S(1)} %copy-done.6, s32[8,128]{1,0:T(8,128)S(1)} %copy-done.4), custom_call_target="tpu_custom_call" | custom-call | tf_op jit(solution)/shard_map/pallas_call | solution.py:306
  4.2 0.0 copy-start.2
  4.2 0.0 copy-start.3
  4.3 7.3 %all-to-all-start = ((s32[32,1,128]{2,1,0:T(1,128)}), s32[32,1,128]{2,1,0:T(1,128)S(1)}, u32[]{:S(2)}, u32[]{:S(2)}) async-start(s32[32,1,128]{2,1,0:T(1,128)} %bitcast.1), calls=%async_computation | async-start | bytes 32768 | tf_op jit(solution)/shard_map/all_to_all | solution.py:287
  11.6 0.0 copy-done.2
  11.6 0.0 copy-done.3
  11.6 0.0 copy-start
  11.6 0.9 %copy-done = f32[6,4096]{1,0:T(8,128)S(1)} copy-done((f32[6,4096]{1,0:T(8,128)S(1)}, f32[6,4096]{1,0:T(8,128)}, u32[]{:S(2)}) %copy-start) | copy-done | bytes 98328
  12.5 0.0 copy-start.1
  12.5 0.9 %copy-done.1 = f32[6,4096]{1,0:T(8,128)S(1)} copy-done((f32[6,4096]{1,0:T(8,128)S(1)}, f32[6,4096]{1,0:T(8,128)}, u32[]{:S(2)}) %copy-start.1) | copy-done | bytes 98328
  13.4 0.2 shard_map.95
  13.6 5.1 %all-to-all-done = s32[32,1,128]{2,1,0:T(1,128)S(1)} async-done(((s32[32,1,128]{2,1,0:T(1,128)}), s32[32,1,128]{2,1,0:T(1,128)S(1)}, u32[]{:S(2)}, u32[]{:S(2)}) %all-to-all-start) | async-done | bytes 16416 | tf_op jit(solution)/shard_map/all_to_all | solution.py:287
  18.7 1.3 %shard_map.96 = (f32[8,256]{1,0:T(8,128)S(1)}, s32[8,256]{1,0:T(8,128)S(1)}, f32[384,128]{1,0:T(8,128)}) custom-call(s32[32,128]{1,0:T(8,128)S(1)} %bitcast.12, bf16[256,384]{1,0:T(8,128)(2,1)S(1)} %get-tuple-element.15.table_ref.star_table_ref), custom_call_target="tpu_custom_call" | custom-call | tf_op jit(solution)/shard_map/pallas_call | solution.py:332
  20.0 2.6 %all-to-all-start.1 = ((f32[32,1,1536]{2,1,0:T(1,128)}), f32[32,1,1536]{2,1,0:T(1,128)S(1)}, u32[]{:S(2)}, u32[]{:S(2)}) async-start(f32[32,1,1536]{2,1,0:T(1,128)} %bitcast.5), calls=%async_computation.1 | async-start | bytes 393216 | tf_op jit(solution)/shard_map/all_to_all | solution.py:287
  22.6 1.3 %shard_map.97 = (f32[128,128]{1,0:T(8,128)S(1)}, s32[16,128]{1,0:T(8,128)S(1)}, f32[32,128]{1,0:T(8,128)S(1)}) custom-call(s32[32,128]{1,0:T(8,128)S(1)} %bitcast.13, bf16[256,384]{1,0:T(8,128)(2,1)S(1)} %get-tuple-element.15.table_ref.star_table_ref, bf16[256,384]{1,0:T(8,128)(2,1)S(1)} %get-tuple-element.18.force_table_ref, ...), custom_call_target="tpu_custom_call" | custom-call | flops 16777216 | bytes 1048576 | tf_op jit(solution)/shard_map/pallas_call | solution.py:340
  23.9 7.6 %all-to-all-done.1 = f32[32,1,1536]{2,1,0:T(1,128)S(1)} async-done(((f32[32,1,1536]{2,1,0:T(1,128)}), f32[32,1,1536]{2,1,0:T(1,128)S(1)}, u32[]{:S(2)}, u32[]{:S(2)}) %all-to-all-start.1) | async-done | bytes 196640 | tf_op jit(solution)/shard_map/all_to_all | solution.py:287
  31.5 7.2 %shard_map.98 = f32[64,128]{1,0:T(8,128)S(1)} custom-call(f32[384,128]{1,0:T(8,128)S(1)} %bitcast.11, f32[32,7,8,128]{3,2,1,0:T(8,128)S(1)} %get-tuple-element.17.source_ref, f32[128,128]{1,0:T(8,128)S(1)} %get-tuple-element.21.listed_ref, s32[16,128]{1,0:T(8,128)S(1)} %get-tuple-element.22.slot_ref, f32[32,128]{1,0:T(8,128)S(1)} %get-tuple-element.23.back_ref), custom_call_target="tpu_custom_call" | custom-call | tf_op jit(solution)/shard_map/pallas_call | solution.py:348
  38.7 9.7 %all_to_all.15 = f32[32,1,256]{2,1,0:T(1,128)S(1)} all-to-all(f32[32,1,256]{2,1,0:T(1,128)S(1)} %bitcast.14), channel_id=1, replica_groups=mesh['stars'=32] {'stars'}, dimensions={0} | all-to-all | bytes 65536 | tf_op jit(solution)/shard_map/all_to_all | solution.py:287
  48.3 0.8 %shard_map.99 = (f32[6,8]{1,0:T(8,128)}, f32[8,12]{1,0:T(8,128)}, f32[6,8]{1,0:T(8,128)}) custom-call(f32[64,128]{1,0:T(8,128)S(1)} %bitcast.15), custom_call_target="tpu_custom_call" | custom-call | tf_op jit(solution)/shard_map/pallas_call | solution.py:357
Async XLA Ops:
  0.6 0.7 %copy-start.4 = (s32[8,128]{1,0:T(8,128)S(1)}, s32[8,128]{1,0:T(8,128)}, u32[]{:S(2)}) copy-start(s32[8,128]{1,0:T(8,128)} %listed_hbm.1) | copy-start | bytes 12292
  1.3 0.7 %copy-start.5 = (s32[8]{0:T(128)S(1)}, s32[8]{0:T(128)}, u32[]{:S(2)}) copy-start(s32[8]{0:T(128)} %active_hbm.1) | copy-start | bytes 100
  2.0 0.7 %copy-start.6 = (s32[8]{0:T(128)S(1)}, s32[8]{0:T(128)}, u32[]{:S(2)}) copy-start(s32[8]{0:T(128)} %length_hbm.1) | copy-start | bytes 100
  4.2 7.3 %copy-start.2 = (f32[4096]{0:T(1024)S(1)}, f32[4096]{0:T(1024)}, u32[]{:S(2)}) copy-start(f32[4096]{0:T(1024)} %param.9) | copy-start | bytes 49156
  4.2 7.3 %copy-start.3 = (f32[4096]{0:T(1024)S(1)}, f32[4096]{0:T(1024)}, u32[]{:S(2)}) copy-start(f32[4096]{0:T(1024)} %param.10) | copy-start | bytes 49156
  4.3 14.5 %all-to-all-start = ((s32[32,1,128]{2,1,0:T(1,128)}), s32[32,1,128]{2,1,0:T(1,128)S(1)}, u32[]{:S(2)}, u32[]{:S(2)}) async-start(s32[32,1,128]{2,1,0:T(1,128)} %bitcast.1), calls=%async_computation | async-start | bytes 32768 | tf_op jit(solution)/shard_map/all_to_all | solution.py:287
  11.6 0.9 %copy-start = (f32[6,4096]{1,0:T(8,128)S(1)}, f32[6,4096]{1,0:T(8,128)}, u32[]{:S(2)}) copy-start(f32[6,4096]{1,0:T(8,128)} %state_ref.1) | copy-start | bytes 294916
  12.5 0.9 %copy-start.1 = (f32[6,4096]{1,0:T(8,128)S(1)}, f32[6,4096]{1,0:T(8,128)}, u32[]{:S(2)}) copy-start(f32[6,4096]{1,0:T(8,128)} %force_ref.1) | copy-start | bytes 294916
  20.0 11.5 %all-to-all-start.1 = ((f32[32,1,1536]{2,1,0:T(1,128)}), f32[32,1,1536]{2,1,0:T(1,128)S(1)}, u32[]{:S(2)}, u32[]{:S(2)}) async-start(f32[32,1,1536]{2,1,0:T(1,128)} %bitcast.5), calls=%async_computation.1 | async-start | bytes 393216 | tf_op jit(solution)/shard_map/all_to_all | solution.py:287

commit v3 on v2

--- a/solution.py
+++ b/solution.py
@@ -314,7 +314,7 @@
             pltpu.VMEM((targets, slots), I32),
             pltpu.SemaphoreType.DMA((3,)),
         ],
-        compiler_params=PARAMS,
+
     )(active_ids, list_length, neighbours)
     request = exchange(request, devices)
     source, star_table, force_table = pl.pallas_call(

time: 49.5 us -> 47.7 us (0.964)
  local copies, waits for them, and re-layouts: 3.81 us -> 1.82 us
    unnamed x14 -> x8, local copies, waits for them, and re-layouts: 3.81 us -> 1.82 us
where the time goes in v3:
time: 47.7 us; the launch traced here: 47.4 us
  Pallas kernels  12.7 us (27%)
  waiting for transfers between devices  12.7 us (27%)
  starting transfers between devices  9.88 us (21%)
  blocking collectives  9.67 us (20%)
  local copies, waits for them, and re-layouts  1.82 us (4%)
  between operations  0.71 us (1%)
    all_to_all x2, waiting for transfers between devices, exchange(): return lax.all_to_all(wide, 'stars', 0, 0, tiled=True).reshape(rows.shape)  12.7 us
    all_to_all x2, starting transfers between devices, exchange(): return lax.all_to_all(wide, 'stars', 0, 0, tiled=True).reshape(rows.shape)  9.88 us
    all_to_all x1, blocking collectives, exchange(): return lax.all_to_all(wide, 'stars', 0, 0, tiled=True).reshape(rows.shape)  9.67 us
    pallas_call x1, Pallas kernels, per_device(): pl.pallas_call(functools.partial(force_kernel, softening, cap, targets, 4...  7.19 us
    pallas_call x1, Pallas kernels, per_device(): pl.pallas_call(functools.partial(request_kernel, stars_dev, cap), out_sha...  1.85 us
    unnamed x8, local copies, waits for them, and re-layouts  1.82 us
    pallas_call x1, Pallas kernels, per_device(): pl.pallas_call(functools.partial(listed_kernel, cap, targets), out_shape=...  1.31 us
    pallas_call x1, Pallas kernels, per_device(): pl.pallas_call(functools.partial(own_kernel, stars_dev, cap, targets), ou...  1.27 us
  transfers between devices with their start and end apart: 2, of which 2 were waited for; matrix products, arithmetic and copies ran while one was open for 0% of the time, Pallas kernels for 3%

profile of v3, /device:TPU:0, one launch (start us, length us, event | category | flops | bytes accessed | tf_op | source)
XLA Modules:
  0.0 47.4 jit_solution(11896040380293161494)
XLA Ops:
  0.6 1.9 %shard_map.94 = s32[32,128]{1,0:T(8,128)} custom-call(s32[8]{0:T(128)} %active_hbm.1, s32[8]{0:T(128)} %length_hbm.1, s32[8,128]{1,0:T(8,128)} %listed_hbm.1), custom_call_target="tpu_custom_call" | custom-call | tf_op jit(solution)/shard_map/pallas_call | solution.py:306
  2.5 0.0 copy-start.2
  2.5 0.0 copy-start.3
  2.5 7.3 %all-to-all-start = ((s32[32,1,128]{2,1,0:T(1,128)}), s32[32,1,128]{2,1,0:T(1,128)S(1)}, u32[]{:S(2)}, u32[]{:S(2)}) async-start(s32[32,1,128]{2,1,0:T(1,128)} %bitcast.18), calls=%async_computation | async-start | bytes 32768 | tf_op jit(solution)/shard_map/all_to_all | solution.py:287
  9.8 0.0 copy-done.2
  9.8 0.0 copy-done.3
  9.8 0.0 copy-start
  9.9 0.9 %copy-done = f32[6,4096]{1,0:T(8,128)S(1)} copy-done((f32[6,4096]{1,0:T(8,128)S(1)}, f32[6,4096]{1,0:T(8,128)}, u32[]{:S(2)}) %copy-start) | copy-done | bytes 98328
  10.8 0.0 copy-start.1
  10.8 0.9 %copy-done.1 = f32[6,4096]{1,0:T(8,128)S(1)} copy-done((f32[6,4096]{1,0:T(8,128)S(1)}, f32[6,4096]{1,0:T(8,128)}, u32[]{:S(2)}) %copy-start.1) | copy-done | bytes 98328
  11.7 0.2 shard_map.95
  11.9 5.1 %all-to-all-done = s32[32,1,128]{2,1,0:T(1,128)S(1)} async-done(((s32[32,1,128]{2,1,0:T(1,128)}), s32[32,1,128]{2,1,0:T(1,128)S(1)}, u32[]{:S(2)}, u32[]{:S(2)}) %all-to-all-start) | async-done | bytes 16416 | tf_op jit(solution)/shard_map/all_to_all | solution.py:287
  17.0 1.3 %shard_map.96 = (f32[8,256]{1,0:T(8,128)S(1)}, s32[8,256]{1,0:T(8,128)S(1)}, f32[384,128]{1,0:T(8,128)}) custom-call(s32[32,128]{1,0:T(8,128)S(1)} %bitcast.12, bf16[256,384]{1,0:T(8,128)(2,1)S(1)} %get-tuple-element.15.table_ref.star_table_ref), custom_call_target="tpu_custom_call" | custom-call | tf_op jit(solution)/shard_map/pallas_call | solution.py:332
  18.2 2.6 %all-to-all-start.1 = ((f32[32,1,1536]{2,1,0:T(1,128)}), f32[32,1,1536]{2,1,0:T(1,128)S(1)}, u32[]{:S(2)}, u32[]{:S(2)}) async-start(f32[32,1,1536]{2,1,0:T(1,128)} %bitcast.5), calls=%async_computation.1 | async-start | bytes 393216 | tf_op jit(solution)/shard_map/all_to_all | solution.py:287
  20.8 1.3 %shard_map.97 = (f32[128,128]{1,0:T(8,128)S(1)}, s32[16,128]{1,0:T(8,128)S(1)}, f32[32,128]{1,0:T(8,128)S(1)}) custom-call(s32[32,128]{1,0:T(8,128)S(1)} %bitcast.13, bf16[256,384]{1,0:T(8,128)(2,1)S(1)} %get-tuple-element.15.table_ref.star_table_ref, bf16[256,384]{1,0:T(8,128)(2,1)S(1)} %get-tuple-element.18.force_table_ref, ...), custom_call_target="tpu_custom_call" | custom-call | flops 16777216 | bytes 1048576 | tf_op jit(solution)/shard_map/pallas_call | solution.py:340
  22.2 7.6 %all-to-all-done.1 = f32[32,1,1536]{2,1,0:T(1,128)S(1)} async-done(((f32[32,1,1536]{2,1,0:T(1,128)}), f32[32,1,1536]{2,1,0:T(1,128)S(1)}, u32[]{:S(2)}, u32[]{:S(2)}) %all-to-all-start.1) | async-done | bytes 196640 | tf_op jit(solution)/shard_map/all_to_all | solution.py:287
  29.7 7.2 %shard_map.98 = f32[64,128]{1,0:T(8,128)S(1)} custom-call(f32[384,128]{1,0:T(8,128)S(1)} %bitcast.11, f32[32,7,8,128]{3,2,1,0:T(8,128)S(1)} %get-tuple-element.17.source_ref, f32[128,128]{1,0:T(8,128)S(1)} %get-tuple-element.21.listed_ref, s32[16,128]{1,0:T(8,128)S(1)} %get-tuple-element.22.slot_ref, f32[32,128]{1,0:T(8,128)S(1)} %get-tuple-element.23.back_ref), custom_call_target="tpu_custom_call" | custom-call | tf_op jit(solution)/shard_map/pallas_call | solution.py:348
  36.9 9.7 %all_to_all.15 = f32[32,1,256]{2,1,0:T(1,128)S(1)} all-to-all(f32[32,1,256]{2,1,0:T(1,128)S(1)} %bitcast.14), channel_id=1, replica_groups=mesh['stars'=32] {'stars'}, dimensions={0} | all-to-all | bytes 65536 | tf_op jit(solution)/shard_map/all_to_all | solution.py:287
  46.6 0.8 %shard_map.99 = (f32[6,8]{1,0:T(8,128)}, f32[8,12]{1,0:T(8,128)}, f32[6,8]{1,0:T(8,128)}) custom-call(f32[64,128]{1,0:T(8,128)S(1)} %bitcast.15), custom_call_target="tpu_custom_call" | custom-call | tf_op jit(solution)/shard_map/pallas_call | solution.py:357
Async XLA Ops:
  2.5 7.3 %copy-start.2 = (f32[4096]{0:T(1024)S(1)}, f32[4096]{0:T(1024)}, u32[]{:S(2)}) copy-start(f32[4096]{0:T(1024)} %param.9) | copy-start | bytes 49156
  2.5 7.3 %copy-start.3 = (f32[4096]{0:T(1024)S(1)}, f32[4096]{0:T(1024)}, u32[]{:S(2)}) copy-start(f32[4096]{0:T(1024)} %param.10) | copy-start | bytes 49156
  2.5 14.5 %all-to-all-start = ((s32[32,1,128]{2,1,0:T(1,128)}), s32[32,1,128]{2,1,0:T(1,128)S(1)}, u32[]{:S(2)}, u32[]{:S(2)}) async-start(s32[32,1,128]{2,1,0:T(1,128)} %bitcast.18), calls=%async_computation | async-start | bytes 32768 | tf_op jit(solution)/shard_map/all_to_all | solution.py:287
  9.8 0.9 %copy-start = (f32[6,4096]{1,0:T(8,128)S(1)}, f32[6,4096]{1,0:T(8,128)}, u32[]{:S(2)}) copy-start(f32[6,4096]{1,0:T(8,128)} %state_ref.1) | copy-start | bytes 294916
  10.8 0.9 %copy-start.1 = (f32[6,4096]{1,0:T(8,128)S(1)}, f32[6,4096]{1,0:T(8,128)}, u32[]{:S(2)}) copy-start(f32[6,4096]{1,0:T(8,128)} %force_ref.1) | copy-start | bytes 294916
  18.2 11.5 %all-to-all-start.1 = ((f32[32,1,1536]{2,1,0:T(1,128)}), f32[32,1,1536]{2,1,0:T(1,128)S(1)}, u32[]{:S(2)}, u32[]{:S(2)}) async-start(f32[32,1,1536]{2,1,0:T(1,128)} %bitcast.5), calls=%async_computation.1 | async-start | bytes 393216 | tf_op jit(solution)/shard_map/all_to_all | solution.py:287

commit v4 on v3

v4 whole, which is shorter than its diff:
```python
import functools
import math

import jax
import jax.numpy as jnp
from jax import lax
from jax.experimental import pallas as pl
from jax.experimental.pallas import tpu as pltpu
from jax.sharding import PartitionSpec as P

LANES = 128
PARTS = 4
F32 = jnp.float32
I32 = jnp.int32
BF16 = jnp.bfloat16
VMEM = pl.BlockSpec(memory_space=pltpu.VMEM)
HBM = pl.BlockSpec(memory_space=pltpu.HBM)
PARAMS = pltpu.CompilerParams(vmem_limit_bytes=32 * 1024 * 1024)


def iota(shape, axis):
    return lax.broadcasted_iota(I32, shape, axis)


def part_of(device):
    return (device >> 1) & (PARTS - 1)


def line_of(device):
    return (device >> 3) * 2 + (device & 1)


def device_at(line, part):
    return (line >> 1) * 2 * PARTS + part * 2 + (line & 1)


def turn(value, lanes):
    lanes %= LANES
    return pltpu.roll(value, lanes, 1) if lanes else value


def split3(value):
    high = value.astype(BF16)
    rest = value - high.astype(F32)
    middle = rest.astype(BF16)
    low = (rest - middle.astype(F32)).astype(BF16)
    return jnp.concatenate([high, middle, low], axis=1)


def folding(targets):
    same = iota((LANES, LANES), 0) % targets == iota((LANES, LANES), 1) % targets
    return jnp.concatenate([jnp.where(same, 1.0, 0.0).astype(BF16)] * 3, axis=0)


def pick(table, column):
    count = column.shape[1]
    low = jnp.where(column < 0, -1, column & (LANES - 1))
    high = lax.shift_right_logical(column, 7)
    hot = jnp.where(iota((LANES, count), 0) == low, 1.0, 0.0).astype(BF16)
    found = jnp.dot(table, jnp.concatenate([hot] * 3, axis=0), preferred_element_type=F32)
    total = jnp.zeros((8, count), F32)
    for block in range(table.shape[0] // 8):
        total += jnp.where(high == block, found[block * 8 : (block + 1) * 8], 0.0)
    return total


def request_kernel(
    stars_dev, cap, active_hbm, length_hbm, listed_hbm, out_ref, active_ref, length_ref, listed_ref, sems
):
    pairs = ((listed_hbm, listed_ref), (length_hbm, length_ref), (active_hbm, active_ref))
    copies = [pltpu.make_async_copy(*pair, sems.at[i]) for i, pair in enumerate(pairs)]
    for copy in copies:
        copy.start()
    for copy in copies:
        copy.wait()
    targets, slots = listed_ref.shape
    devices = lax.axis_size("stars")
    listed = listed_ref[...]
    owner = listed // stars_dev if stars_dev & (stars_dev - 1) else lax.shift_right_logical(listed, stars_dev.bit_length() - 1)
    local = listed - owner * stars_dev
    low = (local & (LANES - 1)).astype(F32)
    high = lax.shift_right_logical(local, 7).astype(F32)
    lane = iota((devices, LANES), 1)
    row = iota((devices, LANES), 0)
    before = jnp.where(iota((slots, 2 * LANES), 0) < iota((slots, 2 * LANES), 1), 1.0, 0.0).astype(BF16)
    mine = [
        jnp.where((owner[k : k + 1] == row) & (lane < length_ref[k]), 1.0, 0.0) for k in range(targets)
    ]
    counts = jnp.dot(jnp.concatenate(mine, axis=0).astype(BF16), before, preferred_element_type=F32)
    base = jnp.zeros((devices, LANES), F32)
    order = iota((LANES, slots), 0).astype(F32)
    lows, highs, hots = [], [], []
    place = lane - part_of(row)
    begins = jnp.zeros((devices, LANES), F32)
    for k in range(targets):
        ahead = counts[k * devices : (k + 1) * devices]
        rank = jnp.sum(mine[k] * (ahead[:, :LANES] + base), axis=0, keepdims=True)
        hots.append(jnp.where(order == rank, 1.0, 0.0).astype(BF16))
        lows.append((mine[k] * low[k : k + 1]).astype(BF16))
        highs.append((mine[k] * high[k : k + 1]).astype(BF16))
        base = base + ahead[:, LANES:]
        begins = jnp.where(place == (k + 1) * PARTS, base, begins)
    planes = jnp.concatenate([jnp.concatenate(lows, axis=1), jnp.concatenate(highs, axis=1)], axis=0)
    placed = lax.dot_general(
        planes, jnp.concatenate(hots, axis=1), (((1,), (1,)), ((), ())), preferred_element_type=F32
    )
    packed = (placed[:devices] + LANES * placed[devices:]).astype(I32)
    per_row = min(LANES // cap, PARTS)
    alone = packed
    for i in range(1, per_row):
        packed = jnp.where(lane >= i * cap, turn(pltpu.roll(alone, devices - 2 * i, 0), i * cap), packed)
    lane1 = iota((1, LANES), 1)
    actives = jnp.zeros((1, LANES), I32)
    for k in range(targets):
        actives = jnp.where(lane1 == (targets + 1) * PARTS + k, active_ref[k], actives)
    size = 2 * PARTS
    height = size * (PARTS // per_row + 1)
    for first in range(0, devices, size):
        blocks = []
        for core in range(2):
            begin = jnp.where((row[:size] & 1) == core, begins[first : first + size], 0.0)
            begin = jnp.sum(begin, axis=0, keepdims=True).astype(I32)
            rows = [packed[first + at + core : first + at + core + 1] for at in range(0, size, 2 * per_row)]
            blocks += [*rows, begin + actives]
        at = first // size * height
        out_ref[at : at + height] = jnp.concatenate(blocks * PARTS, axis=0)


def predict_kernel(given_ref, star_ref, star_table_ref, force_table_ref):
    tables = []
    for block in range(given_ref.shape[1] // LANES):
        cols = slice(block * LANES, (block + 1) * LANES)
        state, force, mass, step = (given_ref[first:last, cols] for first, last in ((0, 6), (6, 12), (12, 13), (13, 14)))
        accel, jerk = force[0:3], force[3:6]
        position = state[0:3] + step * (state[3:6] + step * (0.5 * accel + step * jerk / 6.0))
        velocity = state[3:6] + step * (accel + 0.5 * step * jerk)
        stars = jnp.concatenate([position, velocity, mass, step], axis=0)
        star_ref[:, cols] = stars
        tables.append((stars, jnp.concatenate([force, jnp.zeros((2, LANES), F32)], axis=0)))
        if block % 2:
            rows = slice((block - 1) * 8, (block + 1) * 8)
            for table_ref, pair in zip((star_table_ref, force_table_ref), zip(*tables)):
                table_ref[rows] = split3(jnp.concatenate(pair, axis=0))
            tables = []


def own_kernel(stars_dev, targets, request_ref, star_table_ref, force_table_ref, out_ref):
    devices = out_ref.shape[0] // sent_rows(out_ref)
    lines = devices // PARTS
    width = request_ref.shape[0] // devices
    first = (targets + 1) * PARTS
    lane, row = iota((devices, LANES), 1), iota((devices, LANES), 0)
    ids = request_ref[pl.ds(width - 1, devices, stride=width), :]
    ids = jnp.where(lane < targets, turn(ids.astype(F32), -first), 0.0)
    span = targets
    while span < LANES:
        ids = ids + turn(ids, span)
        span *= 2
    per_tile = LANES // targets
    tiles = devices // per_tile
    start = (part_of(row) * lines + line_of(row)) * targets
    flat = []
    for t in range(tiles):
        offset = lane + t * LANES - start
        here = (offset >= 0) & (offset < targets)
        flat.append(jnp.sum(jnp.where(here, ids, 0.0), axis=0, keepdims=True))
    local = jnp.concatenate(flat, axis=1).astype(I32) - lax.axis_index("stars") * stars_dev
    local = jnp.where((local >= 0) & (local < stars_dev), local, -1)
    own = pick(star_table_ref[...], local)
    old = pick(force_table_ref[...], local)
    words = jnp.concatenate([own[7:8], old[0:7]], axis=0)
    span = lines * targets
    last = 6 * span
    fold = folding(targets)
    lane, row = iota((per_tile, LANES), 1), iota((per_tile, LANES), 0)
    on_row = (lane >= row * targets) & (lane < (row + 1) * targets)
    lane1 = iota((1, LANES), 1)
    rows = sent_rows(out_ref)
    backs = []
    for t in range(tiles):
        tile = words[:, t * LANES : (t + 1) * LANES]
        spread = jnp.concatenate([jnp.where(on_row, tile[c : c + 1], 0.0) for c in range(7)], axis=0)
        folded = jnp.dot(split3(spread), fold, preferred_element_type=F32)
        back = jnp.zeros((per_tile, LANES), F32)
        for c in range(7):
            begin = last % LANES + c * targets
            here = (lane >= begin) & (lane < begin + targets)
            back = jnp.where(here, folded[c * per_tile : (c + 1) * per_tile], back)
        backs.append(back)
    piece = min(span, LANES)
    turned = {}
    for part in range(PARTS):
        group = [jnp.zeros((1, LANES), F32) for _ in range(rows)]
        for at in range(0, span, piece):
            tile, source = divmod(part * span + at, LANES)
            for c in range(6):
                to, begin = divmod(c * span + at, LANES)
                shift = (begin - source) % LANES
                if (tile, shift) not in turned:
                    turned[tile, shift] = turn(own[:, tile * LANES : (tile + 1) * LANES], shift)
                here = (lane1 >= begin) & (lane1 < begin + piece)
                group[to] = jnp.where(here, turned[tile, shift][c : c + 1], group[to])
        for line in range(lines):
            at = device_at(line, part) * rows
            for r in range(rows - 1):
                out_ref[at + r : at + r + 1] = group[r]
            tile, source = divmod(part * span + line * targets, LANES)
            block = source // targets
            out_ref[at + rows - 1 : at + rows] = group[rows - 1] + backs[tile][block : block + 1]


def sent_rows(ref):
    return ref.shape[0] // lax.axis_size("stars")


def listed_kernel(cap, targets, request_ref, *refs):
    star_refs, (all_ref, listed_ref, slot_ref, table_ref) = refs[:PARTS], refs[PARTS:]
    blocks = star_refs[0].shape[1] // LANES
    mine = part_of(lax.axis_index("stars"))
    for mask, star_ref in enumerate(star_refs):
        stars = star_ref[...]
        all_ref[mask * 8 : (mask + 1) * 8] = stars
        first = (mine ^ mask) * (blocks * 8)
        for pair in range(blocks // 2):
            tiles = [stars[:, (2 * pair + i) * LANES : (2 * pair + i + 1) * LANES] for i in range(2)]
            start = pl.multiple_of(first + pair * 16, 16)
            table_ref[pl.ds(start, 16), :] = split3(jnp.concatenate(tiles, axis=0))
    devices = lax.axis_size("stars")
    lines = devices // PARTS
    width = request_ref.shape[0] // devices
    rows = width - 1
    per_row = PARTS // rows
    at = [device_at(line, mine) * width for line in range(lines)]
    begins = jnp.concatenate([request_ref[pl.ds(first + rows, 1), :] for first in at], axis=0)
    lane = iota((lines, LANES), 1)
    for j in range(rows):
        slot = jnp.zeros((lines, LANES), I32)
        for k in range(1, targets + 1):
            for i in range(per_row):
                column = k * PARTS + j * per_row + i
                begin = begins[:, column : column + 1]
                here = (lane >= begin + i * cap) & (lane >= i * cap) & (lane < (i + 1) * cap)
                slot += jnp.where(here, 1, 0)
        slot_ref[j * lines : (j + 1) * lines] = slot
    lane = iota((1, LANES), 1)
    lane8 = iota((8, LANES), 1)
    for j in range(rows):
        asked = [request_ref[pl.ds(first + j, 1), :] for first in at]
        found = []
        for i in range(per_row):
            columns = []
            for chunk in range(lines // per_row):
                column = asked[chunk * per_row]
                column = turn(column, -i * cap)
                for b in range(1, per_row):
                    column = jnp.where(lane >= b * cap, turn(asked[chunk * per_row + b], (b - i) * cap), column)
                columns.append(column)
            size = blocks * 8
            table = table_ref[(j * per_row + i) * size : (j * per_row + i + 1) * size]
            found.append(pick(table, jnp.concatenate(columns, axis=1)))
        for line in range(lines):
            chunk, b = divmod(line, per_row)
            cols = slice(chunk * LANES, (chunk + 1) * LANES)
            near = turn(found[0][:, cols], -b * cap)
            for i in range(1, per_row):
                near = jnp.where(lane8 >= i * cap, turn(found[i][:, cols], (i - b) * cap), near)
            listed_ref[(j * lines + line) * 8 : (j * lines + line + 1) * 8] = near


def pair_sums(target, source, mass, softening, sums):
    x, y, z = (source[c] - target[c] for c in range(3))
    u, v, w = (source[c] - target[c] for c in range(3, 6))
    inverse = lax.rsqrt(x * x + y * y + z * z + softening)
    square = inverse * inverse
    strength = mass * inverse * square
    radial = (x * u + y * v + z * w) * (3.0 * square)
    return (
        sums[0] + strength * x,
        sums[1] + strength * y,
        sums[2] + strength * z,
        sums[3] + strength * (u - radial * x),
        sums[4] + strength * (v - radial * y),
        sums[5] + strength * (w - radial * z),
    )


def force_kernel(softening, targets, group_step, core, sent_ref, all_ref, listed_ref, slot_ref, out_ref, kept_ref, target_ref):
    devices = lax.axis_size("stars")
    lines = devices // PARTS
    span = lines * targets
    rows = sent_ref.shape[0] // devices
    height = math.lcm(rows, 8)
    sent = sent_ref[0:height]
    for i in range(1, sent_ref.shape[0] // height):
        sent = sent + sent_ref[i * height : (i + 1) * height]
    block = sent[0:rows]
    for i in range(1, height // rows):
        block = block + sent[i * rows : (i + 1) * rows]
    if kept_ref.shape[0] > rows:
        block = jnp.concatenate([block, jnp.zeros((kept_ref.shape[0] - rows, LANES), F32)], axis=0)
    kept_ref[...] = block
    piece = min(span, LANES)
    for at in range(0, span, piece):
        places = [divmod(c * span + at, LANES) for c in range(6)]
        tile = [turn(block[r : r + 1], -begin) for r, begin in places]
        tile = jnp.concatenate([*tile, jnp.zeros((2, LANES), F32)], axis=0).T
        target_ref[at : at + piece, 0:8] = tile[0:piece]
    side = (lax.axis_index("stars") + core) & 1
    lane, row = iota((8, LANES), 1), iota((8, LANES), 0)
    zeros = (jnp.zeros((8, LANES), F32),) * 6
    count = lines // 2
    for first in range(0, count, group_step):
        groups = [2 * n + side for n in range(first, min(first + group_step, count))]
        held = []
        for group in groups:
            tile = target_ref[pl.ds(pl.multiple_of(group * targets, 8), 8), 0:8]
            held.append([jnp.broadcast_to(tile[:, c : c + 1], (8, LANES)) for c in range(6)])

        def add_stars(part, sums, held=held):
            for s in range(all_ref.shape[1] // LANES):
                tile = all_ref[pl.ds(pl.multiple_of(part * 8, 8), 8), s * LANES : (s + 1) * LANES]
                source = [jnp.broadcast_to(tile[c : c + 1], (8, LANES)) for c in range(7)]
                sums = tuple(pair_sums(held[n], source, source[6], softening, sums[n]) for n in range(len(held)))
            return sums

        sums = lax.fori_loop(0, PARTS, add_stars, (zeros,) * len(held))
        for n, group in enumerate(groups):
            irregular = zeros
            for j in range(slot_ref.shape[0] // lines):
                at = j * lines + group
                near = listed_ref[pl.ds(pl.multiple_of(at * 8, 8), 8), :]
                mass = jnp.where(slot_ref[pl.ds(at, 1), :] == row, near[6:7], 0.0)
                irregular = pair_sums(held[n], [near[c : c + 1] for c in range(6)], mass, softening, irregular)
            result = zeros[0]
            for c, values in enumerate(sums[n] + irregular):
                value = jnp.sum(values, axis=1, keepdims=True)
                result = jnp.where(lane == c * targets + row, value, result)
            out_ref[first + n : first + n + 1] = jnp.sum(result, axis=0, keepdims=True)


def share_kernel(mine_ref, partner_ref, *out_refs):
    total = mine_ref[...] + partner_ref[...]
    place = lax.axis_index("stars") // (2 * PARTS)
    for mask, out_ref in enumerate(out_refs):
        chosen = place ^ mask
        result = total[0:1]
        for n in range(1, len(out_refs)):
            result = jnp.where(chosen == n, total[n : n + 1], result)
        out_ref[...] = result


def correct_kernel(targets, kept_ref, *refs):
    sums_refs, (state_ref, forces_ref, terms_ref) = refs[:-3], refs[-3:]
    lines = 2 * len(sums_refs)
    span = lines * targets
    total = sums_refs[0][...]
    for sums_ref in sums_refs[1:]:
        total = total + sums_ref[...]
    kept = kept_ref[...]
    piece = min(span, LANES)
    at = line_of(lax.axis_index("stars")) * targets
    moved = pltpu.roll(kept, (LANES - at % piece) % LANES, 1)
    lane, row = iota((16, LANES), 1), iota((16, LANES), 0)
    on_row = (lane >= row * targets) & (lane < (row + 1) * targets)
    lane1 = iota((1, LANES), 1)
    spread = [jnp.where(on_row, total, 0.0)]
    for c in range(6):
        r, begin = divmod(c * span, LANES)
        value = moved[r : r + 1]
        for q in range(1, span // piece):
            value = jnp.where(at // piece == q, moved[r + q : r + q + 1], value)
        spread.append(jnp.where((lane1 >= begin) & (lane1 < begin + targets), value, 0.0))
    for c in range(7):
        r, begin = divmod(6 * span + c * targets, LANES)
        spread.append(jnp.where((lane1 >= begin) & (lane1 < begin + targets), kept[r : r + 1], 0.0))
    spread.append(jnp.zeros((3, LANES), F32))
    rows = jnp.dot(split3(jnp.concatenate(spread, axis=0)), folding(targets), preferred_element_type=F32)[:, 0:targets]
    accel, jerk, irregular = rows[0:3], rows[3:6], rows[6:12]
    position, velocity, step = rows[16:19], rows[19:22], rows[22:23]
    old_accel, old_jerk = rows[23:26], rows[26:29]
    change = accel - old_accel
    second = 3.0 * change - step * (2.0 * old_jerk + jerk)
    third = -2.0 * change + step * (old_jerk + jerk)
    state_ref[0:3] = position + step * step * (second / 12.0 + third / 20.0)
    state_ref[3:6] = velocity + step * (second / 3.0 + third / 4.0)
    forces = jnp.concatenate([irregular, rows[0:6] - irregular, jnp.zeros((4, targets), F32)], axis=0)
    forces_ref[...] = forces.T[:, 0:12]
    terms_ref[0:3] = second
    terms_ref[3:6] = third


def exchange(rows, devices):
    wide = rows.reshape(devices, 1, -1)
    return lax.all_to_all(wide, "stars", 0, 0, tiled=True).reshape(rows.shape)


def per_device(star_state, old_force, star_mass, elapsed, active_ids, neighbours, list_length):
    stars_dev = star_state.shape[1]
    devices = lax.axis_size("stars")
    lines = devices // PARTS
    targets, slots = neighbours.shape
    cap = 2 * targets * slots // devices
    blocks = stars_dev // LANES
    request_rows = max(1, PARTS * cap // LANES)
    back_rows = -(-(6 * lines + 7) * targets // LANES)
    softening = 0.25 * math.sqrt(slots) / (stars_dev * devices)

    def shape(*dims, dtype=F32):
        return jax.ShapeDtypeStruct(dims, dtype)

    def cost(flops):
        return pl.CostEstimate(flops=flops, bytes_accessed=1 << 20, transcendentals=0)

    def swap(value, mask):
        return lax.ppermute(value, "stars", [(i, i ^ mask) for i in range(devices)])

    request = pl.pallas_call(
        functools.partial(request_kernel, stars_dev, cap),
        out_shape=shape(devices * (request_rows + 1), LANES, dtype=I32),
        in_specs=[HBM] * 3,
        out_specs=VMEM,
        scratch_shapes=[
            pltpu.SMEM((targets,), I32),
            pltpu.SMEM((targets,), I32),
            pltpu.VMEM((targets, slots), I32),
            pltpu.SemaphoreType.DMA((3,)),
        ],
        cost_estimate=pl.CostEstimate(flops=1 << 20, bytes_accessed=1 << 26, transcendentals=0),
    )(active_ids, list_length, neighbours)
    asked = exchange(request, devices)
    stars, star_table, force_table = pl.pallas_call(
        predict_kernel,
        out_shape=(
            shape(8, stars_dev),
            shape(blocks * 8, 3 * LANES, dtype=BF16),
            shape(blocks * 8, 3 * LANES, dtype=BF16),
        ),
        in_specs=[VMEM],
        out_specs=(VMEM,) * 3,
        compiler_params=PARAMS,
        cost_estimate=cost(1 << 20),
    )(jnp.concatenate([star_state, old_force, star_mass[None], elapsed[None]], axis=0))
    shared = [stars, *(swap(stars, 2 * mask) for mask in range(1, PARTS))]
    sent = pl.pallas_call(
        functools.partial(own_kernel, stars_dev, targets),
        out_shape=shape(devices * back_rows, LANES),
        in_specs=[VMEM] * 3,
        out_specs=VMEM,
        compiler_params=PARAMS,
    )(asked, star_table, force_table)
    sent = exchange(sent, devices)
    every, listed, slot = pl.pallas_call(
        functools.partial(listed_kernel, cap, targets),
        out_shape=(
            shape(PARTS * 8, stars_dev),
            shape(lines * request_rows * 8, LANES),
            shape(lines * request_rows, LANES, dtype=I32),
        ),
        in_specs=[VMEM] * (1 + PARTS),
        out_specs=(VMEM,) * 3,
        scratch_shapes=[pltpu.VMEM((PARTS * blocks * 8, 3 * LANES), BF16)],
        compiler_params=PARAMS,
        cost_estimate=cost(1 << 24),
    )(asked, *shared)
    kept_rows = -(-back_rows // 8) * 8

    def forces_of(core):
        return pl.pallas_call(
            functools.partial(force_kernel, softening, targets, 4, core),
            out_shape=(shape(max(8, lines // 2), LANES), shape(kept_rows, LANES)),
            in_specs=[VMEM] * 4,
            out_specs=(VMEM,) * 2,
            scratch_shapes=[pltpu.VMEM((lines * targets, LANES), F32)],
            compiler_params=PARAMS,
        )(sent, every, listed, slot)

    theirs, _ = forces_of(1)
    mine, kept = forces_of(0)
    sums = pl.pallas_call(
        share_kernel,
        out_shape=(shape(1, LANES),) * (lines // 2),
        in_specs=[VMEM] * 2,
        out_specs=(VMEM,) * (lines // 2),
        compiler_params=PARAMS,
    )(mine, swap(theirs, 1))
    sums = [sums[0], *(swap(sums[mask], mask * 2 * PARTS) for mask in range(lines // 2 - 1, 0, -1))]
    state, forces, terms = pl.pallas_call(
        functools.partial(correct_kernel, targets),
        out_shape=(shape(6, targets), shape(targets, 12), shape(6, targets)),
        in_specs=[VMEM] * (1 + lines // 2),
        out_specs=(VMEM,) * 3,
        compiler_params=PARAMS,
    )(kept, *sums)
    return state, forces.T, terms


def solution(mesh):
    placed = (
        P(None, "stars"),
        P(None, "stars"),
        P("stars"),
        P("stars"),
        P("stars"),
        P("stars", None),
        P("stars"),
    )
    return jax.shard_map(
        per_device,
        mesh=mesh,
        in_specs=placed,
        out_specs=(P(None, "stars"), P(None, "stars"), P(None, "stars")),
        check_vma=False,
    )
```

time: 47.7 us -> 43.3 us (0.908)
  blocking collectives: 9.67 us -> 0 us
  starting transfers between devices: 9.88 us -> 18.7 us
  waiting for transfers between devices: 12.7 us -> 10.4 us
  local copies, waits for them, and re-layouts: 1.82 us -> 0.01 us
  other arithmetic: 0 us -> 1 us
  Pallas kernels: 12.7 us -> 12.2 us
    all_to_all x1 -> x0, blocking collectives: 9.67 us -> none  [exchange(): return lax.all_to_all(wide, 'stars', 0, 0, tiled=True).reshape(rows.shape)]
    ppermute x0 -> x7, starting transfers between devices: none -> 8.18 us  [swap(): return lax.ppermute(value, 'stars', [(i, i ^ mask) for i in range(devices)])]
    all_to_all x2, waiting for transfers between devices: 12.7 us -> 8.87 us  [exchange(): return lax.all_to_all(wide, 'stars', 0, 0, tiled=True).reshape(rows.shape)]
    unnamed x8 -> x4, local copies, waits for them, and re-layouts: 1.82 us -> 0.01 us
    ppermute x0 -> x7, waiting for transfers between devices: none -> 1.53 us  [swap(): return lax.ppermute(value, 'stars', [(i, i ^ mask) for i in range(devices)])]
    concatenate x0 -> x1, other arithmetic: none -> 1 us  [per_device(): jnp.concatenate([star_state, old_force, star_mass[None], elapsed[None]],...]
    all_to_all x2, starting transfers between devices: 9.88 us -> 10.5 us  [exchange(): return lax.all_to_all(wide, 'stars', 0, 0, tiled=True).reshape(rows.shape)]
    pallas_call x3 -> x5, Pallas kernels: 8.68 us -> 8.22 us  [the longest x2 6.47 us: forces_of(): pl.pallas_call(functools.partial(force_kernel, softening, targets, 4, cor...]
  transfers between devices with their start and end apart: 2 -> 9, of which waited for: 2 -> 4; matrix products, arithmetic and copies ran while one was open for 0% -> 2% of each run, Pallas kernels for 3% -> 14%
where the time goes in v4:
time: 43.3 us; the launch traced here: 43 us
  starting transfers between devices  18.7 us (43%)
  Pallas kernels  12.2 us (28%)
  waiting for transfers between devices  10.4 us (24%)
  other arithmetic  1 us (2%)
  between operations  0.75 us (2%)
    all_to_all x2, starting transfers between devices, exchange(): return lax.all_to_all(wide, 'stars', 0, 0, tiled=True).reshape(rows.shape)  10.5 us
    all_to_all x2, waiting for transfers between devices, exchange(): return lax.all_to_all(wide, 'stars', 0, 0, tiled=True).reshape(rows.shape)  8.87 us
    ppermute x7, starting transfers between devices, swap(): return lax.ppermute(value, 'stars', [(i, i ^ mask) for i in range(devices)])  8.18 us
    pallas_call x2, Pallas kernels, forces_of(): pl.pallas_call(functools.partial(force_kernel, softening, targets, 4, cor...  6.47 us
    pallas_call x1, Pallas kernels, per_device(): pl.pallas_call(functools.partial(request_kernel, stars_dev, cap), out_sha...  1.95 us
    ppermute x7, waiting for transfers between devices, swap(): return lax.ppermute(value, 'stars', [(i, i ^ mask) for i in range(devices)])  1.53 us
    pallas_call x1, Pallas kernels, per_device(): pl.pallas_call(functools.partial(own_kernel, stars_dev, targets), out_sha...  1.5 us
    pallas_call x1, Pallas kernels, per_device(): pl.pallas_call(functools.partial(listed_kernel, cap, targets), out_shape=...  1.11 us
  transfers between devices with their start and end apart: 9, of which 4 were waited for; matrix products, arithmetic and copies ran while one was open for 2% of the time, Pallas kernels for 14%

profile of v4, /device:TPU:0, one launch (start us, length us, event | category | flops | bytes accessed | tf_op | source)
XLA Modules:
  0.0 43.0 jit_solution(17375384791182676857)
XLA Ops:
  0.6 0.0 copy-start
  0.6 1.9 %shard_map.94 = s32[96,128]{1,0:T(8,128)} custom-call(s32[8]{0:T(128)} %active_hbm.1, s32[8]{0:T(128)} %length_hbm.1, s32[8,128]{1,0:T(8,128)} %listed_hbm.1), custom_call_target="tpu_custom_call" | custom-call | flops 1048576 | bytes 67108864 | tf_op jit(solution)/shard_map/pallas_call | solution.py:417
  2.6 0.0 copy-start.1
  2.6 7.3 %all-to-all-start = ((s32[32,1,384]{2,1,0:T(1,128)}), s32[32,1,384]{2,1,0:T(1,128)S(1)}, u32[]{:S(2)}, u32[]{:S(2)}) async-start(s32[32,1,384]{2,1,0:T(1,128)} %bitcast.11), calls=%async_computation | async-start | bytes 98304 | tf_op jit(solution)/shard_map/all_to_all | solution.py:394
  9.9 0.0 copy-done
  9.9 0.0 copy-done.1
  9.9 1.0 %pad_maximum_fusion.given_ref = f32[14,4096]{1,0:T(8,128)S(1)} fusion(f32[1,4096]{1,0:T(1,128)S(1)} %bitcast.12, f32[1,4096]{1,0:T(1,128)} %bitcast.13, f32[6,4096]{1,0:T(8,128)S(1)} %copy-done, f32[6,4096]{1,0:T(8,128)} %param.7), kind=kLoop, calls=%fused_computation | loop fusion | flops 172032 | bytes 458752 | tf_op jit(solution)/shard_map/concatenate | solution.py:442
  10.9 0.2 shard_map.95
  11.2 2.7 %collective-permute-start.2 = (f32[8,4096]{1,0:T(8,128)S(1)}, f32[8,4096]{1,0:T(8,128)S(1)}, u32[]{:S(2)}, u32[]{:S(2)}) collective-permute-start(f32[8,4096]{1,0:T(8,128)S(1)} %get-tuple-element.21.refs_0_), channel_id=1, source_target_pairs={{0,6},{1,7},{2,4},{3,5},{4,2},{5,3},{6,0},{7,1},{8,14},{9,15},{10,... | collective-permute-start | bytes 393224 | tf_op jit(solution)/shard_map/ppermute | solution.py:415
  13.9 0.6 %collective-permute-start.1 = (f32[8,4096]{1,0:T(8,128)S(1)}, f32[8,4096]{1,0:T(8,128)S(1)}, u32[]{:S(2)}, u32[]{:S(2)}) collective-permute-start(f32[8,4096]{1,0:T(8,128)S(1)} %get-tuple-element.21.refs_0_), channel_id=1, source_target_pairs={{0,4},{1,5},{2,6},{3,7},{4,0},{5,1},{6,2},{7,3},{8,12},{9,13},{10,... | collective-permute-start | bytes 393224 | tf_op jit(solution)/shard_map/ppermute | solution.py:415
  14.5 0.3 collective-permute-start
  14.7 2.6 %all-to-all-done = s32[32,1,384]{2,1,0:T(1,128)S(1)} async-done(((s32[32,1,384]{2,1,0:T(1,128)}), s32[32,1,384]{2,1,0:T(1,128)S(1)}, u32[]{:S(2)}, u32[]{:S(2)}) %all-to-all-start) | async-done | bytes 49184 | tf_op jit(solution)/shard_map/all_to_all | solution.py:394
  17.3 1.5 %shard_map.96 = f32[128,128]{1,0:T(8,128)} custom-call(s32[96,128]{1,0:T(8,128)S(1)} %bitcast.9, bf16[256,384]{1,0:T(8,128)(2,1)S(1)} %get-tuple-element.19.star_table_ref, bf16[256,384]{1,0:T(8,128)(2,1)S(1)} %get-tuple-element.20.force_table_ref), custom_call_target="tpu_custom_call" | custom-call | tf_op jit(solution)/shard_map/pallas_call | solution.py:444
  18.8 3.2 %all-to-all-start.1 = ((f32[32,1,512]{2,1,0:T(1,128)}), f32[32,1,512]{2,1,0:T(1,128)S(1)}, u32[]{:S(2)}, u32[]{:S(2)}) async-start(f32[32,1,512]{2,1,0:T(1,128)} %bitcast.4), calls=%async_computation.1 | async-start | bytes 131072 | tf_op jit(solution)/shard_map/all_to_all | solution.py:394
  22.1 0.0 collective-permute-done.2.refs_3_
  22.1 0.0 collective-permute-done.1.refs_2_
  22.1 0.0 collective-permute-done.refs_1_
  22.1 1.1 %shard_map.97 = (f32[32,4096]{1,0:T(8,128)S(1)}, f32[128,128]{1,0:T(8,128)S(1)}, s32[16,128]{1,0:T(8,128)S(1)}) custom-call(s32[96,128]{1,0:T(8,128)S(1)} %bitcast.10, f32[8,4096]{1,0:T(8,128)S(1)} %get-tuple-element.21.refs_0_, f32[8,4096]{1,0:T(8,128)S(1)} %collective-permute-done.refs_1_, f32[8,4096]{1,0:T(8,128)S(1)} %collective-permute-done.1.refs_2_, ...), custom_call_target="tpu_custom_call" | custom-call | flops 16777216 | bytes 1048576 | tf_op jit(solution)/shard_map/pallas_call | solution.py:452
  23.2 6.3 %all-to-all-done.1 = f32[32,1,512]{2,1,0:T(1,128)S(1)} async-done(((f32[32,1,512]{2,1,0:T(1,128)}), f32[32,1,512]{2,1,0:T(1,128)S(1)}, u32[]{:S(2)}, u32[]{:S(2)}) %all-to-all-start.1) | async-done | bytes 65568 | tf_op jit(solution)/shard_map/all_to_all | solution.py:394
  29.5 3.2 %shard_map.99 = (f32[8,128]{1,0:T(8,128)S(1)}, f32[8,128]{1,0:T(8,128)}) custom-call(f32[128,128]{1,0:T(8,128)S(1)} %bitcast.7, f32[32,4096]{1,0:T(8,128)S(1)} %get-tuple-element.22.all_ref, f32[128,128]{1,0:T(8,128)S(1)} %get-tuple-element.23.listed_ref, s32[16,128]{1,0:T(8,128)S(1)} %get-tuple-element.24.slot_ref), custom_call_target="tpu_custom_call" | custom-call | tf_op jit(solution)/shard_map/pallas_call | solution.py:468
  32.7 0.2 collective-permute-start.3
  32.9 3.2 %shard_map.98 = (f32[8,128]{1,0:T(8,128)S(1)}, f32[8,128]{1,0:T(8,128)S(1)}) custom-call(f32[128,128]{1,0:T(8,128)S(1)} %bitcast.8, f32[32,4096]{1,0:T(8,128)S(1)} %get-tuple-element.22.all_ref, f32[128,128]{1,0:T(8,128)S(1)} %get-tuple-element.23.listed_ref, s32[16,128]{1,0:T(8,128)S(1)} %get-tuple-element.24.slot_ref), custom_call_target="tpu_custom_call" | custom-call | tf_op jit(solution)/shard_map/pallas_call | solution.py:468
  36.1 0.0 collective-permute-done.3.partner_ref
  36.2 0.9 %collective-permute-start.4 = (f32[1,128]{1,0:T(1,128)S(1)}, f32[1,128]{1,0:T(1,128)S(1)}, u32[]{:S(2)}, u32[]{:S(2)}) collective-permute-start(f32[1,128]{1,0:T(1,128)S(1)} %get-tuple-element.29), channel_id=1, source_target_pairs={{0,24},{1,25},{2,26},{3,27},{4,28},{5,29},{6,30},{7,31},{8,16},{9,... | collective-permute-start | bytes 1544 | tf_op jit(solution)/shard_map/ppermute | solution.py:415
  37.1 1.2 %collective-permute-start.5 = (f32[1,128]{1,0:T(1,128)S(1)}, f32[1,128]{1,0:T(1,128)S(1)}, u32[]{:S(2)}, u32[]{:S(2)}) collective-permute-start(f32[1,128]{1,0:T(1,128)S(1)} %get-tuple-element.30), channel_id=1, source_target_pairs={{0,16},{1,17},{2,18},{3,19},{4,20},{5,21},{6,22},{7,23},{8,24},{9,... | collective-permute-start | bytes 1544 | tf_op jit(solution)/shard_map/ppermute | solution.py:415
  38.2 2.4 %collective-permute-start.6 = (f32[1,128]{1,0:T(1,128)S(1)}, f32[1,128]{1,0:T(1,128)S(1)}, u32[]{:S(2)}, u32[]{:S(2)}) collective-permute-start(f32[1,128]{1,0:T(1,128)S(1)} %get-tuple-element.31), channel_id=1, source_target_pairs={{0,8},{1,9},{2,10},{3,11},{4,12},{5,13},{6,14},{7,15},{8,0},{9,1},... | collective-permute-start | bytes 1544 | tf_op jit(solution)/shard_map/ppermute | solution.py:415
  40.6 0.9 %collective-permute-done.4.refs_1_ = f32[1,128]{1,0:T(1,128)S(1)} collective-permute-done((f32[1,128]{1,0:T(1,128)S(1)}, f32[1,128]{1,0:T(1,128)S(1)}, u32[]{:S(2)}, u32[]{:S(2)}) %collective-permute-start.4) | collective-permute-done | bytes 544 | tf_op jit(solution)/shard_map/ppermute | solution.py:415
  41.6 0.0 collective-permute-done.5.refs_2_
  41.6 0.6 %collective-permute-done.6.refs_3_ = f32[1,128]{1,0:T(1,128)S(1)} collective-permute-done((f32[1,128]{1,0:T(1,128)S(1)}, f32[1,128]{1,0:T(1,128)S(1)}, u32[]{:S(2)}, u32[]{:S(2)}) %collective-permute-start.6) | collective-permute-done | bytes 544 | tf_op jit(solution)/shard_map/ppermute | solution.py:415
  42.2 0.9 %shard_map.101 = (f32[6,8]{1,0:T(8,128)}, f32[8,12]{1,0:T(8,128)}, f32[6,8]{1,0:T(8,128)}) custom-call(f32[8,128]{1,0:T(8,128)S(1)} %get-tuple-element.25.kept_ref, f32[1,128]{1,0:T(1,128)S(1)} %get-tuple-element.28.refs_0_, f32[1,128]{1,0:T(1,128)S(1)} %collective-permute-done.4.refs_1_, f32[1,128]{1,0:T(1,128)S(1)} %collective-permute-done.5.refs_2_, ...), custom_call_target="tpu_custom_call" | custom-call | tf_op jit(solution)/shard_map/pallas_call | solution.py:487
  (1 shorter events, 0.0 us)
Async XLA Ops:
  0.6 9.3 %copy-start = (f32[6,4096]{1,0:T(8,128)S(1)}, f32[6,4096]{1,0:T(8,128)}, u32[]{:S(2)}) copy-start(f32[6,4096]{1,0:T(8,128)} %param.8) | copy-start | bytes 294916
  2.6 7.3 %copy-start.1 = (f32[4096]{0:T(1024)S(1)}, f32[4096]{0:T(1024)}, u32[]{:S(2)}) copy-start(f32[4096]{0:T(1024)} %param.10) | copy-start | bytes 49156
  2.6 14.7 %all-to-all-start = ((s32[32,1,384]{2,1,0:T(1,128)}), s32[32,1,384]{2,1,0:T(1,128)S(1)}, u32[]{:S(2)}, u32[]{:S(2)}) async-start(s32[32,1,384]{2,1,0:T(1,128)} %bitcast.11), calls=%async_computation | async-start | bytes 98304 | tf_op jit(solution)/shard_map/all_to_all | solution.py:394
  11.2 10.9 %collective-permute-start.2 = (f32[8,4096]{1,0:T(8,128)S(1)}, f32[8,4096]{1,0:T(8,128)S(1)}, u32[]{:S(2)}, u32[]{:S(2)}) collective-permute-start(f32[8,4096]{1,0:T(8,128)S(1)} %get-tuple-element.21.refs_0_), channel_id=1, source_target_pairs={{0,6},{1,7},{2,4},{3,5},{4,2},{5,3},{6,0},{7,1},{8,14},{9,15},{10,... | collective-permute-start | bytes 393224 | tf_op jit(solution)/shard_map/ppermute | solution.py:415
  13.9 8.2 %collective-permute-start.1 = (f32[8,4096]{1,0:T(8,128)S(1)}, f32[8,4096]{1,0:T(8,128)S(1)}, u32[]{:S(2)}, u32[]{:S(2)}) collective-permute-start(f32[8,4096]{1,0:T(8,128)S(1)} %get-tuple-element.21.refs_0_), channel_id=1, source_target_pairs={{0,4},{1,5},{2,6},{3,7},{4,0},{5,1},{6,2},{7,3},{8,12},{9,13},{10,... | collective-permute-start | bytes 393224 | tf_op jit(solution)/shard_map/ppermute | solution.py:415
  14.5 7.6 %collective-permute-start = (f32[8,4096]{1,0:T(8,128)S(1)}, f32[8,4096]{1,0:T(8,128)S(1)}, u32[]{:S(2)}, u32[]{:S(2)}) collective-permute-start(f32[8,4096]{1,0:T(8,128)S(1)} %get-tuple-element.21.refs_0_), channel_id=1, source_target_pairs={{0,2},{1,3},{2,0},{3,1},{4,6},{5,7},{6,4},{7,5},{8,10},{9,11},{10,... | collective-permute-start | bytes 393224 | tf_op jit(solution)/shard_map/ppermute | solution.py:415
  18.8 10.6 %all-to-all-start.1 = ((f32[32,1,512]{2,1,0:T(1,128)}), f32[32,1,512]{2,1,0:T(1,128)S(1)}, u32[]{:S(2)}, u32[]{:S(2)}) async-start(f32[32,1,512]{2,1,0:T(1,128)} %bitcast.4), calls=%async_computation.1 | async-start | bytes 131072 | tf_op jit(solution)/shard_map/all_to_all | solution.py:394
  32.7 3.4 %collective-permute-start.3 = (f32[8,128]{1,0:T(8,128)S(1)}, f32[8,128]{1,0:T(8,128)S(1)}, u32[]{:S(2)}, u32[]{:S(2)}) collective-permute-start(f32[8,128]{1,0:T(8,128)S(1)} %get-tuple-element.27), channel_id=1, source_target_pairs={{0,1},{1,0},{2,3},{3,2},{4,5},{5,4},{6,7},{7,6},{8,9},{9,8},{10,11... | collective-permute-start | bytes 12296 | tf_op jit(solution)/shard_map/ppermute | solution.py:415
  36.2 5.4 %collective-permute-start.4 = (f32[1,128]{1,0:T(1,128)S(1)}, f32[1,128]{1,0:T(1,128)S(1)}, u32[]{:S(2)}, u32[]{:S(2)}) collective-permute-start(f32[1,128]{1,0:T(1,128)S(1)} %get-tuple-element.29), channel_id=1, source_target_pairs={{0,24},{1,25},{2,26},{3,27},{4,28},{5,29},{6,30},{7,31},{8,16},{9,... | collective-permute-start | bytes 1544 | tf_op jit(solution)/shard_map/ppermute | solution.py:415
  37.1 4.5 %collective-permute-start.5 = (f32[1,128]{1,0:T(1,128)S(1)}, f32[1,128]{1,0:T(1,128)S(1)}, u32[]{:S(2)}, u32[]{:S(2)}) collective-permute-start(f32[1,128]{1,0:T(1,128)S(1)} %get-tuple-element.30), channel_id=1, source_target_pairs={{0,16},{1,17},{2,18},{3,19},{4,20},{5,21},{6,22},{7,23},{8,24},{9,... | collective-permute-start | bytes 1544 | tf_op jit(solution)/shard_map/ppermute | solution.py:415
  38.2 3.9 %collective-permute-start.6 = (f32[1,128]{1,0:T(1,128)S(1)}, f32[1,128]{1,0:T(1,128)S(1)}, u32[]{:S(2)}, u32[]{:S(2)}) collective-permute-start(f32[1,128]{1,0:T(1,128)S(1)} %get-tuple-element.31), channel_id=1, source_target_pairs={{0,8},{1,9},{2,10},{3,11},{4,12},{5,13},{6,14},{7,15},{8,0},{9,1},... | collective-permute-start | bytes 1544 | tf_op jit(solution)/shard_map/ppermute | solution.py:415

commit v5 on v4

--- a/solution.py
+++ b/solution.py
@@ -52,15 +52,15 @@
     return jnp.concatenate([jnp.where(same, 1.0, 0.0).astype(BF16)] * 3, axis=0)
 
 
-def pick(table, column):
+def pick(table, column, rows=8):
     count = column.shape[1]
     low = jnp.where(column < 0, -1, column & (LANES - 1))
     high = lax.shift_right_logical(column, 7)
     hot = jnp.where(iota((LANES, count), 0) == low, 1.0, 0.0).astype(BF16)
     found = jnp.dot(table, jnp.concatenate([hot] * 3, axis=0), preferred_element_type=F32)
-    total = jnp.zeros((8, count), F32)
-    for block in range(table.shape[0] // 8):
-        total += jnp.where(high == block, found[block * 8 : (block + 1) * 8], 0.0)
+    total = jnp.zeros((rows, count), F32)
+    for block in range(table.shape[0] // rows):
+        total += jnp.where(high == block, found[block * rows : (block + 1) * rows], 0.0)
     return total
 
 
@@ -99,7 +99,7 @@
         lows.append((mine[k] * low[k : k + 1]).astype(BF16))
         highs.append((mine[k] * high[k : k + 1]).astype(BF16))
         base = base + ahead[:, LANES:]
-        begins = jnp.where(place == (k + 1) * PARTS, base, begins)
+        begins = jnp.where(place == LANES // 2 + k * PARTS, base, begins)
     planes = jnp.concatenate([jnp.concatenate(lows, axis=1), jnp.concatenate(highs, axis=1)], axis=0)
     placed = lax.dot_general(
         planes, jnp.concatenate(hots, axis=1), (((1,), (1,)), ((), ())), preferred_element_type=F32
@@ -112,7 +112,7 @@
     lane1 = iota((1, LANES), 1)
     actives = jnp.zeros((1, LANES), I32)
     for k in range(targets):
-        actives = jnp.where(lane1 == (targets + 1) * PARTS + k, active_ref[k], actives)
+        actives = jnp.where((lane1 < LANES // 2) & (lane1 % targets == k), active_ref[k], actives)
     size = 2 * PARTS
     height = size * (PARTS // per_row + 1)
     for first in range(0, devices, size):
@@ -126,8 +126,7 @@
         out_ref[at : at + height] = jnp.concatenate(blocks * PARTS, axis=0)
 
 
-def predict_kernel(given_ref, star_ref, star_table_ref, force_table_ref):
-    tables = []
+def predict_kernel(given_ref, star_ref, table_ref):
     for block in range(given_ref.shape[1] // LANES):
         cols = slice(block * LANES, (block + 1) * LANES)
         state, force, mass, step = (given_ref[first:last, cols] for first, last in ((0, 6), (6, 12), (12, 13), (13, 14)))
@@ -136,26 +135,18 @@
         velocity = state[3:6] + step * (accel + 0.5 * step * jerk)
         stars = jnp.concatenate([position, velocity, mass, step], axis=0)
         star_ref[:, cols] = stars
-        tables.append((stars, jnp.concatenate([force, jnp.zeros((2, LANES), F32)], axis=0)))
-        if block % 2:
-            rows = slice((block - 1) * 8, (block + 1) * 8)
-            for table_ref, pair in zip((star_table_ref, force_table_ref), zip(*tables)):
-                table_ref[rows] = split3(jnp.concatenate(pair, axis=0))
-            tables = []
-
-
-def own_kernel(stars_dev, targets, request_ref, star_table_ref, force_table_ref, out_ref):
+        rows = jnp.concatenate([stars, force, jnp.zeros((2, LANES), F32)], axis=0)
+        table_ref[block * 16 : (block + 1) * 16] = split3(rows)
+
+
+def own_kernel(stars_dev, targets, request_ref, table_ref, out_ref):
     devices = out_ref.shape[0] // sent_rows(out_ref)
     lines = devices // PARTS
     width = request_ref.shape[0] // devices
-    first = (targets + 1) * PARTS
     lane, row = iota((devices, LANES), 1), iota((devices, LANES), 0)
     ids = request_ref[pl.ds(width - 1, devices, stride=width), :]
-    ids = jnp.where(lane < targets, turn(ids.astype(F32), -first), 0.0)
-    span = targets
-    while span < LANES:
-        ids = ids + turn(ids, span)
-        span *= 2
+    ids = ids.astype(F32)
+    ids = jnp.where(lane < LANES // 2, ids, turn(ids, LANES // 2))
     per_tile = LANES // targets
     tiles = devices // per_tile
     start = (part_of(row) * lines + line_of(row)) * targets
@@ -166,9 +157,9 @@
         flat.append(jnp.sum(jnp.where(here, ids, 0.0), axis=0, keepdims=True))
     local = jnp.concatenate(flat, axis=1).astype(I32) - lax.axis_index("stars") * stars_dev
     local = jnp.where((local >= 0) & (local < stars_dev), local, -1)
-    own = pick(star_table_ref[...], local)
-    old = pick(force_table_ref[...], local)
-    words = jnp.concatenate([own[7:8], old[0:7]], axis=0)
+    own = pick(table_ref[...], local, 16)
+    words = own[7:14]
+    own = own[0:8]
     span = lines * targets
     last = 6 * span
     fold = folding(targets)
@@ -237,7 +228,7 @@
         slot = jnp.zeros((lines, LANES), I32)
         for k in range(1, targets + 1):
             for i in range(per_row):
-                column = k * PARTS + j * per_row + i
+                column = LANES // 2 + (k - 1) * PARTS + j * per_row + i
                 begin = begins[:, column : column + 1]
                 here = (lane >= begin + i * cap) & (lane >= i * cap) & (lane < (i + 1) * cap)
                 slot += jnp.where(here, 1, 0)
@@ -284,7 +275,9 @@
     )
 
 
-def force_kernel(softening, targets, group_step, core, sent_ref, all_ref, listed_ref, slot_ref, out_ref, kept_ref, target_ref):
+def force_kernel(
+    softening, targets, group_step, core, masks, sent_ref, all_ref, listed_ref, slot_ref, out_ref, *kept_refs
+):
     devices = lax.axis_size("stars")
     lines = devices // PARTS
     span = lines * targets
@@ -296,21 +289,22 @@
     block = sent[0:rows]
     for i in range(1, height // rows):
         block = block + sent[i * rows : (i + 1) * rows]
-    if kept_ref.shape[0] > rows:
-        block = jnp.concatenate([block, jnp.zeros((kept_ref.shape[0] - rows, LANES), F32)], axis=0)
-    kept_ref[...] = block
+    target_ref = kept_refs[-1]
+    for kept_ref in kept_refs[:-1]:
+        kept_ref[0:rows] = block
+        kept_ref[rows:] = jnp.zeros((kept_ref.shape[0] - rows, LANES), F32)
     piece = min(span, LANES)
     for at in range(0, span, piece):
         places = [divmod(c * span + at, LANES) for c in range(6)]
         tile = [turn(block[r : r + 1], -begin) for r, begin in places]
         tile = jnp.concatenate([*tile, jnp.zeros((2, LANES), F32)], axis=0).T
         target_ref[at : at + piece, 0:8] = tile[0:piece]
-    side = (lax.axis_index("stars") + core) & 1
+    me = lax.axis_index("stars")
+    side, place = (me + core) & 1, me // (2 * PARTS)
     lane, row = iota((8, LANES), 1), iota((8, LANES), 0)
     zeros = (jnp.zeros((8, LANES), F32),) * 6
-    count = lines // 2
-    for first in range(0, count, group_step):
-        groups = [2 * n + side for n in range(first, min(first + group_step, count))]
+    for first in range(0, len(masks), group_step):
+        groups = [2 * (place ^ mask) + side for mask in masks[first : first + group_step]]
         held = []
         for group in groups:
             tile = target_ref[pl.ds(pl.multiple_of(group * targets, 8), 8), 0:8]
@@ -339,22 +333,16 @@
 
 
 def share_kernel(mine_ref, partner_ref, *out_refs):
-    total = mine_ref[...] + partner_ref[...]
-    place = lax.axis_index("stars") // (2 * PARTS)
-    for mask, out_ref in enumerate(out_refs):
-        chosen = place ^ mask
-        result = total[0:1]
-        for n in range(1, len(out_refs)):
-            result = jnp.where(chosen == n, total[n : n + 1], result)
-        out_ref[...] = result
-
-
-def correct_kernel(targets, kept_ref, *refs):
+    for n, out_ref in enumerate(out_refs):
+        out_ref[...] = mine_ref[n : n + 1] + partner_ref[n + 1 : n + 2]
+
+
+def correct_kernel(targets, kept_ref, mine_ref, partner_ref, *refs):
     sums_refs, (state_ref, forces_ref, terms_ref) = refs[:-3], refs[-3:]
-    lines = 2 * len(sums_refs)
+    lines = 2 * (len(sums_refs) + 1)
     span = lines * targets
-    total = sums_refs[0][...]
-    for sums_ref in sums_refs[1:]:
+    total = mine_ref[0:1] + partner_ref[0:1]
+    for sums_ref in sums_refs:
         total = total + sums_ref[...]
     kept = kept_ref[...]
     piece = min(span, LANES)
@@ -428,15 +416,11 @@
         cost_estimate=pl.CostEstimate(flops=1 << 20, bytes_accessed=1 << 26, transcendentals=0),
     )(active_ids, list_length, neighbours)
     asked = exchange(request, devices)
-    stars, star_table, force_table = pl.pallas_call(
+    stars, table = pl.pallas_call(
         predict_kernel,
-        out_shape=(
-            shape(8, stars_dev),
-            shape(blocks * 8, 3 * LANES, dtype=BF16),
-            shape(blocks * 8, 3 * LANES, dtype=BF16),
-        ),
+        out_shape=(shape(8, stars_dev), shape(blocks * 16, 3 * LANES, dtype=BF16)),
         in_specs=[VMEM],
-        out_specs=(VMEM,) * 3,
+        out_specs=(VMEM,) * 2,
         compiler_params=PARAMS,
         cost_estimate=cost(1 << 20),
     )(jnp.concatenate([star_state, old_force, star_mass[None], elapsed[None]], axis=0))
@@ -444,10 +428,10 @@
     sent = pl.pallas_call(
         functools.partial(own_kernel, stars_dev, targets),
         out_shape=shape(devices * back_rows, LANES),
-        in_specs=[VMEM] * 3,
+        in_specs=[VMEM] * 2,
         out_specs=VMEM,
         compiler_params=PARAMS,
-    )(asked, star_table, force_table)
+    )(asked, table)
     sent = exchange(sent, devices)
     every, listed, slot = pl.pallas_call(
         functools.partial(listed_kernel, cap, targets),
@@ -464,33 +448,37 @@
     )(asked, *shared)
     kept_rows = -(-back_rows // 8) * 8
 
-    def forces_of(core):
+    places = lines // 2
+
+    def forces_of(core, masks, *kept):
         return pl.pallas_call(
-            functools.partial(force_kernel, softening, targets, 4, core),
-            out_shape=(shape(max(8, lines // 2), LANES), shape(kept_rows, LANES)),
+            functools.partial(force_kernel, softening, targets, 4, core, masks),
+            out_shape=(shape(-(-len(masks) // 8) * 8, LANES), *kept),
             in_specs=[VMEM] * 4,
-            out_specs=(VMEM,) * 2,
+            out_specs=(VMEM,) * (1 + len(kept)),
             scratch_shapes=[pltpu.VMEM((lines * targets, LANES), F32)],
             compiler_params=PARAMS,
         )(sent, every, listed, slot)
 
-    theirs, _ = forces_of(1)
-    mine, kept = forces_of(0)
+    (theirs,) = forces_of(1, range(places))
+    (others,) = forces_of(0, range(1, places))
+    theirs = swap(theirs, 1)
     sums = pl.pallas_call(
         share_kernel,
-        out_shape=(shape(1, LANES),) * (lines // 2),
+        out_shape=(shape(1, LANES),) * (places - 1),
         in_specs=[VMEM] * 2,
-        out_specs=(VMEM,) * (lines // 2),
+        out_specs=(VMEM,) * (places - 1),
         compiler_params=PARAMS,
-    )(mine, swap(theirs, 1))
-    sums = [sums[0], *(swap(sums[mask], mask * 2 * PARTS) for mask in range(lines // 2 - 1, 0, -1))]
+    )(others, theirs)
+    sums = [swap(sums[mask - 1], mask * 2 * PARTS) for mask in range(places - 1, 0, -1)]
+    mine, kept = forces_of(0, range(1), shape(kept_rows, LANES))
     state, forces, terms = pl.pallas_call(
         functools.partial(correct_kernel, targets),
         out_shape=(shape(6, targets), shape(targets, 12), shape(6, targets)),
-        in_specs=[VMEM] * (1 + lines // 2),
+        in_specs=[VMEM] * (2 + places),
         out_specs=(VMEM,) * 3,
         compiler_params=PARAMS,
-    )(kept, *sums)
+    )(kept, mine, theirs, *sums)
     return state, forces.T, terms
 
 

time: 43.3 us -> 42.5 us (0.982)
  waiting for transfers between devices: 10.4 us -> 9.31 us
    ppermute x7, waiting for transfers between devices: 1.53 us -> 0.45 us  [swap(): return lax.ppermute(value, 'stars', [(i, i ^ mask) for i in range(devices)])]
    pallas_call x2 -> x3, Pallas kernels: 6.47 us -> 6.86 us  [forces_of(): pl.pallas_call(functools.partial(force_kernel, softening, targets, 4, cor...]
  transfers between devices with their start and end apart: 9 -> 9, of which waited for: 4 -> 3; matrix products, arithmetic and copies ran while one was open for 2% -> 2% of each run, Pallas kernels for 14% -> 15%
where the time goes in v5:
time: 42.5 us; the launch traced here: 42.1 us
  starting transfers between devices  18.7 us (44%)
  Pallas kernels  12.3 us (29%)
  waiting for transfers between devices  9.31 us (22%)
  other arithmetic  1 us (2%)
  between operations  0.76 us (2%)
    all_to_all x2, starting transfers between devices, exchange(): return lax.all_to_all(wide, 'stars', 0, 0, tiled=True).reshape(rows.shape)  10.5 us
    all_to_all x2, waiting for transfers between devices, exchange(): return lax.all_to_all(wide, 'stars', 0, 0, tiled=True).reshape(rows.shape)  8.86 us
    ppermute x7, starting transfers between devices, swap(): return lax.ppermute(value, 'stars', [(i, i ^ mask) for i in range(devices)])  8.18 us
    pallas_call x3, Pallas kernels, forces_of(): pl.pallas_call(functools.partial(force_kernel, softening, targets, 4, cor...  6.86 us
    pallas_call x1, Pallas kernels, per_device(): pl.pallas_call(functools.partial(request_kernel, stars_dev, cap), out_sha...  1.94 us
    pallas_call x1, Pallas kernels, per_device(): pl.pallas_call(functools.partial(own_kernel, stars_dev, targets), out_sha...  1.33 us
    pallas_call x1, Pallas kernels, per_device(): pl.pallas_call(functools.partial(listed_kernel, cap, targets), out_shape=...  1.12 us
    concatenate x1, other arithmetic, per_device(): jnp.concatenate([star_state, old_force, star_mass[None], elapsed[None]],...  1 us
  transfers between devices with their start and end apart: 9, of which 3 were waited for; matrix products, arithmetic and copies ran while one was open for 2% of the time, Pallas kernels for 15%

profile of v5, /device:TPU:0, one launch (start us, length us, event | category | flops | bytes accessed | tf_op | source)
XLA Modules:
  0.0 42.1 jit_solution(13879957031155701306)
XLA Ops:
  0.6 0.0 copy-start
  0.6 1.9 %shard_map.94 = s32[96,128]{1,0:T(8,128)} custom-call(s32[8]{0:T(128)} %active_hbm.1, s32[8]{0:T(128)} %length_hbm.1, s32[8,128]{1,0:T(8,128)} %listed_hbm.1), custom_call_target="tpu_custom_call" | custom-call | flops 1048576 | bytes 67108864 | tf_op jit(solution)/shard_map/pallas_call | solution.py:405
  2.6 0.0 copy-start.1
  2.6 7.3 %all-to-all-start = ((s32[32,1,384]{2,1,0:T(1,128)}), s32[32,1,384]{2,1,0:T(1,128)S(1)}, u32[]{:S(2)}, u32[]{:S(2)}) async-start(s32[32,1,384]{2,1,0:T(1,128)} %bitcast.12), calls=%async_computation | async-start | bytes 98304 | tf_op jit(solution)/shard_map/all_to_all | solution.py:382
  9.9 0.0 copy-done
  9.9 0.0 copy-done.1
  9.9 1.0 %pad_maximum_fusion.given_ref = f32[14,4096]{1,0:T(8,128)S(1)} fusion(f32[1,4096]{1,0:T(1,128)S(1)} %bitcast.13, f32[1,4096]{1,0:T(1,128)} %bitcast.14, f32[6,4096]{1,0:T(8,128)S(1)} %copy-done, f32[6,4096]{1,0:T(8,128)} %param.7), kind=kLoop, calls=%fused_computation | loop fusion | flops 172032 | bytes 458752 | tf_op jit(solution)/shard_map/concatenate | solution.py:426
  10.9 0.2 shard_map.95
  11.1 2.7 %collective-permute-start.2 = (f32[8,4096]{1,0:T(8,128)S(1)}, f32[8,4096]{1,0:T(8,128)S(1)}, u32[]{:S(2)}, u32[]{:S(2)}) collective-permute-start(f32[8,4096]{1,0:T(8,128)S(1)} %get-tuple-element.17.refs_0_), channel_id=1, source_target_pairs={{0,6},{1,7},{2,4},{3,5},{4,2},{5,3},{6,0},{7,1},{8,14},{9,15},{10,... | collective-permute-start | bytes 393224 | tf_op jit(solution)/shard_map/ppermute | solution.py:403
  13.9 0.6 %collective-permute-start.1 = (f32[8,4096]{1,0:T(8,128)S(1)}, f32[8,4096]{1,0:T(8,128)S(1)}, u32[]{:S(2)}, u32[]{:S(2)}) collective-permute-start(f32[8,4096]{1,0:T(8,128)S(1)} %get-tuple-element.17.refs_0_), channel_id=1, source_target_pairs={{0,4},{1,5},{2,6},{3,7},{4,0},{5,1},{6,2},{7,3},{8,12},{9,13},{10,... | collective-permute-start | bytes 393224 | tf_op jit(solution)/shard_map/ppermute | solution.py:403
  14.4 0.3 collective-permute-start
  14.7 2.6 %all-to-all-done = s32[32,1,384]{2,1,0:T(1,128)S(1)} async-done(((s32[32,1,384]{2,1,0:T(1,128)}), s32[32,1,384]{2,1,0:T(1,128)S(1)}, u32[]{:S(2)}, u32[]{:S(2)}) %all-to-all-start) | async-done | bytes 49184 | tf_op jit(solution)/shard_map/all_to_all | solution.py:382
  17.3 1.3 %shard_map.96 = f32[128,128]{1,0:T(8,128)} custom-call(s32[96,128]{1,0:T(8,128)S(1)} %bitcast.10, bf16[512,384]{1,0:T(8,128)(2,1)S(1)} %get-tuple-element.16.table_ref), custom_call_target="tpu_custom_call" | custom-call | tf_op jit(solution)/shard_map/pallas_call | solution.py:428
  18.6 3.2 %all-to-all-start.1 = ((f32[32,1,512]{2,1,0:T(1,128)}), f32[32,1,512]{2,1,0:T(1,128)S(1)}, u32[]{:S(2)}, u32[]{:S(2)}) async-start(f32[32,1,512]{2,1,0:T(1,128)} %bitcast.4), calls=%async_computation.1 | async-start | bytes 131072 | tf_op jit(solution)/shard_map/all_to_all | solution.py:382
  21.9 0.0 collective-permute-done.2.refs_3_
  21.9 0.0 collective-permute-done.1.refs_2_
  21.9 0.0 collective-permute-done.refs_1_
  21.9 1.1 %shard_map.97 = (f32[32,4096]{1,0:T(8,128)S(1)}, f32[128,128]{1,0:T(8,128)S(1)}, s32[16,128]{1,0:T(8,128)S(1)}) custom-call(s32[96,128]{1,0:T(8,128)S(1)} %bitcast.11, f32[8,4096]{1,0:T(8,128)S(1)} %get-tuple-element.17.refs_0_, f32[8,4096]{1,0:T(8,128)S(1)} %collective-permute-done.refs_1_, f32[8,4096]{1,0:T(8,128)S(1)} %collective-permute-done.1.refs_2_, ...), custom_call_target="tpu_custom_call" | custom-call | flops 16777216 | bytes 1048576 | tf_op jit(solution)/shard_map/pallas_call | solution.py:436
  23.0 6.3 %all-to-all-done.1 = f32[32,1,512]{2,1,0:T(1,128)S(1)} async-done(((f32[32,1,512]{2,1,0:T(1,128)}), f32[32,1,512]{2,1,0:T(1,128)S(1)}, u32[]{:S(2)}, u32[]{:S(2)}) %all-to-all-start.1) | async-done | bytes 65568 | tf_op jit(solution)/shard_map/all_to_all | solution.py:382
  29.3 3.2 %shard_map.99 = f32[8,128]{1,0:T(8,128)S(1)} custom-call(f32[128,128]{1,0:T(8,128)S(1)} %bitcast.7, f32[32,4096]{1,0:T(8,128)S(1)} %get-tuple-element.18.all_ref, f32[128,128]{1,0:T(8,128)S(1)} %get-tuple-element.19.listed_ref, s32[16,128]{1,0:T(8,128)S(1)} %get-tuple-element.20.slot_ref), custom_call_target="tpu_custom_call" | custom-call | tf_op jit(solution)/shard_map/pallas_call | solution.py:454
  32.5 0.2 collective-permute-start.3
  32.7 2.5 %shard_map.100.mine_ref = f32[8,128]{1,0:T(8,128)S(1)} custom-call(f32[128,128]{1,0:T(8,128)S(1)} %bitcast.8, f32[32,4096]{1,0:T(8,128)S(1)} %get-tuple-element.18.all_ref, f32[128,128]{1,0:T(8,128)S(1)} %get-tuple-element.19.listed_ref, s32[16,128]{1,0:T(8,128)S(1)} %get-tuple-element.20.slot_ref), custom_call_target="tpu_custom_call" | custom-call | tf_op jit(solution)/shard_map/pallas_call | solution.py:454
  35.3 0.0 collective-permute-done.3.partner_ref
  35.3 0.9 %collective-permute-start.4 = (f32[1,128]{1,0:T(1,128)S(1)}, f32[1,128]{1,0:T(1,128)S(1)}, u32[]{:S(2)}, u32[]{:S(2)}) collective-permute-start(f32[1,128]{1,0:T(1,128)S(1)} %get-tuple-element.23), channel_id=1, source_target_pairs={{0,24},{1,25},{2,26},{3,27},{4,28},{5,29},{6,30},{7,31},{8,16},{9,... | collective-permute-start | bytes 1544 | tf_op jit(solution)/shard_map/ppermute | solution.py:403
  36.2 1.2 %collective-permute-start.5 = (f32[1,128]{1,0:T(1,128)S(1)}, f32[1,128]{1,0:T(1,128)S(1)}, u32[]{:S(2)}, u32[]{:S(2)}) collective-permute-start(f32[1,128]{1,0:T(1,128)S(1)} %get-tuple-element.24), channel_id=1, source_target_pairs={{0,16},{1,17},{2,18},{3,19},{4,20},{5,21},{6,22},{7,23},{8,24},{9,... | collective-permute-start | bytes 1544 | tf_op jit(solution)/shard_map/ppermute | solution.py:403
  37.3 2.4 %collective-permute-start.6 = (f32[1,128]{1,0:T(1,128)S(1)}, f32[1,128]{1,0:T(1,128)S(1)}, u32[]{:S(2)}, u32[]{:S(2)}) collective-permute-start(f32[1,128]{1,0:T(1,128)S(1)} %get-tuple-element.25), channel_id=1, source_target_pairs={{0,8},{1,9},{2,10},{3,11},{4,12},{5,13},{6,14},{7,15},{8,0},{9,1},... | collective-permute-start | bytes 1544 | tf_op jit(solution)/shard_map/ppermute | solution.py:403
  39.7 1.1 %shard_map.98 = (f32[8,128]{1,0:T(8,128)S(1)}, f32[8,128]{1,0:T(8,128)S(1)}) custom-call(f32[128,128]{1,0:T(8,128)S(1)} %bitcast.9, f32[32,4096]{1,0:T(8,128)S(1)} %get-tuple-element.18.all_ref, f32[128,128]{1,0:T(8,128)S(1)} %get-tuple-element.19.listed_ref, s32[16,128]{1,0:T(8,128)S(1)} %get-tuple-element.20.slot_ref), custom_call_target="tpu_custom_call" | custom-call | tf_op jit(solution)/shard_map/pallas_call | solution.py:454
  40.8 0.0 collective-permute-done.4.refs_0_
  40.8 0.0 collective-permute-done.5.refs_1_
  40.8 0.4 %collective-permute-done.6.refs_2_ = f32[1,128]{1,0:T(1,128)S(1)} collective-permute-done((f32[1,128]{1,0:T(1,128)S(1)}, f32[1,128]{1,0:T(1,128)S(1)}, u32[]{:S(2)}, u32[]{:S(2)}) %collective-permute-start.6) | collective-permute-done | bytes 544 | tf_op jit(solution)/shard_map/ppermute | solution.py:403
  41.3 0.9 %shard_map.102 = (f32[6,8]{1,0:T(8,128)}, f32[8,12]{1,0:T(8,128)}, f32[6,8]{1,0:T(8,128)}) custom-call(f32[8,128]{1,0:T(8,128)S(1)} %get-tuple-element.21.kept_ref, f32[8,128]{1,0:T(8,128)S(1)} %get-tuple-element.22.mine_ref, f32[8,128]{1,0:T(8,128)S(1)} %collective-permute-done.3.partner_ref, f32[1,128]{1,0:T(1,128)S(1)} %collective-permute-done.4.refs_0_, ...), custom_call_target="tpu_custom_call" | custom-call | tf_op jit(solution)/shard_map/pallas_call | solution.py:475
  (1 shorter events, 0.0 us)
Async XLA Ops:
  0.6 9.3 %copy-start = (f32[6,4096]{1,0:T(8,128)S(1)}, f32[6,4096]{1,0:T(8,128)}, u32[]{:S(2)}) copy-start(f32[6,4096]{1,0:T(8,128)} %param.8) | copy-start | bytes 294916
  2.6 7.3 %copy-start.1 = (f32[4096]{0:T(1024)S(1)}, f32[4096]{0:T(1024)}, u32[]{:S(2)}) copy-start(f32[4096]{0:T(1024)} %param.10) | copy-start | bytes 49156
  2.6 14.7 %all-to-all-start = ((s32[32,1,384]{2,1,0:T(1,128)}), s32[32,1,384]{2,1,0:T(1,128)S(1)}, u32[]{:S(2)}, u32[]{:S(2)}) async-start(s32[32,1,384]{2,1,0:T(1,128)} %bitcast.12), calls=%async_computation | async-start | bytes 98304 | tf_op jit(solution)/shard_map/all_to_all | solution.py:382
  11.1 10.7 %collective-permute-start.2 = (f32[8,4096]{1,0:T(8,128)S(1)}, f32[8,4096]{1,0:T(8,128)S(1)}, u32[]{:S(2)}, u32[]{:S(2)}) collective-permute-start(f32[8,4096]{1,0:T(8,128)S(1)} %get-tuple-element.17.refs_0_), channel_id=1, source_target_pairs={{0,6},{1,7},{2,4},{3,5},{4,2},{5,3},{6,0},{7,1},{8,14},{9,15},{10,... | collective-permute-start | bytes 393224 | tf_op jit(solution)/shard_map/ppermute | solution.py:403
  13.9 8.0 %collective-permute-start.1 = (f32[8,4096]{1,0:T(8,128)S(1)}, f32[8,4096]{1,0:T(8,128)S(1)}, u32[]{:S(2)}, u32[]{:S(2)}) collective-permute-start(f32[8,4096]{1,0:T(8,128)S(1)} %get-tuple-element.17.refs_0_), channel_id=1, source_target_pairs={{0,4},{1,5},{2,6},{3,7},{4,0},{5,1},{6,2},{7,3},{8,12},{9,13},{10,... | collective-permute-start | bytes 393224 | tf_op jit(solution)/shard_map/ppermute | solution.py:403
  14.4 7.5 %collective-permute-start = (f32[8,4096]{1,0:T(8,128)S(1)}, f32[8,4096]{1,0:T(8,128)S(1)}, u32[]{:S(2)}, u32[]{:S(2)}) collective-permute-start(f32[8,4096]{1,0:T(8,128)S(1)} %get-tuple-element.17.refs_0_), channel_id=1, source_target_pairs={{0,2},{1,3},{2,0},{3,1},{4,6},{5,7},{6,4},{7,5},{8,10},{9,11},{10,... | collective-permute-start | bytes 393224 | tf_op jit(solution)/shard_map/ppermute | solution.py:403
  18.6 10.6 %all-to-all-start.1 = ((f32[32,1,512]{2,1,0:T(1,128)}), f32[32,1,512]{2,1,0:T(1,128)S(1)}, u32[]{:S(2)}, u32[]{:S(2)}) async-start(f32[32,1,512]{2,1,0:T(1,128)} %bitcast.4), calls=%async_computation.1 | async-start | bytes 131072 | tf_op jit(solution)/shard_map/all_to_all | solution.py:382
  32.5 2.7 %collective-permute-start.3 = (f32[8,128]{1,0:T(8,128)S(1)}, f32[8,128]{1,0:T(8,128)S(1)}, u32[]{:S(2)}, u32[]{:S(2)}) collective-permute-start(f32[8,128]{1,0:T(8,128)S(1)} %shard_map.99), channel_id=1, source_target_pairs={{0,1},{1,0},{2,3},{3,2},{4,5},{5,4},{6,7},{7,6},{8,9},{9,8},{10,11... | collective-permute-start | bytes 12296 | tf_op jit(solution)/shard_map/ppermute | solution.py:403
  35.3 5.5 %collective-permute-start.4 = (f32[1,128]{1,0:T(1,128)S(1)}, f32[1,128]{1,0:T(1,128)S(1)}, u32[]{:S(2)}, u32[]{:S(2)}) collective-permute-start(f32[1,128]{1,0:T(1,128)S(1)} %get-tuple-element.23), channel_id=1, source_target_pairs={{0,24},{1,25},{2,26},{3,27},{4,28},{5,29},{6,30},{7,31},{8,16},{9,... | collective-permute-start | bytes 1544 | tf_op jit(solution)/shard_map/ppermute | solution.py:403
  36.2 4.7 %collective-permute-start.5 = (f32[1,128]{1,0:T(1,128)S(1)}, f32[1,128]{1,0:T(1,128)S(1)}, u32[]{:S(2)}, u32[]{:S(2)}) collective-permute-start(f32[1,128]{1,0:T(1,128)S(1)} %get-tuple-element.24), channel_id=1, source_target_pairs={{0,16},{1,17},{2,18},{3,19},{4,20},{5,21},{6,22},{7,23},{8,24},{9,... | collective-permute-start | bytes 1544 | tf_op jit(solution)/shard_map/ppermute | solution.py:403
  37.3 3.9 %collective-permute-start.6 = (f32[1,128]{1,0:T(1,128)S(1)}, f32[1,128]{1,0:T(1,128)S(1)}, u32[]{:S(2)}, u32[]{:S(2)}) collective-permute-start(f32[1,128]{1,0:T(1,128)S(1)} %get-tuple-element.25), channel_id=1, source_target_pairs={{0,8},{1,9},{2,10},{3,11},{4,12},{5,13},{6,14},{7,15},{8,0},{9,1},... | collective-permute-start | bytes 1544 | tf_op jit(solution)/shard_map/ppermute | solution.py:403

commit v6 on v5

--- a/solution.py
+++ b/solution.py
@@ -64,15 +64,20 @@
     return total
 
 
-def request_kernel(
-    stars_dev, cap, active_hbm, length_hbm, listed_hbm, out_ref, active_ref, length_ref, listed_ref, sems
-):
-    pairs = ((listed_hbm, listed_ref), (length_hbm, length_ref), (active_hbm, active_ref))
-    copies = [pltpu.make_async_copy(*pair, sems.at[i]) for i, pair in enumerate(pairs)]
+def first_kernel(stars_dev, cap, *refs):
+    sources, (request_ref, star_ref, table_ref), targets, sems = refs[:7], refs[7:10], refs[10:17], refs[17]
+    copies = [pltpu.make_async_copy(*pair, sems.at[i]) for i, pair in enumerate(zip(sources, targets))]
     for copy in copies:
         copy.start()
-    for copy in copies:
+    for copy in copies[:3]:
         copy.wait()
+    sort_requests(stars_dev, cap, *targets[:3], request_ref)
+    for copy in copies[3:]:
+        copy.wait()
+    predict(*targets[3:], star_ref, table_ref)
+
+
+def sort_requests(stars_dev, cap, active_ref, length_ref, listed_ref, out_ref):
     targets, slots = listed_ref.shape
     devices = lax.axis_size("stars")
     listed = listed_ref[...]
@@ -126,10 +131,11 @@
         out_ref[at : at + height] = jnp.concatenate(blocks * PARTS, axis=0)
 
 
-def predict_kernel(given_ref, star_ref, table_ref):
-    for block in range(given_ref.shape[1] // LANES):
+def predict(state_ref, force_ref, mass_ref, elapsed_ref, star_ref, table_ref):
+    for block in range(mass_ref.shape[0]):
         cols = slice(block * LANES, (block + 1) * LANES)
-        state, force, mass, step = (given_ref[first:last, cols] for first, last in ((0, 6), (6, 12), (12, 13), (13, 14)))
+        state, force = state_ref[:, cols], force_ref[:, cols]
+        mass, step = mass_ref[block : block + 1], elapsed_ref[block : block + 1]
         accel, jerk = force[0:3], force[3:6]
         position = state[0:3] + step * (state[3:6] + step * (0.5 * accel + step * jerk / 6.0))
         velocity = state[3:6] + step * (accel + 0.5 * step * jerk)
@@ -208,7 +214,7 @@
     star_refs, (all_ref, listed_ref, slot_ref, table_ref) = refs[:PARTS], refs[PARTS:]
     blocks = star_refs[0].shape[1] // LANES
     mine = part_of(lax.axis_index("stars"))
-    for mask, star_ref in enumerate(star_refs):
+    for mask, star_ref in zip((0, *(3, 2, 1)), star_refs):
         stars = star_ref[...]
         all_ref[mask * 8 : (mask + 1) * 8] = stars
         first = (mine ^ mask) * (blocks * 8)
@@ -402,29 +408,34 @@
     def swap(value, mask):
         return lax.ppermute(value, "stars", [(i, i ^ mask) for i in range(devices)])
 
-    request = pl.pallas_call(
-        functools.partial(request_kernel, stars_dev, cap),
-        out_shape=shape(devices * (request_rows + 1), LANES, dtype=I32),
-        in_specs=[HBM] * 3,
-        out_specs=VMEM,
+    given = (
+        active_ids,
+        list_length,
+        neighbours,
+        star_state,
+        old_force,
+        star_mass.reshape(blocks, LANES),
+        elapsed.reshape(blocks, LANES),
+    )
+    request, stars, table = pl.pallas_call(
+        functools.partial(first_kernel, stars_dev, cap),
+        out_shape=(
+            shape(devices * (request_rows + 1), LANES, dtype=I32),
+            pltpu.VMEM((8, stars_dev), F32),
+            pltpu.VMEM((blocks * 16, 3 * LANES), BF16),
+        ),
+        in_specs=[HBM] * 7,
+        out_specs=(VMEM,) * 3,
         scratch_shapes=[
             pltpu.SMEM((targets,), I32),
             pltpu.SMEM((targets,), I32),
-            pltpu.VMEM((targets, slots), I32),
-            pltpu.SemaphoreType.DMA((3,)),
+            *(pltpu.VMEM(value.shape, value.dtype) for value in given[2:]),
+            pltpu.SemaphoreType.DMA((7,)),
         ],
-        cost_estimate=pl.CostEstimate(flops=1 << 20, bytes_accessed=1 << 26, transcendentals=0),
-    )(active_ids, list_length, neighbours)
+        compiler_params=PARAMS,
+    )(*(pltpu.with_memory_space_constraint(value, pltpu.HBM) for value in given))
     asked = exchange(request, devices)
-    stars, table = pl.pallas_call(
-        predict_kernel,
-        out_shape=(shape(8, stars_dev), shape(blocks * 16, 3 * LANES, dtype=BF16)),
-        in_specs=[VMEM],
-        out_specs=(VMEM,) * 2,
-        compiler_params=PARAMS,
-        cost_estimate=cost(1 << 20),
-    )(jnp.concatenate([star_state, old_force, star_mass[None], elapsed[None]], axis=0))
-    shared = [stars, *(swap(stars, 2 * mask) for mask in range(1, PARTS))]
+    shared = [stars, *(swap(stars, 2 * mask) for mask in (3, 2, 1))]
     sent = pl.pallas_call(
         functools.partial(own_kernel, stars_dev, targets),
         out_shape=shape(devices * back_rows, LANES),

time: 42.5 us -> 41.5 us (0.976)
  waiting for transfers between devices: 9.31 us -> 10.5 us
  other arithmetic: 1 us -> 0 us
  starting transfers between devices: 18.7 us -> 18 us
    all_to_all x2, waiting for transfers between devices: 8.86 us -> 10 us  [exchange(): return lax.all_to_all(wide, 'stars', 0, 0, tiled=True).reshape(rows.shape)]
    concatenate x1 -> x0, other arithmetic: 1 us -> none  [per_device(): jnp.concatenate([star_state, old_force, star_mass[None], elapsed[None]],...]
    all_to_all x2, starting transfers between devices: 10.5 us -> 9.85 us  [exchange(): return lax.all_to_all(wide, 'stars', 0, 0, tiled=True).reshape(rows.shape)]
    pallas_call x2 -> x1, Pallas kernels: 2.15 us -> 1.88 us  [per_device(): pl.pallas_call(functools.partial(first_kernel, stars_dev, cap), out_shape...]
  transfers between devices with their start and end apart: 9 -> 9, of which waited for: 3 -> 3; matrix products, arithmetic and copies ran while one was open for 2% -> 0% of each run, Pallas kernels for 15% -> 15%
where the time goes in v6:
time: 41.5 us; the launch traced here: 41.3 us
  starting transfers between devices  18 us (43%)
  Pallas kernels  12.1 us (29%)
  waiting for transfers between devices  10.5 us (25%)
  between operations  0.73 us (2%)
    all_to_all x2, waiting for transfers between devices, exchange(): return lax.all_to_all(wide, 'stars', 0, 0, tiled=True).reshape(rows.shape)  10 us
    all_to_all x2, starting transfers between devices, exchange(): return lax.all_to_all(wide, 'stars', 0, 0, tiled=True).reshape(rows.shape)  9.85 us
    ppermute x7, starting transfers between devices, swap(): return lax.ppermute(value, 'stars', [(i, i ^ mask) for i in range(devices)])  8.18 us
    pallas_call x3, Pallas kernels, forces_of(): pl.pallas_call(functools.partial(force_kernel, softening, targets, 4, cor...  6.86 us
    pallas_call x1, Pallas kernels, per_device(): pl.pallas_call(functools.partial(first_kernel, stars_dev, cap), out_shape...  1.88 us
    pallas_call x1, Pallas kernels, per_device(): pl.pallas_call(functools.partial(own_kernel, stars_dev, targets), out_sha...  1.31 us
    pallas_call x1, Pallas kernels, per_device(): pl.pallas_call(functools.partial(listed_kernel, cap, targets), out_shape=...  1.12 us
    pallas_call x1, Pallas kernels, per_device(): pl.pallas_call(functools.partial(correct_kernel, targets), out_shape=(sha...  0.88 us
  transfers between devices with their start and end apart: 9, of which 3 were waited for; matrix products, arithmetic and copies ran while one was open for 0% of the time, Pallas kernels for 15%

profile of v6, /device:TPU:0, one launch (start us, length us, event | category | flops | bytes accessed | tf_op | source)
XLA Modules:
  0.0 41.3 jit_solution(11424629395880083264)
XLA Ops:
  0.6 1.9 %shard_map.94 = (s32[96,128]{1,0:T(8,128)}, f32[8,4096]{1,0:T(8,128)S(1)}, bf16[512,384]{1,0:T(8,128)(2,1)S(1)}) custom-call(s32[8]{0:T(128)} %refs_0_.1, s32[8]{0:T(128)} %refs_1_.1, s32[8,128]{1,0:T(8,128)} %refs_2_.1, f32[6,4096]{1,0:T(8,128)} %refs_3_.1, f32[6,4096]{1,0:T(8,128)} %refs_4_.1, f32[32,128]{1,0:T(8,128)} %bitcast.12, f32[32,128]{1,0:T(8,128)} %bitcast.13), custom_call_target="tpu_custom_call" | custom-call | tf_op jit(solution)/shard_map/pallas_call | solution.py:420
  2.5 7.3 %all-to-all-start = ((s32[32,1,384]{2,1,0:T(1,128)}), s32[32,1,384]{2,1,0:T(1,128)S(1)}, u32[]{:S(2)}, u32[]{:S(2)}) async-start(s32[32,1,384]{2,1,0:T(1,128)} %bitcast.2), calls=%async_computation | async-start | bytes 98304 | tf_op jit(solution)/shard_map/all_to_all | solution.py:388
  9.8 1.8 %collective-permute-start.2 = (f32[8,4096]{1,0:T(8,128)S(1)}, f32[8,4096]{1,0:T(8,128)S(1)}, u32[]{:S(2)}, u32[]{:S(2)}) collective-permute-start(f32[8,4096]{1,0:T(8,128)S(1)} %get-tuple-element.19.refs_0_), channel_id=1, source_target_pairs={{0,2},{1,3},{2,0},{3,1},{4,6},{5,7},{6,4},{7,5},{8,10},{9,11},{10,... | collective-permute-start | bytes 393224 | tf_op jit(solution)/shard_map/ppermute | solution.py:409
  11.7 1.5 %collective-permute-start.1 = (f32[8,4096]{1,0:T(8,128)S(1)}, f32[8,4096]{1,0:T(8,128)S(1)}, u32[]{:S(2)}, u32[]{:S(2)}) collective-permute-start(f32[8,4096]{1,0:T(8,128)S(1)} %get-tuple-element.19.refs_0_), channel_id=1, source_target_pairs={{0,4},{1,5},{2,6},{3,7},{4,0},{5,1},{6,2},{7,3},{8,12},{9,13},{10,... | collective-permute-start | bytes 393224 | tf_op jit(solution)/shard_map/ppermute | solution.py:409
  13.1 0.3 collective-permute-start
  13.4 3.8 %all-to-all-done = s32[32,1,384]{2,1,0:T(1,128)S(1)} async-done(((s32[32,1,384]{2,1,0:T(1,128)}), s32[32,1,384]{2,1,0:T(1,128)S(1)}, u32[]{:S(2)}, u32[]{:S(2)}) %all-to-all-start) | async-done | bytes 49184 | tf_op jit(solution)/shard_map/all_to_all | solution.py:388
  17.2 1.3 %shard_map.95 = f32[128,128]{1,0:T(8,128)} custom-call(s32[96,128]{1,0:T(8,128)S(1)} %bitcast.10, bf16[512,384]{1,0:T(8,128)(2,1)S(1)} %get-tuple-element.18.table_ref), custom_call_target="tpu_custom_call" | custom-call | tf_op jit(solution)/shard_map/pallas_call | solution.py:439
  18.5 2.5 %all-to-all-start.1 = ((f32[32,1,512]{2,1,0:T(1,128)}), f32[32,1,512]{2,1,0:T(1,128)S(1)}, u32[]{:S(2)}, u32[]{:S(2)}) async-start(f32[32,1,512]{2,1,0:T(1,128)} %bitcast.4), calls=%async_computation.1 | async-start | bytes 131072 | tf_op jit(solution)/shard_map/all_to_all | solution.py:388
  21.0 0.0 collective-permute-done.2.refs_3_
  21.1 0.0 collective-permute-done.1.refs_2_
  21.1 0.0 collective-permute-done.refs_1_
  21.1 1.1 %shard_map.96 = (f32[32,4096]{1,0:T(8,128)S(1)}, f32[128,128]{1,0:T(8,128)S(1)}, s32[16,128]{1,0:T(8,128)S(1)}) custom-call(s32[96,128]{1,0:T(8,128)S(1)} %bitcast.11, f32[8,4096]{1,0:T(8,128)S(1)} %get-tuple-element.19.refs_0_, f32[8,4096]{1,0:T(8,128)S(1)} %collective-permute-done.refs_1_, f32[8,4096]{1,0:T(8,128)S(1)} %collective-permute-done.1.refs_2_, ...), custom_call_target="tpu_custom_call" | custom-call | flops 16777216 | bytes 1048576 | tf_op jit(solution)/shard_map/pallas_call | solution.py:447
  22.2 6.3 %all-to-all-done.1 = f32[32,1,512]{2,1,0:T(1,128)S(1)} async-done(((f32[32,1,512]{2,1,0:T(1,128)}), f32[32,1,512]{2,1,0:T(1,128)S(1)}, u32[]{:S(2)}, u32[]{:S(2)}) %all-to-all-start.1) | async-done | bytes 65568 | tf_op jit(solution)/shard_map/all_to_all | solution.py:388
  28.4 3.2 %shard_map.98 = f32[8,128]{1,0:T(8,128)S(1)} custom-call(f32[128,128]{1,0:T(8,128)S(1)} %bitcast.7, f32[32,4096]{1,0:T(8,128)S(1)} %get-tuple-element.20.all_ref, f32[128,128]{1,0:T(8,128)S(1)} %get-tuple-element.21.listed_ref, s32[16,128]{1,0:T(8,128)S(1)} %get-tuple-element.22.slot_ref), custom_call_target="tpu_custom_call" | custom-call | tf_op jit(solution)/shard_map/pallas_call | solution.py:465
  31.7 0.2 collective-permute-start.3
  31.9 2.5 %shard_map.99.mine_ref = f32[8,128]{1,0:T(8,128)S(1)} custom-call(f32[128,128]{1,0:T(8,128)S(1)} %bitcast.8, f32[32,4096]{1,0:T(8,128)S(1)} %get-tuple-element.20.all_ref, f32[128,128]{1,0:T(8,128)S(1)} %get-tuple-element.21.listed_ref, s32[16,128]{1,0:T(8,128)S(1)} %get-tuple-element.22.slot_ref), custom_call_target="tpu_custom_call" | custom-call | tf_op jit(solution)/shard_map/pallas_call | solution.py:465
  34.4 0.0 collective-permute-done.3.partner_ref
  34.5 0.8 %collective-permute-start.4 = (f32[1,128]{1,0:T(1,128)S(1)}, f32[1,128]{1,0:T(1,128)S(1)}, u32[]{:S(2)}, u32[]{:S(2)}) collective-permute-start(f32[1,128]{1,0:T(1,128)S(1)} %get-tuple-element.25), channel_id=1, source_target_pairs={{0,24},{1,25},{2,26},{3,27},{4,28},{5,29},{6,30},{7,31},{8,16},{9,... | collective-permute-start | bytes 1544 | tf_op jit(solution)/shard_map/ppermute | solution.py:409
  35.3 1.2 %collective-permute-start.5 = (f32[1,128]{1,0:T(1,128)S(1)}, f32[1,128]{1,0:T(1,128)S(1)}, u32[]{:S(2)}, u32[]{:S(2)}) collective-permute-start(f32[1,128]{1,0:T(1,128)S(1)} %get-tuple-element.26), channel_id=1, source_target_pairs={{0,16},{1,17},{2,18},{3,19},{4,20},{5,21},{6,22},{7,23},{8,24},{9,... | collective-permute-start | bytes 1544 | tf_op jit(solution)/shard_map/ppermute | solution.py:409
  36.5 2.4 %collective-permute-start.6 = (f32[1,128]{1,0:T(1,128)S(1)}, f32[1,128]{1,0:T(1,128)S(1)}, u32[]{:S(2)}, u32[]{:S(2)}) collective-permute-start(f32[1,128]{1,0:T(1,128)S(1)} %get-tuple-element.27), channel_id=1, source_target_pairs={{0,8},{1,9},{2,10},{3,11},{4,12},{5,13},{6,14},{7,15},{8,0},{9,1},... | collective-permute-start | bytes 1544 | tf_op jit(solution)/shard_map/ppermute | solution.py:409
  38.9 1.1 %shard_map.97 = (f32[8,128]{1,0:T(8,128)S(1)}, f32[8,128]{1,0:T(8,128)S(1)}) custom-call(f32[128,128]{1,0:T(8,128)S(1)} %bitcast.9, f32[32,4096]{1,0:T(8,128)S(1)} %get-tuple-element.20.all_ref, f32[128,128]{1,0:T(8,128)S(1)} %get-tuple-element.21.listed_ref, s32[16,128]{1,0:T(8,128)S(1)} %get-tuple-element.22.slot_ref), custom_call_target="tpu_custom_call" | custom-call | tf_op jit(solution)/shard_map/pallas_call | solution.py:465
  40.0 0.0 collective-permute-done.4.refs_0_
  40.0 0.0 collective-permute-done.5.refs_1_
  40.0 0.4 %collective-permute-done.6.refs_2_ = f32[1,128]{1,0:T(1,128)S(1)} collective-permute-done((f32[1,128]{1,0:T(1,128)S(1)}, f32[1,128]{1,0:T(1,128)S(1)}, u32[]{:S(2)}, u32[]{:S(2)}) %collective-permute-start.6) | collective-permute-done | bytes 544 | tf_op jit(solution)/shard_map/ppermute | solution.py:409
  40.4 0.9 %shard_map.101 = (f32[6,8]{1,0:T(8,128)}, f32[8,12]{1,0:T(8,128)}, f32[6,8]{1,0:T(8,128)}) custom-call(f32[8,128]{1,0:T(8,128)S(1)} %get-tuple-element.23.kept_ref, f32[8,128]{1,0:T(8,128)S(1)} %get-tuple-element.24.mine_ref, f32[8,128]{1,0:T(8,128)S(1)} %collective-permute-done.3.partner_ref, f32[1,128]{1,0:T(1,128)S(1)} %collective-permute-done.4.refs_0_, ...), custom_call_target="tpu_custom_call" | custom-call | tf_op jit(solution)/shard_map/pallas_call | solution.py:486
  (1 shorter events, 0.0 us)
Async XLA Ops:
  2.5 14.7 %all-to-all-start = ((s32[32,1,384]{2,1,0:T(1,128)}), s32[32,1,384]{2,1,0:T(1,128)S(1)}, u32[]{:S(2)}, u32[]{:S(2)}) async-start(s32[32,1,384]{2,1,0:T(1,128)} %bitcast.2), calls=%async_computation | async-start | bytes 98304 | tf_op jit(solution)/shard_map/all_to_all | solution.py:388
  9.8 11.2 %collective-permute-start.2 = (f32[8,4096]{1,0:T(8,128)S(1)}, f32[8,4096]{1,0:T(8,128)S(1)}, u32[]{:S(2)}, u32[]{:S(2)}) collective-permute-start(f32[8,4096]{1,0:T(8,128)S(1)} %get-tuple-element.19.refs_0_), channel_id=1, source_target_pairs={{0,2},{1,3},{2,0},{3,1},{4,6},{5,7},{6,4},{7,5},{8,10},{9,11},{10,... | collective-permute-start | bytes 393224 | tf_op jit(solution)/shard_map/ppermute | solution.py:409
  11.7 9.4 %collective-permute-start.1 = (f32[8,4096]{1,0:T(8,128)S(1)}, f32[8,4096]{1,0:T(8,128)S(1)}, u32[]{:S(2)}, u32[]{:S(2)}) collective-permute-start(f32[8,4096]{1,0:T(8,128)S(1)} %get-tuple-element.19.refs_0_), channel_id=1, source_target_pairs={{0,4},{1,5},{2,6},{3,7},{4,0},{5,1},{6,2},{7,3},{8,12},{9,13},{10,... | collective-permute-start | bytes 393224 | tf_op jit(solution)/shard_map/ppermute | solution.py:409
  13.1 7.9 %collective-permute-start = (f32[8,4096]{1,0:T(8,128)S(1)}, f32[8,4096]{1,0:T(8,128)S(1)}, u32[]{:S(2)}, u32[]{:S(2)}) collective-permute-start(f32[8,4096]{1,0:T(8,128)S(1)} %get-tuple-element.19.refs_0_), channel_id=1, source_target_pairs={{0,6},{1,7},{2,4},{3,5},{4,2},{5,3},{6,0},{7,1},{8,14},{9,15},{10,... | collective-permute-start | bytes 393224 | tf_op jit(solution)/shard_map/ppermute | solution.py:409
  18.5 10.0 %all-to-all-start.1 = ((f32[32,1,512]{2,1,0:T(1,128)}), f32[32,1,512]{2,1,0:T(1,128)S(1)}, u32[]{:S(2)}, u32[]{:S(2)}) async-start(f32[32,1,512]{2,1,0:T(1,128)} %bitcast.4), calls=%async_computation.1 | async-start | bytes 131072 | tf_op jit(solution)/shard_map/all_to_all | solution.py:388
  31.7 2.7 %collective-permute-start.3 = (f32[8,128]{1,0:T(8,128)S(1)}, f32[8,128]{1,0:T(8,128)S(1)}, u32[]{:S(2)}, u32[]{:S(2)}) collective-permute-start(f32[8,128]{1,0:T(8,128)S(1)} %shard_map.98), channel_id=1, source_target_pairs={{0,1},{1,0},{2,3},{3,2},{4,5},{5,4},{6,7},{7,6},{8,9},{9,8},{10,11... | collective-permute-start | bytes 12296 | tf_op jit(solution)/shard_map/ppermute | solution.py:409
  34.5 5.5 %collective-permute-start.4 = (f32[1,128]{1,0:T(1,128)S(1)}, f32[1,128]{1,0:T(1,128)S(1)}, u32[]{:S(2)}, u32[]{:S(2)}) collective-permute-start(f32[1,128]{1,0:T(1,128)S(1)} %get-tuple-element.25), channel_id=1, source_target_pairs={{0,24},{1,25},{2,26},{3,27},{4,28},{5,29},{6,30},{7,31},{8,16},{9,... | collective-permute-start | bytes 1544 | tf_op jit(solution)/shard_map/ppermute | solution.py:409
  35.3 4.7 %collective-permute-start.5 = (f32[1,128]{1,0:T(1,128)S(1)}, f32[1,128]{1,0:T(1,128)S(1)}, u32[]{:S(2)}, u32[]{:S(2)}) collective-permute-start(f32[1,128]{1,0:T(1,128)S(1)} %get-tuple-element.26), channel_id=1, source_target_pairs={{0,16},{1,17},{2,18},{3,19},{4,20},{5,21},{6,22},{7,23},{8,24},{9,... | collective-permute-start | bytes 1544 | tf_op jit(solution)/shard_map/ppermute | solution.py:409
  36.5 3.9 %collective-permute-start.6 = (f32[1,128]{1,0:T(1,128)S(1)}, f32[1,128]{1,0:T(1,128)S(1)}, u32[]{:S(2)}, u32[]{:S(2)}) collective-permute-start(f32[1,128]{1,0:T(1,128)S(1)} %get-tuple-element.27), channel_id=1, source_target_pairs={{0,8},{1,9},{2,10},{3,11},{4,12},{5,13},{6,14},{7,15},{8,0},{9,1},... | collective-permute-start | bytes 1544 | tf_op jit(solution)/shard_map/ppermute | solution.py:409

commit v7 on v6

--- a/solution.py
+++ b/solution.py
@@ -47,21 +47,21 @@
     return jnp.concatenate([high, middle, low], axis=1)
 
 
-def folding(targets):
-    same = iota((LANES, LANES), 0) % targets == iota((LANES, LANES), 1) % targets
-    return jnp.concatenate([jnp.where(same, 1.0, 0.0).astype(BF16)] * 3, axis=0)
-
-
 def pick(table, column, rows=8):
     count = column.shape[1]
     low = jnp.where(column < 0, -1, column & (LANES - 1))
     high = lax.shift_right_logical(column, 7)
     hot = jnp.where(iota((LANES, count), 0) == low, 1.0, 0.0).astype(BF16)
     found = jnp.dot(table, jnp.concatenate([hot] * 3, axis=0), preferred_element_type=F32)
-    total = jnp.zeros((rows, count), F32)
-    for block in range(table.shape[0] // rows):
-        total += jnp.where(high == block, found[block * rows : (block + 1) * rows], 0.0)
-    return total
+    level = [found[first : first + rows] for first in range(0, table.shape[0], rows)]
+    bit = 1
+    while len(level) > 1:
+        odd = (high & bit) != 0
+        level = [
+            jnp.where(odd, level[i + 1], level[i]) if i + 1 < len(level) else level[i] for i in range(0, len(level), 2)
+        ]
+        bit *= 2
+    return level[0]
 
 
 def first_kernel(stars_dev, cap, *refs):
@@ -164,25 +164,23 @@
     local = jnp.concatenate(flat, axis=1).astype(I32) - lax.axis_index("stars") * stars_dev
     local = jnp.where((local >= 0) & (local < stars_dev), local, -1)
     own = pick(table_ref[...], local, 16)
-    words = own[7:14]
+    words = own[7:15]
     own = own[0:8]
     span = lines * targets
     last = 6 * span
-    fold = folding(targets)
-    lane, row = iota((per_tile, LANES), 1), iota((per_tile, LANES), 0)
-    on_row = (lane >= row * targets) & (lane < (row + 1) * targets)
+    lane = iota((per_tile, LANES), 1)
     lane1 = iota((1, LANES), 1)
     rows = sent_rows(out_ref)
     backs = []
     for t in range(tiles):
-        tile = words[:, t * LANES : (t + 1) * LANES]
-        spread = jnp.concatenate([jnp.where(on_row, tile[c : c + 1], 0.0) for c in range(7)], axis=0)
-        folded = jnp.dot(split3(spread), fold, preferred_element_type=F32)
         back = jnp.zeros((per_tile, LANES), F32)
+        tile = pltpu.roll(words[:, t * LANES : (t + 1) * LANES], targets, 1, stride=targets, stride_axis=0)
+        tile = turn(tile, last)
         for c in range(7):
             begin = last % LANES + c * targets
             here = (lane >= begin) & (lane < begin + targets)
-            back = jnp.where(here, folded[c * per_tile : (c + 1) * per_tile], back)
+            spread = jnp.broadcast_to(tile[c : c + 1], (per_tile, LANES))
+            back = jnp.where(here, pltpu.roll(spread, 0, 1, stride=targets, stride_axis=0), back)
         backs.append(back)
     piece = min(span, LANES)
     turned = {}
@@ -202,7 +200,7 @@
             for r in range(rows - 1):
                 out_ref[at + r : at + r + 1] = group[r]
             tile, source = divmod(part * span + line * targets, LANES)
-            block = source // targets
+            block = per_tile - 1 - source // targets
             out_ref[at + rows - 1 : at + rows] = group[rows - 1] + backs[tile][block : block + 1]
 
 
@@ -281,12 +279,9 @@
     )
 
 
-def force_kernel(
-    softening, targets, group_step, core, masks, sent_ref, all_ref, listed_ref, slot_ref, out_ref, *kept_refs
-):
+def add_sent(sent_ref, kept_ref, target_ref):
     devices = lax.axis_size("stars")
-    lines = devices // PARTS
-    span = lines * targets
+    span = target_ref.shape[0]
     rows = sent_ref.shape[0] // devices
     height = math.lcm(rows, 8)
     sent = sent_ref[0:height]
@@ -295,16 +290,23 @@
     block = sent[0:rows]
     for i in range(1, height // rows):
         block = block + sent[i * rows : (i + 1) * rows]
-    target_ref = kept_refs[-1]
-    for kept_ref in kept_refs[:-1]:
-        kept_ref[0:rows] = block
-        kept_ref[rows:] = jnp.zeros((kept_ref.shape[0] - rows, LANES), F32)
+    kept_ref[...] = jnp.zeros(kept_ref.shape, F32)
+    kept_ref[0:rows] = block
     piece = min(span, LANES)
     for at in range(0, span, piece):
         places = [divmod(c * span + at, LANES) for c in range(6)]
         tile = [turn(block[r : r + 1], -begin) for r, begin in places]
         tile = jnp.concatenate([*tile, jnp.zeros((2, LANES), F32)], axis=0).T
         target_ref[at : at + piece, 0:8] = tile[0:piece]
+
+
+def first_force_kernel(softening, targets, group_step, core, masks, sent_ref, all_ref, listed_ref, slot_ref, out_ref, kept_ref, target_ref):
+    add_sent(sent_ref, kept_ref, target_ref)
+    force_kernel(softening, targets, group_step, core, masks, target_ref, all_ref, listed_ref, slot_ref, out_ref)
+
+
+def force_kernel(softening, targets, group_step, core, masks, target_ref, all_ref, listed_ref, slot_ref, out_ref):
+    lines = lax.axis_size("stars") // PARTS
     me = lax.axis_index("stars")
     side, place = (me + core) & 1, me // (2 * PARTS)
     lane, row = iota((8, LANES), 1), iota((8, LANES), 0)
@@ -334,13 +336,18 @@
             result = zeros[0]
             for c, values in enumerate(sums[n] + irregular):
                 value = jnp.sum(values, axis=1, keepdims=True)
-                result = jnp.where(lane == c * targets + row, value, result)
+                result = jnp.where(lane == -c * targets % LANES + row, value, result)
             out_ref[first + n : first + n + 1] = jnp.sum(result, axis=0, keepdims=True)
 
 
 def share_kernel(mine_ref, partner_ref, *out_refs):
     for n, out_ref in enumerate(out_refs):
         out_ref[...] = mine_ref[n : n + 1] + partner_ref[n + 1 : n + 2]
+
+
+def unfold(row, targets):
+    wide = jnp.broadcast_to(row, (LANES // targets, LANES))
+    return pltpu.roll(wide, 0, 1, stride=targets, stride_axis=0)[:, 0:targets]
 
 
 def correct_kernel(targets, kept_ref, mine_ref, partner_ref, *refs):
@@ -354,24 +361,24 @@
     piece = min(span, LANES)
     at = line_of(lax.axis_index("stars")) * targets
     moved = pltpu.roll(kept, (LANES - at % piece) % LANES, 1)
-    lane, row = iota((16, LANES), 1), iota((16, LANES), 0)
-    on_row = (lane >= row * targets) & (lane < (row + 1) * targets)
-    lane1 = iota((1, LANES), 1)
-    spread = [jnp.where(on_row, total, 0.0)]
+    turned = {}
+    rows = []
     for c in range(6):
         r, begin = divmod(c * span, LANES)
-        value = moved[r : r + 1]
+        if begin not in turned:
+            turned[begin] = turn(moved, -begin)
+        value = turned[begin][r : r + 1]
         for q in range(1, span // piece):
-            value = jnp.where(at // piece == q, moved[r + q : r + q + 1], value)
-        spread.append(jnp.where((lane1 >= begin) & (lane1 < begin + targets), value, 0.0))
-    for c in range(7):
-        r, begin = divmod(6 * span + c * targets, LANES)
-        spread.append(jnp.where((lane1 >= begin) & (lane1 < begin + targets), kept[r : r + 1], 0.0))
-    spread.append(jnp.zeros((3, LANES), F32))
-    rows = jnp.dot(split3(jnp.concatenate(spread, axis=0)), folding(targets), preferred_element_type=F32)[:, 0:targets]
+            value = jnp.where(at // piece == q, turned[begin][r + q : r + q + 1], value)
+        rows.append(value[:, 0:targets])
+    position, velocity = jnp.concatenate(rows[0:3], axis=0), jnp.concatenate(rows[3:6], axis=0)
+    r, begin = divmod(6 * span, LANES)
+    words = unfold(turn(kept[r : r + 1], -begin), targets)
+    step = words[0:1]
+    old_accel = jnp.concatenate([words[-c : LANES // targets + 1 - c] for c in (1, 2, 3)], axis=0)
+    old_jerk = jnp.concatenate([words[-c : LANES // targets + 1 - c] for c in (4, 5, 6)], axis=0)
+    rows = unfold(total, targets)
     accel, jerk, irregular = rows[0:3], rows[3:6], rows[6:12]
-    position, velocity, step = rows[16:19], rows[19:22], rows[22:23]
-    old_accel, old_jerk = rows[23:26], rows[26:29]
     change = accel - old_accel
     second = 3.0 * change - step * (2.0 * old_jerk + jerk)
     third = -2.0 * change + step * (old_jerk + jerk)
@@ -461,18 +468,19 @@
 
     places = lines // 2
 
-    def forces_of(core, masks, *kept):
+    def forces_of(kernel, core, masks, given, *kept):
         return pl.pallas_call(
-            functools.partial(force_kernel, softening, targets, 4, core, masks),
+            functools.partial(kernel, softening, targets, 4, core, masks),
             out_shape=(shape(-(-len(masks) // 8) * 8, LANES), *kept),
             in_specs=[VMEM] * 4,
             out_specs=(VMEM,) * (1 + len(kept)),
-            scratch_shapes=[pltpu.VMEM((lines * targets, LANES), F32)],
             compiler_params=PARAMS,
-        )(sent, every, listed, slot)
-
-    (theirs,) = forces_of(1, range(places))
-    (others,) = forces_of(0, range(1, places))
+        )(given, every, listed, slot)
+
+    theirs, kept, upright = forces_of(
+        first_force_kernel, 1, range(places), sent, shape(kept_rows, LANES), shape(lines * targets, LANES)
+    )
+    (others,) = forces_of(force_kernel, 0, range(1, places), upright)
     theirs = swap(theirs, 1)
     sums = pl.pallas_call(
         share_kernel,
@@ -482,7 +490,7 @@
         compiler_params=PARAMS,
     )(others, theirs)
     sums = [swap(sums[mask - 1], mask * 2 * PARTS) for mask in range(places - 1, 0, -1)]
-    mine, kept = forces_of(0, range(1), shape(kept_rows, LANES))
+    (mine,) = forces_of(force_kernel, 0, range(1), upright)
     state, forces, terms = pl.pallas_call(
         functools.partial(correct_kernel, targets),
         out_shape=(shape(6, targets), shape(targets, 12), shape(6, targets)),

time: 41.5 us -> 41.1 us (level)
  Pallas kernels: 12.1 us -> 11.3 us
  transfers between devices with their start and end apart: 9 -> 9, of which waited for: 3 -> 4; matrix products, arithmetic and copies ran while one was open for 0% -> 0% of each run, Pallas kernels for 15% -> 13%
where the time goes in v7:
time: 41.1 us; the launch traced here: 40.8 us
  starting transfers between devices  18 us (44%)
  Pallas kernels  11.3 us (27%)
  waiting for transfers between devices  10.8 us (26%)
  between operations  0.72 us (2%)
    all_to_all x2, waiting for transfers between devices, exchange(): return lax.all_to_all(wide, 'stars', 0, 0, tiled=True).reshape(rows.shape)  10.2 us
    all_to_all x2, starting transfers between devices, exchange(): return lax.all_to_all(wide, 'stars', 0, 0, tiled=True).reshape(rows.shape)  9.85 us
    ppermute x7, starting transfers between devices, swap(): return lax.ppermute(value, 'stars', [(i, i ^ mask) for i in range(devices)])  8.18 us
    pallas_call x3, Pallas kernels, forces_of(): pl.pallas_call(functools.partial(kernel, softening, targets, 4, core, mas...  6.5 us
    pallas_call x1, Pallas kernels, per_device(): pl.pallas_call(functools.partial(first_kernel, stars_dev, cap), out_shape...  1.88 us
    pallas_call x1, Pallas kernels, per_device(): pl.pallas_call(functools.partial(own_kernel, stars_dev, targets), out_sha...  1.16 us
    pallas_call x1, Pallas kernels, per_device(): pl.pallas_call(functools.partial(listed_kernel, cap, targets), out_shape=...  0.99 us
  transfers between devices with their start and end apart: 9, of which 4 were waited for; matrix products, arithmetic and copies ran while one was open for 0% of the time, Pallas kernels for 13%

profile of v7, /device:TPU:0, one launch (start us, length us, event | category | flops | bytes accessed | tf_op | source)
XLA Modules:
  0.0 40.8 jit_solution(928007444175729523)
XLA Ops:
  0.6 1.9 %shard_map.94 = (s32[96,128]{1,0:T(8,128)}, f32[8,4096]{1,0:T(8,128)S(1)}, bf16[512,384]{1,0:T(8,128)(2,1)S(1)}) custom-call(s32[8]{0:T(128)} %refs_0_.1, s32[8]{0:T(128)} %refs_1_.1, s32[8,128]{1,0:T(8,128)} %refs_2_.1, f32[6,4096]{1,0:T(8,128)} %refs_3_.1, f32[6,4096]{1,0:T(8,128)} %refs_4_.1, f32[32,128]{1,0:T(8,128)} %bitcast.10, f32[32,128]{1,0:T(8,128)} %bitcast.11), custom_call_target="tpu_custom_call" | custom-call | tf_op jit(solution)/shard_map/pallas_call | solution.py:427
  2.5 7.3 %all-to-all-start = ((s32[32,1,384]{2,1,0:T(1,128)}), s32[32,1,384]{2,1,0:T(1,128)S(1)}, u32[]{:S(2)}, u32[]{:S(2)}) async-start(s32[32,1,384]{2,1,0:T(1,128)} %bitcast.2), calls=%async_computation | async-start | bytes 98304 | tf_op jit(solution)/shard_map/all_to_all | solution.py:395
  9.8 1.8 %collective-permute-start.2 = (f32[8,4096]{1,0:T(8,128)S(1)}, f32[8,4096]{1,0:T(8,128)S(1)}, u32[]{:S(2)}, u32[]{:S(2)}) collective-permute-start(f32[8,4096]{1,0:T(8,128)S(1)} %get-tuple-element.20.refs_0_), channel_id=1, source_target_pairs={{0,2},{1,3},{2,0},{3,1},{4,6},{5,7},{6,4},{7,5},{8,10},{9,11},{10,... | collective-permute-start | bytes 393224 | tf_op jit(solution)/shard_map/ppermute | solution.py:416
  11.7 1.5 %collective-permute-start.1 = (f32[8,4096]{1,0:T(8,128)S(1)}, f32[8,4096]{1,0:T(8,128)S(1)}, u32[]{:S(2)}, u32[]{:S(2)}) collective-permute-start(f32[8,4096]{1,0:T(8,128)S(1)} %get-tuple-element.20.refs_0_), channel_id=1, source_target_pairs={{0,4},{1,5},{2,6},{3,7},{4,0},{5,1},{6,2},{7,3},{8,12},{9,13},{10,... | collective-permute-start | bytes 393224 | tf_op jit(solution)/shard_map/ppermute | solution.py:416
  13.1 0.3 collective-permute-start
  13.4 3.8 %all-to-all-done = s32[32,1,384]{2,1,0:T(1,128)S(1)} async-done(((s32[32,1,384]{2,1,0:T(1,128)}), s32[32,1,384]{2,1,0:T(1,128)S(1)}, u32[]{:S(2)}, u32[]{:S(2)}) %all-to-all-start) | async-done | bytes 49184 | tf_op jit(solution)/shard_map/all_to_all | solution.py:395
  17.2 1.2 %shard_map.95 = f32[128,128]{1,0:T(8,128)} custom-call(s32[96,128]{1,0:T(8,128)S(1)} %bitcast.7, bf16[512,384]{1,0:T(8,128)(2,1)S(1)} %get-tuple-element.19.table_ref), custom_call_target="tpu_custom_call" | custom-call | tf_op jit(solution)/shard_map/pallas_call | solution.py:446
  18.3 2.5 %all-to-all-start.1 = ((f32[32,1,512]{2,1,0:T(1,128)}), f32[32,1,512]{2,1,0:T(1,128)S(1)}, u32[]{:S(2)}, u32[]{:S(2)}) async-start(f32[32,1,512]{2,1,0:T(1,128)} %bitcast.4), calls=%async_computation.1 | async-start | bytes 131072 | tf_op jit(solution)/shard_map/all_to_all | solution.py:395
  20.9 0.0 collective-permute-done.2.refs_3_
  20.9 0.0 collective-permute-done.1.refs_2_
  20.9 0.0 collective-permute-done.refs_1_
  20.9 1.0 %shard_map.96 = (f32[32,4096]{1,0:T(8,128)S(1)}, f32[128,128]{1,0:T(8,128)S(1)}, s32[16,128]{1,0:T(8,128)S(1)}) custom-call(s32[96,128]{1,0:T(8,128)S(1)} %bitcast.8, f32[8,4096]{1,0:T(8,128)S(1)} %get-tuple-element.20.refs_0_, f32[8,4096]{1,0:T(8,128)S(1)} %collective-permute-done.refs_1_, f32[8,4096]{1,0:T(8,128)S(1)} %collective-permute-done.1.refs_2_, ...), custom_call_target="tpu_custom_call" | custom-call | flops 16777216 | bytes 1048576 | tf_op jit(solution)/shard_map/pallas_call | solution.py:454
  21.9 6.4 %all-to-all-done.1 = f32[32,1,512]{2,1,0:T(1,128)S(1)} async-done(((f32[32,1,512]{2,1,0:T(1,128)}), f32[32,1,512]{2,1,0:T(1,128)S(1)}, u32[]{:S(2)}, u32[]{:S(2)}) %all-to-all-start.1) | async-done | bytes 65568 | tf_op jit(solution)/shard_map/all_to_all | solution.py:395
  28.3 3.2 %shard_map.97 = (f32[8,128]{1,0:T(8,128)S(1)}, f32[8,128]{1,0:T(8,128)S(1)}, f32[64,128]{1,0:T(8,128)S(1)}) custom-call(f32[128,128]{1,0:T(8,128)S(1)} %bitcast.9, f32[32,4096]{1,0:T(8,128)S(1)} %get-tuple-element.21.all_ref, f32[128,128]{1,0:T(8,128)S(1)} %get-tuple-element.22.listed_ref, s32[16,128]{1,0:T(8,128)S(1)} %get-tuple-element.23.slot_ref), custom_call_target="tpu_custom_call" | custom-call | tf_op jit(solution)/shard_map/pallas_call | solution.py:472
  31.5 0.2 collective-permute-start.3
  31.7 2.4 %shard_map.99.mine_ref = f32[8,128]{1,0:T(8,128)S(1)} custom-call(f32[64,128]{1,0:T(8,128)S(1)} %get-tuple-element.25.target_ref, f32[32,4096]{1,0:T(8,128)S(1)} %get-tuple-element.21.all_ref, f32[128,128]{1,0:T(8,128)S(1)} %get-tuple-element.22.listed_ref, s32[16,128]{1,0:T(8,128)S(1)} %get-tuple-element.23.slot_ref), custom_call_target="tpu_custom_call" | custom-call | tf_op jit(solution)/shard_map/pallas_call | solution.py:472
  34.1 0.0 collective-permute-done.3.partner_ref
  34.1 0.8 %collective-permute-start.4 = (f32[1,128]{1,0:T(1,128)S(1)}, f32[1,128]{1,0:T(1,128)S(1)}, u32[]{:S(2)}, u32[]{:S(2)}) collective-permute-start(f32[1,128]{1,0:T(1,128)S(1)} %get-tuple-element.27), channel_id=1, source_target_pairs={{0,24},{1,25},{2,26},{3,27},{4,28},{5,29},{6,30},{7,31},{8,16},{9,... | collective-permute-start | bytes 1544 | tf_op jit(solution)/shard_map/ppermute | solution.py:416
  34.9 1.2 %collective-permute-start.5 = (f32[1,128]{1,0:T(1,128)S(1)}, f32[1,128]{1,0:T(1,128)S(1)}, u32[]{:S(2)}, u32[]{:S(2)}) collective-permute-start(f32[1,128]{1,0:T(1,128)S(1)} %get-tuple-element.28), channel_id=1, source_target_pairs={{0,16},{1,17},{2,18},{3,19},{4,20},{5,21},{6,22},{7,23},{8,24},{9,... | collective-permute-start | bytes 1544 | tf_op jit(solution)/shard_map/ppermute | solution.py:416
  36.2 2.4 %collective-permute-start.6 = (f32[1,128]{1,0:T(1,128)S(1)}, f32[1,128]{1,0:T(1,128)S(1)}, u32[]{:S(2)}, u32[]{:S(2)}) collective-permute-start(f32[1,128]{1,0:T(1,128)S(1)} %get-tuple-element.29), channel_id=1, source_target_pairs={{0,8},{1,9},{2,10},{3,11},{4,12},{5,13},{6,14},{7,15},{8,0},{9,1},... | collective-permute-start | bytes 1544 | tf_op jit(solution)/shard_map/ppermute | solution.py:416
  38.6 0.9 %shard_map.98.mine_ref = f32[8,128]{1,0:T(8,128)S(1)} custom-call(f32[64,128]{1,0:T(8,128)S(1)} %get-tuple-element.25.target_ref, f32[32,4096]{1,0:T(8,128)S(1)} %get-tuple-element.21.all_ref, f32[128,128]{1,0:T(8,128)S(1)} %get-tuple-element.22.listed_ref, s32[16,128]{1,0:T(8,128)S(1)} %get-tuple-element.23.slot_ref), custom_call_target="tpu_custom_call" | custom-call | tf_op jit(solution)/shard_map/pallas_call | solution.py:472
  39.5 0.1 collective-permute-done.4.refs_0_
  39.5 0.0 collective-permute-done.5.refs_1_
  39.5 0.6 %collective-permute-done.6.refs_2_ = f32[1,128]{1,0:T(1,128)S(1)} collective-permute-done((f32[1,128]{1,0:T(1,128)S(1)}, f32[1,128]{1,0:T(1,128)S(1)}, u32[]{:S(2)}, u32[]{:S(2)}) %collective-permute-start.6) | collective-permute-done | bytes 544 | tf_op jit(solution)/shard_map/ppermute | solution.py:416
  40.1 0.8 %shard_map.101 = (f32[6,8]{1,0:T(8,128)}, f32[8,12]{1,0:T(8,128)}, f32[6,8]{1,0:T(8,128)}) custom-call(f32[8,128]{1,0:T(8,128)S(1)} %get-tuple-element.24.kept_ref, f32[8,128]{1,0:T(8,128)S(1)} %shard_map.98.mine_ref, f32[8,128]{1,0:T(8,128)S(1)} %collective-permute-done.3.partner_ref, f32[1,128]{1,0:T(1,128)S(1)} %collective-permute-done.4.refs_0_, ...), custom_call_target="tpu_custom_call" | custom-call | tf_op jit(solution)/shard_map/pallas_call | solution.py:494
  (1 shorter events, 0.0 us)
Async XLA Ops:
  2.5 14.7 %all-to-all-start = ((s32[32,1,384]{2,1,0:T(1,128)}), s32[32,1,384]{2,1,0:T(1,128)S(1)}, u32[]{:S(2)}, u32[]{:S(2)}) async-start(s32[32,1,384]{2,1,0:T(1,128)} %bitcast.2), calls=%async_computation | async-start | bytes 98304 | tf_op jit(solution)/shard_map/all_to_all | solution.py:395
  9.8 11.1 %collective-permute-start.2 = (f32[8,4096]{1,0:T(8,128)S(1)}, f32[8,4096]{1,0:T(8,128)S(1)}, u32[]{:S(2)}, u32[]{:S(2)}) collective-permute-start(f32[8,4096]{1,0:T(8,128)S(1)} %get-tuple-element.20.refs_0_), channel_id=1, source_target_pairs={{0,2},{1,3},{2,0},{3,1},{4,6},{5,7},{6,4},{7,5},{8,10},{9,11},{10,... | collective-permute-start | bytes 393224 | tf_op jit(solution)/shard_map/ppermute | solution.py:416
  11.7 9.2 %collective-permute-start.1 = (f32[8,4096]{1,0:T(8,128)S(1)}, f32[8,4096]{1,0:T(8,128)S(1)}, u32[]{:S(2)}, u32[]{:S(2)}) collective-permute-start(f32[8,4096]{1,0:T(8,128)S(1)} %get-tuple-element.20.refs_0_), channel_id=1, source_target_pairs={{0,4},{1,5},{2,6},{3,7},{4,0},{5,1},{6,2},{7,3},{8,12},{9,13},{10,... | collective-permute-start | bytes 393224 | tf_op jit(solution)/shard_map/ppermute | solution.py:416
  13.1 7.8 %collective-permute-start = (f32[8,4096]{1,0:T(8,128)S(1)}, f32[8,4096]{1,0:T(8,128)S(1)}, u32[]{:S(2)}, u32[]{:S(2)}) collective-permute-start(f32[8,4096]{1,0:T(8,128)S(1)} %get-tuple-element.20.refs_0_), channel_id=1, source_target_pairs={{0,6},{1,7},{2,4},{3,5},{4,2},{5,3},{6,0},{7,1},{8,14},{9,15},{10,... | collective-permute-start | bytes 393224 | tf_op jit(solution)/shard_map/ppermute | solution.py:416
  18.3 10.0 %all-to-all-start.1 = ((f32[32,1,512]{2,1,0:T(1,128)}), f32[32,1,512]{2,1,0:T(1,128)S(1)}, u32[]{:S(2)}, u32[]{:S(2)}) async-start(f32[32,1,512]{2,1,0:T(1,128)} %bitcast.4), calls=%async_computation.1 | async-start | bytes 131072 | tf_op jit(solution)/shard_map/all_to_all | solution.py:395
  31.5 2.5 %collective-permute-start.3 = (f32[8,128]{1,0:T(8,128)S(1)}, f32[8,128]{1,0:T(8,128)S(1)}, u32[]{:S(2)}, u32[]{:S(2)}) collective-permute-start(f32[8,128]{1,0:T(8,128)S(1)} %get-tuple-element.26), channel_id=1, source_target_pairs={{0,1},{1,0},{2,3},{3,2},{4,5},{5,4},{6,7},{7,6},{8,9},{9,8},{10,11... | collective-permute-start | bytes 12296 | tf_op jit(solution)/shard_map/ppermute | solution.py:416
  34.1 5.4 %collective-permute-start.4 = (f32[1,128]{1,0:T(1,128)S(1)}, f32[1,128]{1,0:T(1,128)S(1)}, u32[]{:S(2)}, u32[]{:S(2)}) collective-permute-start(f32[1,128]{1,0:T(1,128)S(1)} %get-tuple-element.27), channel_id=1, source_target_pairs={{0,24},{1,25},{2,26},{3,27},{4,28},{5,29},{6,30},{7,31},{8,16},{9,... | collective-permute-start | bytes 1544 | tf_op jit(solution)/shard_map/ppermute | solution.py:416
  34.9 4.6 %collective-permute-start.5 = (f32[1,128]{1,0:T(1,128)S(1)}, f32[1,128]{1,0:T(1,128)S(1)}, u32[]{:S(2)}, u32[]{:S(2)}) collective-permute-start(f32[1,128]{1,0:T(1,128)S(1)} %get-tuple-element.28), channel_id=1, source_target_pairs={{0,16},{1,17},{2,18},{3,19},{4,20},{5,21},{6,22},{7,23},{8,24},{9,... | collective-permute-start | bytes 1544 | tf_op jit(solution)/shard_map/ppermute | solution.py:416
  36.2 3.9 %collective-permute-start.6 = (f32[1,128]{1,0:T(1,128)S(1)}, f32[1,128]{1,0:T(1,128)S(1)}, u32[]{:S(2)}, u32[]{:S(2)}) collective-permute-start(f32[1,128]{1,0:T(1,128)S(1)} %get-tuple-element.29), channel_id=1, source_target_pairs={{0,8},{1,9},{2,10},{3,11},{4,12},{5,13},{6,14},{7,15},{8,0},{9,1},... | collective-permute-start | bytes 1544 | tf_op jit(solution)/shard_map/ppermute | solution.py:416

commit v8 on v7

--- a/solution.py
+++ b/solution.py
@@ -10,6 +10,7 @@
 
 LANES = 128
 PARTS = 4
+SPACING = 11
 F32 = jnp.float32
 I32 = jnp.int32
 BF16 = jnp.bfloat16
@@ -32,6 +33,14 @@
 
 def device_at(line, part):
     return (line >> 1) * 2 * PARTS + part * 2 + (line & 1)
+
+
+def spaced(device, devices):
+    return device * SPACING & (devices - 1)
+
+
+def place_of(device, devices):
+    return device * pow(SPACING, -1, devices) & (devices - 1)
 
 
 def turn(value, lanes):
@@ -119,7 +128,7 @@
     for k in range(targets):
         actives = jnp.where((lane1 < LANES // 2) & (lane1 % targets == k), active_ref[k], actives)
     size = 2 * PARTS
-    height = size * (PARTS // per_row + 1)
+    width = PARTS // per_row + 1
     for first in range(0, devices, size):
         blocks = []
         for core in range(2):
@@ -127,8 +136,11 @@
             begin = jnp.sum(begin, axis=0, keepdims=True).astype(I32)
             rows = [packed[first + at + core : first + at + core + 1] for at in range(0, size, 2 * per_row)]
             blocks += [*rows, begin + actives]
-        at = first // size * height
-        out_ref[at : at + height] = jnp.concatenate(blocks * PARTS, axis=0)
+        for core in range(2):
+            block = jnp.concatenate(blocks[core * width : (core + 1) * width], axis=0)
+            for device in range(first + core, first + size, 2):
+                at = place_of(device, devices) * width
+                out_ref[at : at + width] = block
 
 
 def predict(state_ref, force_ref, mass_ref, elapsed_ref, star_ref, table_ref):
@@ -155,7 +167,8 @@
     ids = jnp.where(lane < LANES // 2, ids, turn(ids, LANES // 2))
     per_tile = LANES // targets
     tiles = devices // per_tile
-    start = (part_of(row) * lines + line_of(row)) * targets
+    sender = spaced(row, devices)
+    start = (part_of(sender) * lines + line_of(sender)) * targets
     flat = []
     for t in range(tiles):
         offset = lane + t * LANES - start
@@ -196,7 +209,7 @@
                 here = (lane1 >= begin) & (lane1 < begin + piece)
                 group[to] = jnp.where(here, turned[tile, shift][c : c + 1], group[to])
         for line in range(lines):
-            at = device_at(line, part) * rows
+            at = place_of(device_at(line, part), devices) * rows
             for r in range(rows - 1):
                 out_ref[at + r : at + r + 1] = group[r]
             tile, source = divmod(part * span + line * targets, LANES)
@@ -225,7 +238,7 @@
     width = request_ref.shape[0] // devices
     rows = width - 1
     per_row = PARTS // rows
-    at = [device_at(line, mine) * width for line in range(lines)]
+    at = [place_of(device_at(line, mine), devices) * width for line in range(lines)]
     begins = jnp.concatenate([request_ref[pl.ds(first + rows, 1), :] for first in at], axis=0)
     lane = iota((lines, LANES), 1)
     for j in range(rows):
@@ -392,7 +405,8 @@
 
 def exchange(rows, devices):
     wide = rows.reshape(devices, 1, -1)
-    return lax.all_to_all(wide, "stars", 0, 0, tiled=True).reshape(rows.shape)
+    order = [[spaced(place, devices) for place in range(devices)]]
+    return lax.all_to_all(wide, "stars", 0, 0, axis_index_groups=order, tiled=True).reshape(rows.shape)
 
 
 def per_device(star_state, old_force, star_mass, elapsed, active_ids, neighbours, list_length):

time: 41.1 us -> 40.6 us (0.988)
    all_to_all x2, waiting for transfers between devices: 10.2 us -> 9.72 us  [exchange(): lax.all_to_all(wide, 'stars', 0, 0, axis_index_groups=order, tiled=True)]
where the time goes in v8:
time: 40.6 us; the launch traced here: 40.4 us
  starting transfers between devices  18 us (44%)
  Pallas kernels  11.3 us (28%)
  waiting for transfers between devices  10.4 us (26%)
  between operations  0.72 us (2%)
    all_to_all x2, starting transfers between devices, exchange(): lax.all_to_all(wide, 'stars', 0, 0, axis_index_groups=order, tiled=True)  9.85 us
    all_to_all x2, waiting for transfers between devices, exchange(): lax.all_to_all(wide, 'stars', 0, 0, axis_index_groups=order, tiled=True)  9.72 us
    ppermute x7, starting transfers between devices, swap(): return lax.ppermute(value, 'stars', [(i, i ^ mask) for i in range(devices)])  8.18 us
    pallas_call x3, Pallas kernels, forces_of(): pl.pallas_call(functools.partial(kernel, softening, targets, 4, core, mas...  6.5 us
    pallas_call x1, Pallas kernels, per_device(): pl.pallas_call(functools.partial(first_kernel, stars_dev, cap), out_shape...  1.87 us
    pallas_call x1, Pallas kernels, per_device(): pl.pallas_call(functools.partial(own_kernel, stars_dev, targets), out_sha...  1.16 us
    pallas_call x1, Pallas kernels, per_device(): pl.pallas_call(functools.partial(listed_kernel, cap, targets), out_shape=...  1.02 us
  transfers between devices with their start and end apart: 9, of which 4 were waited for; matrix products, arithmetic and copies ran while one was open for 0% of the time, Pallas kernels for 13%

profile of v8, /device:TPU:0, one launch (start us, length us, event | category | flops | bytes accessed | tf_op | source)
XLA Modules:
  0.0 40.4 jit_solution(15659578127995386935)
XLA Ops:
  0.6 1.9 %shard_map.94 = (s32[96,128]{1,0:T(8,128)}, f32[8,4096]{1,0:T(8,128)S(1)}, bf16[512,384]{1,0:T(8,128)(2,1)S(1)}) custom-call(s32[8]{0:T(128)} %refs_0_.1, s32[8]{0:T(128)} %refs_1_.1, s32[8,128]{1,0:T(8,128)} %refs_2_.1, f32[6,4096]{1,0:T(8,128)} %refs_3_.1, f32[6,4096]{1,0:T(8,128)} %refs_4_.1, f32[32,128]{1,0:T(8,128)} %bitcast.10, f32[32,128]{1,0:T(8,128)} %bitcast.11), custom_call_target="tpu_custom_call" | custom-call | tf_op jit(solution)/shard_map/pallas_call | solution.py:441
  2.5 7.3 %all-to-all-start = ((s32[32,1,384]{2,1,0:T(1,128)}), s32[32,1,384]{2,1,0:T(1,128)S(1)}, u32[]{:S(2)}, u32[]{:S(2)}) async-start(s32[32,1,384]{2,1,0:T(1,128)} %bitcast.2), calls=%async_computation | async-start | bytes 98304 | tf_op jit(solution)/shard_map/all_to_all | solution.py:409
  9.8 1.8 %collective-permute-start.2 = (f32[8,4096]{1,0:T(8,128)S(1)}, f32[8,4096]{1,0:T(8,128)S(1)}, u32[]{:S(2)}, u32[]{:S(2)}) collective-permute-start(f32[8,4096]{1,0:T(8,128)S(1)} %get-tuple-element.20.refs_0_), channel_id=1, source_target_pairs={{0,2},{1,3},{2,0},{3,1},{4,6},{5,7},{6,4},{7,5},{8,10},{9,11},{10,... | collective-permute-start | bytes 393224 | tf_op jit(solution)/shard_map/ppermute | solution.py:430
  11.7 1.5 %collective-permute-start.1 = (f32[8,4096]{1,0:T(8,128)S(1)}, f32[8,4096]{1,0:T(8,128)S(1)}, u32[]{:S(2)}, u32[]{:S(2)}) collective-permute-start(f32[8,4096]{1,0:T(8,128)S(1)} %get-tuple-element.20.refs_0_), channel_id=1, source_target_pairs={{0,4},{1,5},{2,6},{3,7},{4,0},{5,1},{6,2},{7,3},{8,12},{9,13},{10,... | collective-permute-start | bytes 393224 | tf_op jit(solution)/shard_map/ppermute | solution.py:430
  13.1 0.3 collective-permute-start
  13.4 3.6 %all-to-all-done = s32[32,1,384]{2,1,0:T(1,128)S(1)} async-done(((s32[32,1,384]{2,1,0:T(1,128)}), s32[32,1,384]{2,1,0:T(1,128)S(1)}, u32[]{:S(2)}, u32[]{:S(2)}) %all-to-all-start) | async-done | bytes 49184 | tf_op jit(solution)/shard_map/all_to_all | solution.py:409
  17.0 1.2 %shard_map.95 = f32[128,128]{1,0:T(8,128)} custom-call(s32[96,128]{1,0:T(8,128)S(1)} %bitcast.7, bf16[512,384]{1,0:T(8,128)(2,1)S(1)} %get-tuple-element.19.table_ref), custom_call_target="tpu_custom_call" | custom-call | tf_op jit(solution)/shard_map/pallas_call | solution.py:460
  18.1 2.5 %all-to-all-start.1 = ((f32[32,1,512]{2,1,0:T(1,128)}), f32[32,1,512]{2,1,0:T(1,128)S(1)}, u32[]{:S(2)}, u32[]{:S(2)}) async-start(f32[32,1,512]{2,1,0:T(1,128)} %bitcast.4), calls=%async_computation.1 | async-start | bytes 131072 | tf_op jit(solution)/shard_map/all_to_all | solution.py:409
  20.7 0.0 collective-permute-done.2.refs_3_
  20.7 0.0 collective-permute-done.1.refs_2_
  20.7 0.0 collective-permute-done.refs_1_
  20.7 1.0 %shard_map.96 = (f32[32,4096]{1,0:T(8,128)S(1)}, f32[128,128]{1,0:T(8,128)S(1)}, s32[16,128]{1,0:T(8,128)S(1)}) custom-call(s32[96,128]{1,0:T(8,128)S(1)} %bitcast.8, f32[8,4096]{1,0:T(8,128)S(1)} %get-tuple-element.20.refs_0_, f32[8,4096]{1,0:T(8,128)S(1)} %collective-permute-done.refs_1_, f32[8,4096]{1,0:T(8,128)S(1)} %collective-permute-done.1.refs_2_, ...), custom_call_target="tpu_custom_call" | custom-call | flops 16777216 | bytes 1048576 | tf_op jit(solution)/shard_map/pallas_call | solution.py:468
  21.8 6.1 %all-to-all-done.1 = f32[32,1,512]{2,1,0:T(1,128)S(1)} async-done(((f32[32,1,512]{2,1,0:T(1,128)}), f32[32,1,512]{2,1,0:T(1,128)S(1)}, u32[]{:S(2)}, u32[]{:S(2)}) %all-to-all-start.1) | async-done | bytes 65568 | tf_op jit(solution)/shard_map/all_to_all | solution.py:409
  27.9 3.2 %shard_map.97 = (f32[8,128]{1,0:T(8,128)S(1)}, f32[8,128]{1,0:T(8,128)S(1)}, f32[64,128]{1,0:T(8,128)S(1)}) custom-call(f32[128,128]{1,0:T(8,128)S(1)} %bitcast.9, f32[32,4096]{1,0:T(8,128)S(1)} %get-tuple-element.21.all_ref, f32[128,128]{1,0:T(8,128)S(1)} %get-tuple-element.22.listed_ref, s32[16,128]{1,0:T(8,128)S(1)} %get-tuple-element.23.slot_ref), custom_call_target="tpu_custom_call" | custom-call | tf_op jit(solution)/shard_map/pallas_call | solution.py:486
  31.1 0.2 collective-permute-start.3
  31.3 2.4 %shard_map.99.mine_ref = f32[8,128]{1,0:T(8,128)S(1)} custom-call(f32[64,128]{1,0:T(8,128)S(1)} %get-tuple-element.25.target_ref, f32[32,4096]{1,0:T(8,128)S(1)} %get-tuple-element.21.all_ref, f32[128,128]{1,0:T(8,128)S(1)} %get-tuple-element.22.listed_ref, s32[16,128]{1,0:T(8,128)S(1)} %get-tuple-element.23.slot_ref), custom_call_target="tpu_custom_call" | custom-call | tf_op jit(solution)/shard_map/pallas_call | solution.py:486
  33.7 0.0 collective-permute-done.3.partner_ref
  33.7 1.0 %collective-permute-start.4 = (f32[1,128]{1,0:T(1,128)S(1)}, f32[1,128]{1,0:T(1,128)S(1)}, u32[]{:S(2)}, u32[]{:S(2)}) collective-permute-start(f32[1,128]{1,0:T(1,128)S(1)} %get-tuple-element.27), channel_id=1, source_target_pairs={{0,24},{1,25},{2,26},{3,27},{4,28},{5,29},{6,30},{7,31},{8,16},{9,... | collective-permute-start | bytes 1544 | tf_op jit(solution)/shard_map/ppermute | solution.py:430
  34.7 1.2 %collective-permute-start.5 = (f32[1,128]{1,0:T(1,128)S(1)}, f32[1,128]{1,0:T(1,128)S(1)}, u32[]{:S(2)}, u32[]{:S(2)}) collective-permute-start(f32[1,128]{1,0:T(1,128)S(1)} %get-tuple-element.28), channel_id=1, source_target_pairs={{0,16},{1,17},{2,18},{3,19},{4,20},{5,21},{6,22},{7,23},{8,24},{9,... | collective-permute-start | bytes 1544 | tf_op jit(solution)/shard_map/ppermute | solution.py:430
  35.9 2.3 %collective-permute-start.6 = (f32[1,128]{1,0:T(1,128)S(1)}, f32[1,128]{1,0:T(1,128)S(1)}, u32[]{:S(2)}, u32[]{:S(2)}) collective-permute-start(f32[1,128]{1,0:T(1,128)S(1)} %get-tuple-element.29), channel_id=1, source_target_pairs={{0,8},{1,9},{2,10},{3,11},{4,12},{5,13},{6,14},{7,15},{8,0},{9,1},... | collective-permute-start | bytes 1544 | tf_op jit(solution)/shard_map/ppermute | solution.py:430
  38.1 0.9 %shard_map.98.mine_ref = f32[8,128]{1,0:T(8,128)S(1)} custom-call(f32[64,128]{1,0:T(8,128)S(1)} %get-tuple-element.25.target_ref, f32[32,4096]{1,0:T(8,128)S(1)} %get-tuple-element.21.all_ref, f32[128,128]{1,0:T(8,128)S(1)} %get-tuple-element.22.listed_ref, s32[16,128]{1,0:T(8,128)S(1)} %get-tuple-element.23.slot_ref), custom_call_target="tpu_custom_call" | custom-call | tf_op jit(solution)/shard_map/pallas_call | solution.py:486
  39.0 0.1 collective-permute-done.4.refs_0_
  39.1 0.0 collective-permute-done.5.refs_1_
  39.1 0.5 %collective-permute-done.6.refs_2_ = f32[1,128]{1,0:T(1,128)S(1)} collective-permute-done((f32[1,128]{1,0:T(1,128)S(1)}, f32[1,128]{1,0:T(1,128)S(1)}, u32[]{:S(2)}, u32[]{:S(2)}) %collective-permute-start.6) | collective-permute-done | bytes 544 | tf_op jit(solution)/shard_map/ppermute | solution.py:430
  39.7 0.8 %shard_map.101 = (f32[6,8]{1,0:T(8,128)}, f32[8,12]{1,0:T(8,128)}, f32[6,8]{1,0:T(8,128)}) custom-call(f32[8,128]{1,0:T(8,128)S(1)} %get-tuple-element.24.kept_ref, f32[8,128]{1,0:T(8,128)S(1)} %shard_map.98.mine_ref, f32[8,128]{1,0:T(8,128)S(1)} %collective-permute-done.3.partner_ref, f32[1,128]{1,0:T(1,128)S(1)} %collective-permute-done.4.refs_0_, ...), custom_call_target="tpu_custom_call" | custom-call | tf_op jit(solution)/shard_map/pallas_call | solution.py:508
  (1 shorter events, 0.0 us)
Async XLA Ops:
  2.5 14.5 %all-to-all-start = ((s32[32,1,384]{2,1,0:T(1,128)}), s32[32,1,384]{2,1,0:T(1,128)S(1)}, u32[]{:S(2)}, u32[]{:S(2)}) async-start(s32[32,1,384]{2,1,0:T(1,128)} %bitcast.2), calls=%async_computation | async-start | bytes 98304 | tf_op jit(solution)/shard_map/all_to_all | solution.py:409
  9.8 10.9 %collective-permute-start.2 = (f32[8,4096]{1,0:T(8,128)S(1)}, f32[8,4096]{1,0:T(8,128)S(1)}, u32[]{:S(2)}, u32[]{:S(2)}) collective-permute-start(f32[8,4096]{1,0:T(8,128)S(1)} %get-tuple-element.20.refs_0_), channel_id=1, source_target_pairs={{0,2},{1,3},{2,0},{3,1},{4,6},{5,7},{6,4},{7,5},{8,10},{9,11},{10,... | collective-permute-start | bytes 393224 | tf_op jit(solution)/shard_map/ppermute | solution.py:430
  11.7 9.1 %collective-permute-start.1 = (f32[8,4096]{1,0:T(8,128)S(1)}, f32[8,4096]{1,0:T(8,128)S(1)}, u32[]{:S(2)}, u32[]{:S(2)}) collective-permute-start(f32[8,4096]{1,0:T(8,128)S(1)} %get-tuple-element.20.refs_0_), channel_id=1, source_target_pairs={{0,4},{1,5},{2,6},{3,7},{4,0},{5,1},{6,2},{7,3},{8,12},{9,13},{10,... | collective-permute-start | bytes 393224 | tf_op jit(solution)/shard_map/ppermute | solution.py:430
  13.1 7.6 %collective-permute-start = (f32[8,4096]{1,0:T(8,128)S(1)}, f32[8,4096]{1,0:T(8,128)S(1)}, u32[]{:S(2)}, u32[]{:S(2)}) collective-permute-start(f32[8,4096]{1,0:T(8,128)S(1)} %get-tuple-element.20.refs_0_), channel_id=1, source_target_pairs={{0,6},{1,7},{2,4},{3,5},{4,2},{5,3},{6,0},{7,1},{8,14},{9,15},{10,... | collective-permute-start | bytes 393224 | tf_op jit(solution)/shard_map/ppermute | solution.py:430
  18.1 9.7 %all-to-all-start.1 = ((f32[32,1,512]{2,1,0:T(1,128)}), f32[32,1,512]{2,1,0:T(1,128)S(1)}, u32[]{:S(2)}, u32[]{:S(2)}) async-start(f32[32,1,512]{2,1,0:T(1,128)} %bitcast.4), calls=%async_computation.1 | async-start | bytes 131072 | tf_op jit(solution)/shard_map/all_to_all | solution.py:409
  31.1 2.5 %collective-permute-start.3 = (f32[8,128]{1,0:T(8,128)S(1)}, f32[8,128]{1,0:T(8,128)S(1)}, u32[]{:S(2)}, u32[]{:S(2)}) collective-permute-start(f32[8,128]{1,0:T(8,128)S(1)} %get-tuple-element.26), channel_id=1, source_target_pairs={{0,1},{1,0},{2,3},{3,2},{4,5},{5,4},{6,7},{7,6},{8,9},{9,8},{10,11... | collective-permute-start | bytes 12296 | tf_op jit(solution)/shard_map/ppermute | solution.py:430
  33.7 5.4 %collective-permute-start.4 = (f32[1,128]{1,0:T(1,128)S(1)}, f32[1,128]{1,0:T(1,128)S(1)}, u32[]{:S(2)}, u32[]{:S(2)}) collective-permute-start(f32[1,128]{1,0:T(1,128)S(1)} %get-tuple-element.27), channel_id=1, source_target_pairs={{0,24},{1,25},{2,26},{3,27},{4,28},{5,29},{6,30},{7,31},{8,16},{9,... | collective-permute-start | bytes 1544 | tf_op jit(solution)/shard_map/ppermute | solution.py:430
  34.7 4.4 %collective-permute-start.5 = (f32[1,128]{1,0:T(1,128)S(1)}, f32[1,128]{1,0:T(1,128)S(1)}, u32[]{:S(2)}, u32[]{:S(2)}) collective-permute-start(f32[1,128]{1,0:T(1,128)S(1)} %get-tuple-element.28), channel_id=1, source_target_pairs={{0,16},{1,17},{2,18},{3,19},{4,20},{5,21},{6,22},{7,23},{8,24},{9,... | collective-permute-start | bytes 1544 | tf_op jit(solution)/shard_map/ppermute | solution.py:430
  35.9 3.8 %collective-permute-start.6 = (f32[1,128]{1,0:T(1,128)S(1)}, f32[1,128]{1,0:T(1,128)S(1)}, u32[]{:S(2)}, u32[]{:S(2)}) collective-permute-start(f32[1,128]{1,0:T(1,128)S(1)} %get-tuple-element.29), channel_id=1, source_target_pairs={{0,8},{1,9},{2,10},{3,11},{4,12},{5,13},{6,14},{7,15},{8,0},{9,1},... | collective-permute-start | bytes 1544 | tf_op jit(solution)/shard_map/ppermute | solution.py:430

commit v9 on v8

--- a/solution.py
+++ b/solution.py
@@ -135,7 +135,7 @@
             begin = jnp.where((row[:size] & 1) == core, begins[first : first + size], 0.0)
             begin = jnp.sum(begin, axis=0, keepdims=True).astype(I32)
             rows = [packed[first + at + core : first + at + core + 1] for at in range(0, size, 2 * per_row)]
-            blocks += [*rows, begin + actives]
+            blocks += [begin + actives, *rows]
         for core in range(2):
             block = jnp.concatenate(blocks[core * width : (core + 1) * width], axis=0)
             for device in range(first + core, first + size, 2):
@@ -162,7 +162,7 @@
     lines = devices // PARTS
     width = request_ref.shape[0] // devices
     lane, row = iota((devices, LANES), 1), iota((devices, LANES), 0)
-    ids = request_ref[pl.ds(width - 1, devices, stride=width), :]
+    ids = request_ref[pl.ds(0, devices, stride=width), :]
     ids = ids.astype(F32)
     ids = jnp.where(lane < LANES // 2, ids, turn(ids, LANES // 2))
     per_tile = LANES // targets
@@ -239,7 +239,7 @@
     rows = width - 1
     per_row = PARTS // rows
     at = [place_of(device_at(line, mine), devices) * width for line in range(lines)]
-    begins = jnp.concatenate([request_ref[pl.ds(first + rows, 1), :] for first in at], axis=0)
+    begins = jnp.concatenate([request_ref[pl.ds(first, 1), :] for first in at], axis=0)
     lane = iota((lines, LANES), 1)
     for j in range(rows):
         slot = jnp.zeros((lines, LANES), I32)
@@ -253,7 +253,7 @@
     lane = iota((1, LANES), 1)
     lane8 = iota((8, LANES), 1)
     for j in range(rows):
-        asked = [request_ref[pl.ds(first + j, 1), :] for first in at]
+        asked = [request_ref[pl.ds(first + 1 + j, 1), :] for first in at]
         found = []
         for i in range(per_row):
             columns = []

time: 40.6 us -> 40.6 us (level)
  no operation moved by 1% of the time
where the time goes in v9:
time: 40.6 us; the launch traced here: 40.4 us
  starting transfers between devices  18 us (44%)
  Pallas kernels  11.3 us (28%)
  waiting for transfers between devices  10.4 us (26%)
  between operations  0.72 us (2%)
    all_to_all x2, starting transfers between devices, exchange(): lax.all_to_all(wide, 'stars', 0, 0, axis_index_groups=order, tiled=True)  9.85 us
    all_to_all x2, waiting for transfers between devices, exchange(): lax.all_to_all(wide, 'stars', 0, 0, axis_index_groups=order, tiled=True)  9.72 us
    ppermute x7, starting transfers between devices, swap(): return lax.ppermute(value, 'stars', [(i, i ^ mask) for i in range(devices)])  8.18 us
    pallas_call x3, Pallas kernels, forces_of(): pl.pallas_call(functools.partial(kernel, softening, targets, 4, core, mas...  6.5 us
    pallas_call x1, Pallas kernels, per_device(): pl.pallas_call(functools.partial(first_kernel, stars_dev, cap), out_shape...  1.87 us
    pallas_call x1, Pallas kernels, per_device(): pl.pallas_call(functools.partial(own_kernel, stars_dev, targets), out_sha...  1.16 us
    pallas_call x1, Pallas kernels, per_device(): pl.pallas_call(functools.partial(listed_kernel, cap, targets), out_shape=...  1.02 us
  transfers between devices with their start and end apart: 9, of which 4 were waited for; matrix products, arithmetic and copies ran while one was open for 0% of the time, Pallas kernels for 13%

profile of v9, /device:TPU:0, one launch (start us, length us, event | category | flops | bytes accessed | tf_op | source)
XLA Modules:
  0.0 40.4 jit_solution(6803027052806407002)
XLA Ops:
  0.6 1.9 %shard_map.94 = (s32[96,128]{1,0:T(8,128)}, f32[8,4096]{1,0:T(8,128)S(1)}, bf16[512,384]{1,0:T(8,128)(2,1)S(1)}) custom-call(s32[8]{0:T(128)} %refs_0_.1, s32[8]{0:T(128)} %refs_1_.1, s32[8,128]{1,0:T(8,128)} %refs_2_.1, f32[6,4096]{1,0:T(8,128)} %refs_3_.1, f32[6,4096]{1,0:T(8,128)} %refs_4_.1, f32[32,128]{1,0:T(8,128)} %bitcast.10, f32[32,128]{1,0:T(8,128)} %bitcast.11), custom_call_target="tpu_custom_call" | custom-call | tf_op jit(solution)/shard_map/pallas_call | solution.py:441
  2.5 7.3 %all-to-all-start = ((s32[32,1,384]{2,1,0:T(1,128)}), s32[32,1,384]{2,1,0:T(1,128)S(1)}, u32[]{:S(2)}, u32[]{:S(2)}) async-start(s32[32,1,384]{2,1,0:T(1,128)} %bitcast.2), calls=%async_computation | async-start | bytes 98304 | tf_op jit(solution)/shard_map/all_to_all | solution.py:409
  9.8 1.8 %collective-permute-start.2 = (f32[8,4096]{1,0:T(8,128)S(1)}, f32[8,4096]{1,0:T(8,128)S(1)}, u32[]{:S(2)}, u32[]{:S(2)}) collective-permute-start(f32[8,4096]{1,0:T(8,128)S(1)} %get-tuple-element.20.refs_0_), channel_id=1, source_target_pairs={{0,2},{1,3},{2,0},{3,1},{4,6},{5,7},{6,4},{7,5},{8,10},{9,11},{10,... | collective-permute-start | bytes 393224 | tf_op jit(solution)/shard_map/ppermute | solution.py:430
  11.7 1.5 %collective-permute-start.1 = (f32[8,4096]{1,0:T(8,128)S(1)}, f32[8,4096]{1,0:T(8,128)S(1)}, u32[]{:S(2)}, u32[]{:S(2)}) collective-permute-start(f32[8,4096]{1,0:T(8,128)S(1)} %get-tuple-element.20.refs_0_), channel_id=1, source_target_pairs={{0,4},{1,5},{2,6},{3,7},{4,0},{5,1},{6,2},{7,3},{8,12},{9,13},{10,... | collective-permute-start | bytes 393224 | tf_op jit(solution)/shard_map/ppermute | solution.py:430
  13.1 0.3 collective-permute-start
  13.4 3.6 %all-to-all-done = s32[32,1,384]{2,1,0:T(1,128)S(1)} async-done(((s32[32,1,384]{2,1,0:T(1,128)}), s32[32,1,384]{2,1,0:T(1,128)S(1)}, u32[]{:S(2)}, u32[]{:S(2)}) %all-to-all-start) | async-done | bytes 49184 | tf_op jit(solution)/shard_map/all_to_all | solution.py:409
  17.0 1.2 %shard_map.95 = f32[128,128]{1,0:T(8,128)} custom-call(s32[96,128]{1,0:T(8,128)S(1)} %bitcast.7, bf16[512,384]{1,0:T(8,128)(2,1)S(1)} %get-tuple-element.19.table_ref), custom_call_target="tpu_custom_call" | custom-call | tf_op jit(solution)/shard_map/pallas_call | solution.py:460
  18.1 2.5 %all-to-all-start.1 = ((f32[32,1,512]{2,1,0:T(1,128)}), f32[32,1,512]{2,1,0:T(1,128)S(1)}, u32[]{:S(2)}, u32[]{:S(2)}) async-start(f32[32,1,512]{2,1,0:T(1,128)} %bitcast.4), calls=%async_computation.1 | async-start | bytes 131072 | tf_op jit(solution)/shard_map/all_to_all | solution.py:409
  20.7 0.0 collective-permute-done.2.refs_3_
  20.7 0.0 collective-permute-done.1.refs_2_
  20.7 0.0 collective-permute-done.refs_1_
  20.7 1.0 %shard_map.96 = (f32[32,4096]{1,0:T(8,128)S(1)}, f32[128,128]{1,0:T(8,128)S(1)}, s32[16,128]{1,0:T(8,128)S(1)}) custom-call(s32[96,128]{1,0:T(8,128)S(1)} %bitcast.8, f32[8,4096]{1,0:T(8,128)S(1)} %get-tuple-element.20.refs_0_, f32[8,4096]{1,0:T(8,128)S(1)} %collective-permute-done.refs_1_, f32[8,4096]{1,0:T(8,128)S(1)} %collective-permute-done.1.refs_2_, ...), custom_call_target="tpu_custom_call" | custom-call | flops 16777216 | bytes 1048576 | tf_op jit(solution)/shard_map/pallas_call | solution.py:468
  21.8 6.1 %all-to-all-done.1 = f32[32,1,512]{2,1,0:T(1,128)S(1)} async-done(((f32[32,1,512]{2,1,0:T(1,128)}), f32[32,1,512]{2,1,0:T(1,128)S(1)}, u32[]{:S(2)}, u32[]{:S(2)}) %all-to-all-start.1) | async-done | bytes 65568 | tf_op jit(solution)/shard_map/all_to_all | solution.py:409
  27.9 3.2 %shard_map.97 = (f32[8,128]{1,0:T(8,128)S(1)}, f32[8,128]{1,0:T(8,128)S(1)}, f32[64,128]{1,0:T(8,128)S(1)}) custom-call(f32[128,128]{1,0:T(8,128)S(1)} %bitcast.9, f32[32,4096]{1,0:T(8,128)S(1)} %get-tuple-element.21.all_ref, f32[128,128]{1,0:T(8,128)S(1)} %get-tuple-element.22.listed_ref, s32[16,128]{1,0:T(8,128)S(1)} %get-tuple-element.23.slot_ref), custom_call_target="tpu_custom_call" | custom-call | tf_op jit(solution)/shard_map/pallas_call | solution.py:486
  31.1 0.2 collective-permute-start.3
  31.3 2.4 %shard_map.99.mine_ref = f32[8,128]{1,0:T(8,128)S(1)} custom-call(f32[64,128]{1,0:T(8,128)S(1)} %get-tuple-element.25.target_ref, f32[32,4096]{1,0:T(8,128)S(1)} %get-tuple-element.21.all_ref, f32[128,128]{1,0:T(8,128)S(1)} %get-tuple-element.22.listed_ref, s32[16,128]{1,0:T(8,128)S(1)} %get-tuple-element.23.slot_ref), custom_call_target="tpu_custom_call" | custom-call | tf_op jit(solution)/shard_map/pallas_call | solution.py:486
  33.7 0.0 collective-permute-done.3.partner_ref
  33.7 1.0 %collective-permute-start.4 = (f32[1,128]{1,0:T(1,128)S(1)}, f32[1,128]{1,0:T(1,128)S(1)}, u32[]{:S(2)}, u32[]{:S(2)}) collective-permute-start(f32[1,128]{1,0:T(1,128)S(1)} %get-tuple-element.27), channel_id=1, source_target_pairs={{0,24},{1,25},{2,26},{3,27},{4,28},{5,29},{6,30},{7,31},{8,16},{9,... | collective-permute-start | bytes 1544 | tf_op jit(solution)/shard_map/ppermute | solution.py:430
  34.7 1.2 %collective-permute-start.5 = (f32[1,128]{1,0:T(1,128)S(1)}, f32[1,128]{1,0:T(1,128)S(1)}, u32[]{:S(2)}, u32[]{:S(2)}) collective-permute-start(f32[1,128]{1,0:T(1,128)S(1)} %get-tuple-element.28), channel_id=1, source_target_pairs={{0,16},{1,17},{2,18},{3,19},{4,20},{5,21},{6,22},{7,23},{8,24},{9,... | collective-permute-start | bytes 1544 | tf_op jit(solution)/shard_map/ppermute | solution.py:430
  35.9 2.3 %collective-permute-start.6 = (f32[1,128]{1,0:T(1,128)S(1)}, f32[1,128]{1,0:T(1,128)S(1)}, u32[]{:S(2)}, u32[]{:S(2)}) collective-permute-start(f32[1,128]{1,0:T(1,128)S(1)} %get-tuple-element.29), channel_id=1, source_target_pairs={{0,8},{1,9},{2,10},{3,11},{4,12},{5,13},{6,14},{7,15},{8,0},{9,1},... | collective-permute-start | bytes 1544 | tf_op jit(solution)/shard_map/ppermute | solution.py:430
  38.1 0.9 %shard_map.98.mine_ref = f32[8,128]{1,0:T(8,128)S(1)} custom-call(f32[64,128]{1,0:T(8,128)S(1)} %get-tuple-element.25.target_ref, f32[32,4096]{1,0:T(8,128)S(1)} %get-tuple-element.21.all_ref, f32[128,128]{1,0:T(8,128)S(1)} %get-tuple-element.22.listed_ref, s32[16,128]{1,0:T(8,128)S(1)} %get-tuple-element.23.slot_ref), custom_call_target="tpu_custom_call" | custom-call | tf_op jit(solution)/shard_map/pallas_call | solution.py:486
  39.0 0.1 collective-permute-done.4.refs_0_
  39.1 0.0 collective-permute-done.5.refs_1_
  39.1 0.5 %collective-permute-done.6.refs_2_ = f32[1,128]{1,0:T(1,128)S(1)} collective-permute-done((f32[1,128]{1,0:T(1,128)S(1)}, f32[1,128]{1,0:T(1,128)S(1)}, u32[]{:S(2)}, u32[]{:S(2)}) %collective-permute-start.6) | collective-permute-done | bytes 544 | tf_op jit(solution)/shard_map/ppermute | solution.py:430
  39.7 0.8 %shard_map.101 = (f32[6,8]{1,0:T(8,128)}, f32[8,12]{1,0:T(8,128)}, f32[6,8]{1,0:T(8,128)}) custom-call(f32[8,128]{1,0:T(8,128)S(1)} %get-tuple-element.24.kept_ref, f32[8,128]{1,0:T(8,128)S(1)} %shard_map.98.mine_ref, f32[8,128]{1,0:T(8,128)S(1)} %collective-permute-done.3.partner_ref, f32[1,128]{1,0:T(1,128)S(1)} %collective-permute-done.4.refs_0_, ...), custom_call_target="tpu_custom_call" | custom-call | tf_op jit(solution)/shard_map/pallas_call | solution.py:508
  (1 shorter events, 0.0 us)
Async XLA Ops:
  2.5 14.5 %all-to-all-start = ((s32[32,1,384]{2,1,0:T(1,128)}), s32[32,1,384]{2,1,0:T(1,128)S(1)}, u32[]{:S(2)}, u32[]{:S(2)}) async-start(s32[32,1,384]{2,1,0:T(1,128)} %bitcast.2), calls=%async_computation | async-start | bytes 98304 | tf_op jit(solution)/shard_map/all_to_all | solution.py:409
  9.8 10.9 %collective-permute-start.2 = (f32[8,4096]{1,0:T(8,128)S(1)}, f32[8,4096]{1,0:T(8,128)S(1)}, u32[]{:S(2)}, u32[]{:S(2)}) collective-permute-start(f32[8,4096]{1,0:T(8,128)S(1)} %get-tuple-element.20.refs_0_), channel_id=1, source_target_pairs={{0,2},{1,3},{2,0},{3,1},{4,6},{5,7},{6,4},{7,5},{8,10},{9,11},{10,... | collective-permute-start | bytes 393224 | tf_op jit(solution)/shard_map/ppermute | solution.py:430
  11.7 9.1 %collective-permute-start.1 = (f32[8,4096]{1,0:T(8,128)S(1)}, f32[8,4096]{1,0:T(8,128)S(1)}, u32[]{:S(2)}, u32[]{:S(2)}) collective-permute-start(f32[8,4096]{1,0:T(8,128)S(1)} %get-tuple-element.20.refs_0_), channel_id=1, source_target_pairs={{0,4},{1,5},{2,6},{3,7},{4,0},{5,1},{6,2},{7,3},{8,12},{9,13},{10,... | collective-permute-start | bytes 393224 | tf_op jit(solution)/shard_map/ppermute | solution.py:430
  13.1 7.6 %collective-permute-start = (f32[8,4096]{1,0:T(8,128)S(1)}, f32[8,4096]{1,0:T(8,128)S(1)}, u32[]{:S(2)}, u32[]{:S(2)}) collective-permute-start(f32[8,4096]{1,0:T(8,128)S(1)} %get-tuple-element.20.refs_0_), channel_id=1, source_target_pairs={{0,6},{1,7},{2,4},{3,5},{4,2},{5,3},{6,0},{7,1},{8,14},{9,15},{10,... | collective-permute-start | bytes 393224 | tf_op jit(solution)/shard_map/ppermute | solution.py:430
  18.1 9.7 %all-to-all-start.1 = ((f32[32,1,512]{2,1,0:T(1,128)}), f32[32,1,512]{2,1,0:T(1,128)S(1)}, u32[]{:S(2)}, u32[]{:S(2)}) async-start(f32[32,1,512]{2,1,0:T(1,128)} %bitcast.4), calls=%async_computation.1 | async-start | bytes 131072 | tf_op jit(solution)/shard_map/all_to_all | solution.py:409
  31.1 2.5 %collective-permute-start.3 = (f32[8,128]{1,0:T(8,128)S(1)}, f32[8,128]{1,0:T(8,128)S(1)}, u32[]{:S(2)}, u32[]{:S(2)}) collective-permute-start(f32[8,128]{1,0:T(8,128)S(1)} %get-tuple-element.26), channel_id=1, source_target_pairs={{0,1},{1,0},{2,3},{3,2},{4,5},{5,4},{6,7},{7,6},{8,9},{9,8},{10,11... | collective-permute-start | bytes 12296 | tf_op jit(solution)/shard_map/ppermute | solution.py:430
  33.7 5.4 %collective-permute-start.4 = (f32[1,128]{1,0:T(1,128)S(1)}, f32[1,128]{1,0:T(1,128)S(1)}, u32[]{:S(2)}, u32[]{:S(2)}) collective-permute-start(f32[1,128]{1,0:T(1,128)S(1)} %get-tuple-element.27), channel_id=1, source_target_pairs={{0,24},{1,25},{2,26},{3,27},{4,28},{5,29},{6,30},{7,31},{8,16},{9,... | collective-permute-start | bytes 1544 | tf_op jit(solution)/shard_map/ppermute | solution.py:430
  34.7 4.4 %collective-permute-start.5 = (f32[1,128]{1,0:T(1,128)S(1)}, f32[1,128]{1,0:T(1,128)S(1)}, u32[]{:S(2)}, u32[]{:S(2)}) collective-permute-start(f32[1,128]{1,0:T(1,128)S(1)} %get-tuple-element.28), channel_id=1, source_target_pairs={{0,16},{1,17},{2,18},{3,19},{4,20},{5,21},{6,22},{7,23},{8,24},{9,... | collective-permute-start | bytes 1544 | tf_op jit(solution)/shard_map/ppermute | solution.py:430
  35.9 3.8 %collective-permute-start.6 = (f32[1,128]{1,0:T(1,128)S(1)}, f32[1,128]{1,0:T(1,128)S(1)}, u32[]{:S(2)}, u32[]{:S(2)}) collective-permute-start(f32[1,128]{1,0:T(1,128)S(1)} %get-tuple-element.29), channel_id=1, source_target_pairs={{0,8},{1,9},{2,10},{3,11},{4,12},{5,13},{6,14},{7,15},{8,0},{9,1},... | collective-permute-start | bytes 1544 | tf_op jit(solution)/shard_map/ppermute | solution.py:430

commit v10 on v9

--- a/solution.py
+++ b/solution.py
@@ -338,7 +338,7 @@
                 sums = tuple(pair_sums(held[n], source, source[6], softening, sums[n]) for n in range(len(held)))
             return sums
 
-        sums = lax.fori_loop(0, PARTS, add_stars, (zeros,) * len(held))
+        sums = lax.fori_loop(0, PARTS // 2, lambda n, sums: add_stars(2 * n + 1, add_stars(2 * n, sums)), (zeros,) * len(held))
         for n, group in enumerate(groups):
             irregular = zeros
             for j in range(slot_ref.shape[0] // lines):

time: 40.6 us -> 40.6 us (level)
  no operation moved by 1% of the time
where the time goes in v10:
time: 40.6 us; the launch traced here: 40.4 us
  starting transfers between devices  18 us (44%)
  Pallas kernels  11.3 us (28%)
  waiting for transfers between devices  10.4 us (26%)
  between operations  0.72 us (2%)
    all_to_all x2, starting transfers between devices, exchange(): lax.all_to_all(wide, 'stars', 0, 0, axis_index_groups=order, tiled=True)  9.85 us
    all_to_all x2, waiting for transfers between devices, exchange(): lax.all_to_all(wide, 'stars', 0, 0, axis_index_groups=order, tiled=True)  9.72 us
    ppermute x7, starting transfers between devices, swap(): return lax.ppermute(value, 'stars', [(i, i ^ mask) for i in range(devices)])  8.19 us
    pallas_call x3, Pallas kernels, forces_of(): pl.pallas_call(functools.partial(kernel, softening, targets, 4, core, mas...  6.47 us
    pallas_call x1, Pallas kernels, per_device(): pl.pallas_call(functools.partial(first_kernel, stars_dev, cap), out_shape...  1.87 us
    pallas_call x1, Pallas kernels, per_device(): pl.pallas_call(functools.partial(own_kernel, stars_dev, targets), out_sha...  1.16 us
    pallas_call x1, Pallas kernels, per_device(): pl.pallas_call(functools.partial(listed_kernel, cap, targets), out_shape=...  1.02 us
  transfers between devices with their start and end apart: 9, of which 4 were waited for; matrix products, arithmetic and copies ran while one was open for 0% of the time, Pallas kernels for 13%

profile of v10, /device:TPU:0, one launch (start us, length us, event | category | flops | bytes accessed | tf_op | source)
XLA Modules:
  0.0 40.4 jit_solution(8092438723525152198)
XLA Ops:
  0.6 1.9 %shard_map.94 = (s32[96,128]{1,0:T(8,128)}, f32[8,4096]{1,0:T(8,128)S(1)}, bf16[512,384]{1,0:T(8,128)(2,1)S(1)}) custom-call(s32[8]{0:T(128)} %refs_0_.1, s32[8]{0:T(128)} %refs_1_.1, s32[8,128]{1,0:T(8,128)} %refs_2_.1, f32[6,4096]{1,0:T(8,128)} %refs_3_.1, f32[6,4096]{1,0:T(8,128)} %refs_4_.1, f32[32,128]{1,0:T(8,128)} %bitcast.10, f32[32,128]{1,0:T(8,128)} %bitcast.11), custom_call_target="tpu_custom_call" | custom-call | tf_op jit(solution)/shard_map/pallas_call | solution.py:441
  2.5 7.3 %all-to-all-start = ((s32[32,1,384]{2,1,0:T(1,128)}), s32[32,1,384]{2,1,0:T(1,128)S(1)}, u32[]{:S(2)}, u32[]{:S(2)}) async-start(s32[32,1,384]{2,1,0:T(1,128)} %bitcast.2), calls=%async_computation | async-start | bytes 98304 | tf_op jit(solution)/shard_map/all_to_all | solution.py:409
  9.8 1.8 %collective-permute-start.2 = (f32[8,4096]{1,0:T(8,128)S(1)}, f32[8,4096]{1,0:T(8,128)S(1)}, u32[]{:S(2)}, u32[]{:S(2)}) collective-permute-start(f32[8,4096]{1,0:T(8,128)S(1)} %get-tuple-element.20.refs_0_), channel_id=1, source_target_pairs={{0,2},{1,3},{2,0},{3,1},{4,6},{5,7},{6,4},{7,5},{8,10},{9,11},{10,... | collective-permute-start | bytes 393224 | tf_op jit(solution)/shard_map/ppermute | solution.py:430
  11.7 1.5 %collective-permute-start.1 = (f32[8,4096]{1,0:T(8,128)S(1)}, f32[8,4096]{1,0:T(8,128)S(1)}, u32[]{:S(2)}, u32[]{:S(2)}) collective-permute-start(f32[8,4096]{1,0:T(8,128)S(1)} %get-tuple-element.20.refs_0_), channel_id=1, source_target_pairs={{0,4},{1,5},{2,6},{3,7},{4,0},{5,1},{6,2},{7,3},{8,12},{9,13},{10,... | collective-permute-start | bytes 393224 | tf_op jit(solution)/shard_map/ppermute | solution.py:430
  13.1 0.3 collective-permute-start
  13.4 3.6 %all-to-all-done = s32[32,1,384]{2,1,0:T(1,128)S(1)} async-done(((s32[32,1,384]{2,1,0:T(1,128)}), s32[32,1,384]{2,1,0:T(1,128)S(1)}, u32[]{:S(2)}, u32[]{:S(2)}) %all-to-all-start) | async-done | bytes 49184 | tf_op jit(solution)/shard_map/all_to_all | solution.py:409
  17.0 1.2 %shard_map.95 = f32[128,128]{1,0:T(8,128)} custom-call(s32[96,128]{1,0:T(8,128)S(1)} %bitcast.7, bf16[512,384]{1,0:T(8,128)(2,1)S(1)} %get-tuple-element.19.table_ref), custom_call_target="tpu_custom_call" | custom-call | tf_op jit(solution)/shard_map/pallas_call | solution.py:460
  18.1 2.5 %all-to-all-start.1 = ((f32[32,1,512]{2,1,0:T(1,128)}), f32[32,1,512]{2,1,0:T(1,128)S(1)}, u32[]{:S(2)}, u32[]{:S(2)}) async-start(f32[32,1,512]{2,1,0:T(1,128)} %bitcast.4), calls=%async_computation.1 | async-start | bytes 131072 | tf_op jit(solution)/shard_map/all_to_all | solution.py:409
  20.7 0.0 collective-permute-done.2.refs_3_
  20.7 0.0 collective-permute-done.1.refs_2_
  20.7 0.0 collective-permute-done.refs_1_
  20.7 1.0 %shard_map.96 = (f32[32,4096]{1,0:T(8,128)S(1)}, f32[128,128]{1,0:T(8,128)S(1)}, s32[16,128]{1,0:T(8,128)S(1)}) custom-call(s32[96,128]{1,0:T(8,128)S(1)} %bitcast.8, f32[8,4096]{1,0:T(8,128)S(1)} %get-tuple-element.20.refs_0_, f32[8,4096]{1,0:T(8,128)S(1)} %collective-permute-done.refs_1_, f32[8,4096]{1,0:T(8,128)S(1)} %collective-permute-done.1.refs_2_, ...), custom_call_target="tpu_custom_call" | custom-call | flops 16777216 | bytes 1048576 | tf_op jit(solution)/shard_map/pallas_call | solution.py:468
  21.8 6.1 %all-to-all-done.1 = f32[32,1,512]{2,1,0:T(1,128)S(1)} async-done(((f32[32,1,512]{2,1,0:T(1,128)}), f32[32,1,512]{2,1,0:T(1,128)S(1)}, u32[]{:S(2)}, u32[]{:S(2)}) %all-to-all-start.1) | async-done | bytes 65568 | tf_op jit(solution)/shard_map/all_to_all | solution.py:409
  27.9 3.2 %shard_map.97 = (f32[8,128]{1,0:T(8,128)S(1)}, f32[8,128]{1,0:T(8,128)S(1)}, f32[64,128]{1,0:T(8,128)S(1)}) custom-call(f32[128,128]{1,0:T(8,128)S(1)} %bitcast.9, f32[32,4096]{1,0:T(8,128)S(1)} %get-tuple-element.21.all_ref, f32[128,128]{1,0:T(8,128)S(1)} %get-tuple-element.22.listed_ref, s32[16,128]{1,0:T(8,128)S(1)} %get-tuple-element.23.slot_ref), custom_call_target="tpu_custom_call" | custom-call | tf_op jit(solution)/shard_map/pallas_call | solution.py:486
  31.1 0.2 collective-permute-start.3
  31.3 2.3 %shard_map.99.mine_ref = f32[8,128]{1,0:T(8,128)S(1)} custom-call(f32[64,128]{1,0:T(8,128)S(1)} %get-tuple-element.25.target_ref, f32[32,4096]{1,0:T(8,128)S(1)} %get-tuple-element.21.all_ref, f32[128,128]{1,0:T(8,128)S(1)} %get-tuple-element.22.listed_ref, s32[16,128]{1,0:T(8,128)S(1)} %get-tuple-element.23.slot_ref), custom_call_target="tpu_custom_call" | custom-call | tf_op jit(solution)/shard_map/pallas_call | solution.py:486
  33.7 0.0 collective-permute-done.3.partner_ref
  33.7 1.0 %collective-permute-start.4 = (f32[1,128]{1,0:T(1,128)S(1)}, f32[1,128]{1,0:T(1,128)S(1)}, u32[]{:S(2)}, u32[]{:S(2)}) collective-permute-start(f32[1,128]{1,0:T(1,128)S(1)} %get-tuple-element.27), channel_id=1, source_target_pairs={{0,24},{1,25},{2,26},{3,27},{4,28},{5,29},{6,30},{7,31},{8,16},{9,... | collective-permute-start | bytes 1544 | tf_op jit(solution)/shard_map/ppermute | solution.py:430
  34.7 1.2 %collective-permute-start.5 = (f32[1,128]{1,0:T(1,128)S(1)}, f32[1,128]{1,0:T(1,128)S(1)}, u32[]{:S(2)}, u32[]{:S(2)}) collective-permute-start(f32[1,128]{1,0:T(1,128)S(1)} %get-tuple-element.28), channel_id=1, source_target_pairs={{0,16},{1,17},{2,18},{3,19},{4,20},{5,21},{6,22},{7,23},{8,24},{9,... | collective-permute-start | bytes 1544 | tf_op jit(solution)/shard_map/ppermute | solution.py:430
  35.8 2.3 %collective-permute-start.6 = (f32[1,128]{1,0:T(1,128)S(1)}, f32[1,128]{1,0:T(1,128)S(1)}, u32[]{:S(2)}, u32[]{:S(2)}) collective-permute-start(f32[1,128]{1,0:T(1,128)S(1)} %get-tuple-element.29), channel_id=1, source_target_pairs={{0,8},{1,9},{2,10},{3,11},{4,12},{5,13},{6,14},{7,15},{8,0},{9,1},... | collective-permute-start | bytes 1544 | tf_op jit(solution)/shard_map/ppermute | solution.py:430
  38.1 0.9 %shard_map.98.mine_ref = f32[8,128]{1,0:T(8,128)S(1)} custom-call(f32[64,128]{1,0:T(8,128)S(1)} %get-tuple-element.25.target_ref, f32[32,4096]{1,0:T(8,128)S(1)} %get-tuple-element.21.all_ref, f32[128,128]{1,0:T(8,128)S(1)} %get-tuple-element.22.listed_ref, s32[16,128]{1,0:T(8,128)S(1)} %get-tuple-element.23.slot_ref), custom_call_target="tpu_custom_call" | custom-call | tf_op jit(solution)/shard_map/pallas_call | solution.py:486
  39.0 0.1 collective-permute-done.4.refs_0_
  39.1 0.0 collective-permute-done.5.refs_1_
  39.1 0.5 %collective-permute-done.6.refs_2_ = f32[1,128]{1,0:T(1,128)S(1)} collective-permute-done((f32[1,128]{1,0:T(1,128)S(1)}, f32[1,128]{1,0:T(1,128)S(1)}, u32[]{:S(2)}, u32[]{:S(2)}) %collective-permute-start.6) | collective-permute-done | bytes 544 | tf_op jit(solution)/shard_map/ppermute | solution.py:430
  39.7 0.8 %shard_map.101 = (f32[6,8]{1,0:T(8,128)}, f32[8,12]{1,0:T(8,128)}, f32[6,8]{1,0:T(8,128)}) custom-call(f32[8,128]{1,0:T(8,128)S(1)} %get-tuple-element.24.kept_ref, f32[8,128]{1,0:T(8,128)S(1)} %shard_map.98.mine_ref, f32[8,128]{1,0:T(8,128)S(1)} %collective-permute-done.3.partner_ref, f32[1,128]{1,0:T(1,128)S(1)} %collective-permute-done.4.refs_0_, ...), custom_call_target="tpu_custom_call" | custom-call | tf_op jit(solution)/shard_map/pallas_call | solution.py:508
  (1 shorter events, 0.0 us)
Async XLA Ops:
  2.5 14.5 %all-to-all-start = ((s32[32,1,384]{2,1,0:T(1,128)}), s32[32,1,384]{2,1,0:T(1,128)S(1)}, u32[]{:S(2)}, u32[]{:S(2)}) async-start(s32[32,1,384]{2,1,0:T(1,128)} %bitcast.2), calls=%async_computation | async-start | bytes 98304 | tf_op jit(solution)/shard_map/all_to_all | solution.py:409
  9.8 10.9 %collective-permute-start.2 = (f32[8,4096]{1,0:T(8,128)S(1)}, f32[8,4096]{1,0:T(8,128)S(1)}, u32[]{:S(2)}, u32[]{:S(2)}) collective-permute-start(f32[8,4096]{1,0:T(8,128)S(1)} %get-tuple-element.20.refs_0_), channel_id=1, source_target_pairs={{0,2},{1,3},{2,0},{3,1},{4,6},{5,7},{6,4},{7,5},{8,10},{9,11},{10,... | collective-permute-start | bytes 393224 | tf_op jit(solution)/shard_map/ppermute | solution.py:430
  11.7 9.1 %collective-permute-start.1 = (f32[8,4096]{1,0:T(8,128)S(1)}, f32[8,4096]{1,0:T(8,128)S(1)}, u32[]{:S(2)}, u32[]{:S(2)}) collective-permute-start(f32[8,4096]{1,0:T(8,128)S(1)} %get-tuple-element.20.refs_0_), channel_id=1, source_target_pairs={{0,4},{1,5},{2,6},{3,7},{4,0},{5,1},{6,2},{7,3},{8,12},{9,13},{10,... | collective-permute-start | bytes 393224 | tf_op jit(solution)/shard_map/ppermute | solution.py:430
  13.1 7.6 %collective-permute-start = (f32[8,4096]{1,0:T(8,128)S(1)}, f32[8,4096]{1,0:T(8,128)S(1)}, u32[]{:S(2)}, u32[]{:S(2)}) collective-permute-start(f32[8,4096]{1,0:T(8,128)S(1)} %get-tuple-element.20.refs_0_), channel_id=1, source_target_pairs={{0,6},{1,7},{2,4},{3,5},{4,2},{5,3},{6,0},{7,1},{8,14},{9,15},{10,... | collective-permute-start | bytes 393224 | tf_op jit(solution)/shard_map/ppermute | solution.py:430
  18.1 9.7 %all-to-all-start.1 = ((f32[32,1,512]{2,1,0:T(1,128)}), f32[32,1,512]{2,1,0:T(1,128)S(1)}, u32[]{:S(2)}, u32[]{:S(2)}) async-start(f32[32,1,512]{2,1,0:T(1,128)} %bitcast.4), calls=%async_computation.1 | async-start | bytes 131072 | tf_op jit(solution)/shard_map/all_to_all | solution.py:409
  31.1 2.5 %collective-permute-start.3 = (f32[8,128]{1,0:T(8,128)S(1)}, f32[8,128]{1,0:T(8,128)S(1)}, u32[]{:S(2)}, u32[]{:S(2)}) collective-permute-start(f32[8,128]{1,0:T(8,128)S(1)} %get-tuple-element.26), channel_id=1, source_target_pairs={{0,1},{1,0},{2,3},{3,2},{4,5},{5,4},{6,7},{7,6},{8,9},{9,8},{10,11... | collective-permute-start | bytes 12296 | tf_op jit(solution)/shard_map/ppermute | solution.py:430
  33.7 5.4 %collective-permute-start.4 = (f32[1,128]{1,0:T(1,128)S(1)}, f32[1,128]{1,0:T(1,128)S(1)}, u32[]{:S(2)}, u32[]{:S(2)}) collective-permute-start(f32[1,128]{1,0:T(1,128)S(1)} %get-tuple-element.27), channel_id=1, source_target_pairs={{0,24},{1,25},{2,26},{3,27},{4,28},{5,29},{6,30},{7,31},{8,16},{9,... | collective-permute-start | bytes 1544 | tf_op jit(solution)/shard_map/ppermute | solution.py:430
  34.7 4.4 %collective-permute-start.5 = (f32[1,128]{1,0:T(1,128)S(1)}, f32[1,128]{1,0:T(1,128)S(1)}, u32[]{:S(2)}, u32[]{:S(2)}) collective-permute-start(f32[1,128]{1,0:T(1,128)S(1)} %get-tuple-element.28), channel_id=1, source_target_pairs={{0,16},{1,17},{2,18},{3,19},{4,20},{5,21},{6,22},{7,23},{8,24},{9,... | collective-permute-start | bytes 1544 | tf_op jit(solution)/shard_map/ppermute | solution.py:430
  35.8 3.8 %collective-permute-start.6 = (f32[1,128]{1,0:T(1,128)S(1)}, f32[1,128]{1,0:T(1,128)S(1)}, u32[]{:S(2)}, u32[]{:S(2)}) collective-permute-start(f32[1,128]{1,0:T(1,128)S(1)} %get-tuple-element.29), channel_id=1, source_target_pairs={{0,8},{1,9},{2,10},{3,11},{4,12},{5,13},{6,14},{7,15},{8,0},{9,1},... | collective-permute-start | bytes 1544 | tf_op jit(solution)/shard_map/ppermute | solution.py:430
